TPU v7x, 32 devices: a whole 2x2x4 slice. The times are simulated.
32 devices in a mesh: groups: 2 (over y), adapter: 4 (over z), replica: 2 (over x), tp: 2 (over core).
Axes of the slice: x: 2, y: 2, z: 4, core: 2. Of those that a mesh axis runs over, the one named last changes fastest.
Arguments:
- tokens: bfloat16 [4, 256, 8192], P(('groups', 'replica'), 'adapter', 'tp'), parts along dimension 0, may hold values from -6 to 6
- token_adapter_index: int32 [4, 256, 1], P(('groups', 'replica')), parts along dimension 0, may hold values from 0 to 3; in each aligned block of 64 rows (0 to 63, 64 to 127, ..., all dimensions but the last counted through in order) at most 32 rows name the same one
- query_weight: bfloat16 [8192, 8192], P('tp', 'adapter'), may hold values from -0.0625 to 0.0625
- shrink_weight: bfloat16 [4, 8192, 64], P('adapter', 'tp'), may hold values from -0.0625 to 0.0625
- expand_weight: bfloat16 [4, 64, 8192], P('adapter'), may hold values from -0.75 to 0.75
Outputs:
- queries: bfloat16 [4, 256, 8192], P(('groups', 'replica'), ('adapter', 'tp')), parts along dimension 0
There are 2 independent parts, one for each index of `groups`. A program takes and returns all parts, laid end to end along the dimension named above; an argument that names none is the same for every part. Nothing has to cross between parts.
Inputs may be any that keep to these rules, and one draw needn't show every extreme that they name: `token_adapter_index`: in each aligned block of 64 tokens of a replica (the tokens of one device), no adapter is named by more than 32 tokens, and in some blocks one adapter is named by exactly 32.
All inputs are finite; a program needn't handle non-finite values.
Results may differ from a plain program's by a relative error of at most 0.0054.
Values may be sent and summed in bfloat16 or wider, within the bound.
No kernel may reach another device: no remote copies, remote signals or barrier semaphores. Data moves between devices by JAX's collectives and lax.ppermute only.
A program may use at most 64 MiB of HBM per device.

v0:
```python
import jax
import jax.numpy as jnp
from jax import lax
from jax.sharding import PartitionSpec as P

LOW_RANK_SCALE = 2.0


def local(tokens, token_adapter_index, query_weight, shrink_weight, expand_weight):
    own_rows = tokens[0]
    tok_rows = own_rows.shape[0]
    features = own_rows.shape[1]
    neighbor_count = lax.axis_size("adapter")
    slot_capacity = max(2, 2 * tok_rows // neighbor_count)
    own_index = lax.axis_index("adapter")
    tp_index = lax.axis_index("tp")
    all_ids = token_adapter_index[0, :, 0]
    by_source = all_ids.reshape(neighbor_count, tok_rows)
    matches = (
        by_source[:, :, None] == jnp.arange(neighbor_count, dtype=jnp.int32)[None, None, :]
    ).astype(jnp.int32)
    order_in = jnp.sum((jnp.cumsum(matches, axis=1) - matches) * matches, axis=2)
    slot_index = by_source * slot_capacity + order_in
    send_slots = lax.dynamic_index_in_dim(slot_index, own_index, 0, keepdims=False)
    slot_range = jnp.arange(neighbor_count * slot_capacity, dtype=jnp.int32)
    partial_value = jnp.dot(
        lax.all_gather(own_rows, "adapter", axis=0, tiled=True),
        query_weight,
        preferred_element_type=jnp.float32,
    )
    packer = (slot_range[:, None] == send_slots[None, :]).astype(jnp.bfloat16)
    outgoing = jnp.dot(packer, own_rows, preferred_element_type=jnp.float32).astype(jnp.bfloat16)
    outgoing = outgoing.reshape(neighbor_count, slot_capacity, features)
    received_rows = lax.all_to_all(
        outgoing, "adapter", split_axis=0, concat_axis=0, tiled=True
    ).reshape(neighbor_count * slot_capacity, features)
    shrink_output = jnp.dot(received_rows, shrink_weight[0], preferred_element_type=jnp.float32)
    rank_activation = lax.psum(shrink_output, "tp").astype(jnp.bfloat16)
    half_rows = tok_rows // 2
    low_rank_delta = (
        LOW_RANK_SCALE
        * jnp.dot(rank_activation, expand_weight[0], preferred_element_type=jnp.float32)
    ).astype(jnp.bfloat16)
    returned = lax.all_to_all(
        low_rank_delta.reshape(neighbor_count, slot_capacity, -1),
        "adapter",
        split_axis=0,
        concat_axis=0,
        tiled=True,
    )
    returned = returned.reshape(neighbor_count * slot_capacity, -1)
    my_slots = lax.dynamic_slice_in_dim(send_slots, tp_index * half_rows, half_rows)
    placer = (my_slots[:, None] == slot_range[None, :]).astype(jnp.bfloat16)
    added = jnp.dot(placer, returned, preferred_element_type=jnp.float32)
    moved = lax.all_to_all(partial_value, "adapter", split_axis=0, concat_axis=1, tiled=True)
    home_rows = lax.psum_scatter(moved, "tp", scatter_dimension=0, tiled=True)
    queries = (home_rows + added).astype(jnp.bfloat16)
    return queries[None]


def solution(mesh):
    placed = (
        P(("groups", "replica"), "adapter", "tp"),
        P(("groups", "replica"), None, None),
        P("tp", "adapter"),
        P("adapter", "tp", None),
        P("adapter", None, None),
    )
    return jax.shard_map(
        local,
        mesh=mesh,
        in_specs=placed,
        out_specs=P(("groups", "replica"), ("adapter", "tp"), None),
        check_vma=False,
    )
```

profile of v0, /device:TPU:0, one launch (start us, length us, event | category | flops | bytes accessed | tf_op | source)
XLA Modules:
  0.0 220.8 jit_solution(417745332051639863)
XLA Ops:
  6.5 0.0 copy-start
  6.5 0.0 all-gather.3.cloned.1.call-start
  6.5 0.7 all-gather.3.cloned.1.call-update
  7.3 50.3 %all-gather.3.cloned.1.call-done = bf16[1,256,4096]{2,1,0:T(8,128)(2,1)} async-done(((bf16[1,64,4096]{2,1,0:T(8,128)(2,1)}), bf16[1,256,4096]{2,1,0:T(8,128)(2,1)}) %all-gather.3.cloned.1.call-update) | async-done | bytes 2097168 | tf_op jit(solution)/shard_map/all_gather | solution.py:27
  57.6 12.2 %fusion.3 = f32[256,2048]{1,0:T(8,128)} fusion(bf16[4096,2048]{1,0:T(8,128)(2,1)} %param.7, bf16[1,256,4096]{2,1,0:T(8,128)(2,1)} %all-gather.3.cloned.1.call-done), kind=kOutput, calls=%fused_computation.6 | convolution fusion | flops 4294967296 | bytes 20971520 | tf_op jit(solution)/shard_map/dot_general | solution.py:26
  69.8 0.0 copy-start.2
  69.8 3.7 %all-to-all-start = ((f32[4,64,2048]{2,1,0:T(8,128)}), f32[4,64,2048]{2,1,0:T(8,128)S(1)}, u32[]{:S(2)}, u32[]{:S(2)}) async-start(f32[4,64,2048]{2,1,0:T(8,128)} %bitcast.36), calls=%async_computation | async-start | bytes 4194304 | tf_op jit(solution)/shard_map/all_to_all | solution.py:55
  73.6 0.5 broadcast.8
  74.1 0.0 copy-done.2
  74.1 0.7 reduce.3
  74.8 0.1 reshape_squeeze.3
  74.9 0.1 fusion.9
  75.0 0.1 reduce_window_sum.11
  75.1 0.2 select_reduce_fusion
  75.4 2.5 %convolution_convert_fusion = bf16[128,4096]{1,0:T(8,128)(2,1)} fusion(bf16[1,64,4096]{2,1,0:T(8,128)(2,1)} %param.5, s32[64]{0:T(128)S(1)} %dynamic-slice_bitcast_fusion), kind=kOutput, calls=%fused_computation.5 | convolution fusion | flops 67641344 | bytes 1573120 | tf_op jit(solution)/shard_map/dot_general | solution.py:32
  77.8 44.2 %all-to-all-done = f32[4,64,2048]{2,1,0:T(8,128)S(1)} async-done(((f32[4,64,2048]{2,1,0:T(8,128)}), f32[4,64,2048]{2,1,0:T(8,128)S(1)}, u32[]{:S(2)}, u32[]{:S(2)}) %all-to-all-start) | async-done | bytes 2097184 | tf_op jit(solution)/shard_map/all_to_all | solution.py:55
  122.0 4.3 %all-to-all-start.1 = ((bf16[4,32,4096]{2,1,0:T(8,128)(2,1)}), bf16[4,32,4096]{2,1,0:T(8,128)(2,1)}, u32[]{:S(2)}, u32[]{:S(2)}) async-start(bf16[4,32,4096]{2,1,0:T(8,128)(2,1)} %bitcast.35), calls=%async_computation.2 | async-start | bytes 2097152 | tf_op jit(solution)/shard_map/all_to_all | solution.py:34
  126.3 0.0 reduce-scatter.2.cloned.1.call-start
  126.3 1.5 copy.7
  127.8 0.0 copy-start.1
  127.8 0.0 reduce-scatter.2.cloned.1.call-update
  127.9 23.8 %all-to-all-done.1 = bf16[4,32,4096]{2,1,0:T(8,128)(2,1)} async-done(((bf16[4,32,4096]{2,1,0:T(8,128)(2,1)}), bf16[4,32,4096]{2,1,0:T(8,128)(2,1)}, u32[]{:S(2)}, u32[]{:S(2)}) %all-to-all-start.1) | async-done | bytes 1048608 | tf_op jit(solution)/shard_map/all_to_all | solution.py:34
  151.6 0.0 copy-done.1
  151.6 1.6 fusion.6
  153.3 3.6 %psum.7 = bf16[128,64]{1,0:T(8,128)(2,1)S(1)} all-reduce(f32[128,64]{1,0:T(8,128)S(1)} %fusion.6), channel_id=1, replica_groups=mesh['groups'=2,'adapter'=4,'replica'=2,'tp'=2] {'tp'}, use_global_device_ids=true, to_apply=%region_3.4 | all-reduce | flops 8192 | bytes 49152 | tf_op jit(solution)/shard_map/psum | solution.py:38
  156.9 0.0 copy-done
  156.9 2.0 fusion
  158.9 3.6 %all-to-all-start.2 = ((bf16[4,32,8192]{2,1,0:T(8,128)(2,1)}), bf16[4,32,8192]{2,1,0:T(8,128)(2,1)S(1)}, u32[]{:S(2)}, u32[]{:S(2)}) async-start(bf16[4,32,8192]{2,1,0:T(8,128)(2,1)} %bitcast.34), calls=%async_computation.3 | async-start | bytes 4194304 | tf_op jit(solution)/shard_map/all_to_all | solution.py:44
  162.5 0.1 dynamic-slice_bitcast_fusion.1
  162.6 48.9 %all-to-all-done.2 = bf16[4,32,8192]{2,1,0:T(8,128)(2,1)S(1)} async-done(((bf16[4,32,8192]{2,1,0:T(8,128)(2,1)}), bf16[4,32,8192]{2,1,0:T(8,128)(2,1)S(1)}, u32[]{:S(2)}, u32[]{:S(2)}) %all-to-all-start.2) | async-done | bytes 2097184 | tf_op jit(solution)/shard_map/all_to_all | solution.py:44
  211.5 0.0 reduce-scatter.2.cloned.1.call-done
  211.5 2.5 %fusion.2 = bf16[1,32,8192]{2,1,0:T(8,128)(2,1)} fusion(f32[32,8192]{1,0:T(8,128)} %reduce-scatter.2.cloned.1.call-done, bf16[128,8192]{1,0:T(8,128)(2,1)S(1)} %bitcast.33, s32[32]{0:T(128)S(1)} %dynamic-slice_bitcast_fusion.1), kind=kOutput, calls=%fused_computation.4 | convolution fusion | flops 67637248 | bytes 3670144 | tf_op jit(solution)/shard_map/dot_general | solution.py:54
  (2 shorter events, 0.0 us)
Async XLA Ops:
  6.5 150.4 %copy-start = (bf16[1,64,8192]{2,1,0:T(8,128)(2,1)S(1)}, bf16[1,64,8192]{2,1,0:T(8,128)(2,1)}, u32[]{:S(2)}) copy-start(bf16[1,64,8192]{2,1,0:T(8,128)(2,1)} %param.9) | copy-start | bytes 3145732
  6.5 51.1 %all-gather.3.cloned.1.call-start = ((), (), s32[]{:S(2)}) async-start(), calls=%async_computation.5 | async-start | bytes 2621440 | tf_op jit(solution)/shard_map/all_gather | solution.py:27
  69.8 4.3 %copy-start.2 = (s32[1,256,1]{1,2,0:T(1,128)S(1)}, s32[1,256,1]{1,2,0:T(1,128)}, u32[]{:S(2)}) copy-start(s32[1,256,1]{1,2,0:T(1,128)} %param.6) | copy-start | bytes 3076
  69.8 52.2 %all-to-all-start = ((f32[4,64,2048]{2,1,0:T(8,128)}), f32[4,64,2048]{2,1,0:T(8,128)S(1)}, u32[]{:S(2)}, u32[]{:S(2)}) async-start(f32[4,64,2048]{2,1,0:T(8,128)} %bitcast.36), calls=%async_computation | async-start | bytes 4194304 | tf_op jit(solution)/shard_map/all_to_all | solution.py:55
  122.0 29.6 %all-to-all-start.1 = ((bf16[4,32,4096]{2,1,0:T(8,128)(2,1)}), bf16[4,32,4096]{2,1,0:T(8,128)(2,1)}, u32[]{:S(2)}, u32[]{:S(2)}) async-start(bf16[4,32,4096]{2,1,0:T(8,128)(2,1)} %bitcast.35), calls=%async_computation.2 | async-start | bytes 2097152 | tf_op jit(solution)/shard_map/all_to_all | solution.py:34
  126.3 85.2 %reduce-scatter.2.cloned.1.call-start = ((), (), s32[]{:S(2)}) async-start(), calls=%async_computation.4 | async-start | bytes 3145728 | tf_op jit(solution)/shard_map/reduce_scatter | solution.py:56
  127.8 23.8 %copy-start.1 = (bf16[1,4096,64]{1,2,0:T(8,128)(2,1)S(1)}, bf16[1,4096,64]{1,2,0:T(8,128)(2,1)}, u32[]{:S(2)}) copy-start(bf16[1,4096,64]{1,2,0:T(8,128)(2,1)} %param.8) | copy-start | bytes 1572868
  158.9 52.6 %all-to-all-start.2 = ((bf16[4,32,8192]{2,1,0:T(8,128)(2,1)}), bf16[4,32,8192]{2,1,0:T(8,128)(2,1)S(1)}, u32[]{:S(2)}, u32[]{:S(2)}) async-start(bf16[4,32,8192]{2,1,0:T(8,128)(2,1)} %bitcast.34), calls=%async_computation.3 | async-start | bytes 4194304 | tf_op jit(solution)/shard_map/all_to_all | solution.py:44
Sparse Core Ops, SparseCore 0:
  8.9 48.6 all-gather.2
  129.4 10.9 reduce-scatter.1
where the time goes:
time: 221 us
  waiting for transfers between devices  168 us (76%)
  matrix products  20.8 us (9%)
  between operations  13.5 us (6%)
  starting transfers between devices  11.6 us (5%)
  blocking collectives  3.62 us (2%)
    all_gather x1, waiting for transfers between devices, local(): lax.all_gather(own_rows, 'adapter', axis=0, tiled=True)  50.3 us
    all_to_all x1, waiting for transfers between devices, local(): lax.all_to_all(low_rank_delta.reshape(neighbor_count, slot_capacity, -1),...  48.9 us
    all_to_all x1, waiting for transfers between devices, local(): lax.all_to_all(partial_value, 'adapter', split_axis=0, concat_axis=1, til...  44.2 us
    all_to_all x1, waiting for transfers between devices, local(): lax.all_to_all(outgoing, 'adapter', split_axis=0, concat_axis=0, tiled=True)  23.8 us
    dot_general x1, matrix products, local(): jnp.dot(lax.all_gather(own_rows, 'adapter', axis=0, tiled=True), query_we...  12.2 us
  transfers between devices with their start and end apart: 5, of which 4 were waited for; matrix products, arithmetic and copies ran while one was open for 4% of the time, Pallas kernels for 0%

commit v1 on v0

--- a/solution.py
+++ b/solution.py
@@ -1,12 +1,139 @@
 import jax
 import jax.numpy as jnp
 from jax import lax
+from jax.experimental import pallas as pl
+from jax.experimental.pallas import tpu as pltpu
 from jax.sharding import PartitionSpec as P
 
 LOW_RANK_SCALE = 2.0
-
-
-def local(tokens, token_adapter_index, query_weight, shrink_weight, expand_weight):
+F32 = jnp.float32
+BF16 = jnp.bfloat16
+
+FROM_NEXT = ((1, 0), (3, 1), (2, 3), (0, 2))
+FROM_LAST = ((0, 1), (1, 3), (3, 2), (2, 0))
+OPPOSITE = ((0, 3), (3, 0), (1, 2), (2, 1))
+INNER = ((1, 2), (2, 1))
+RELAY = ((2, 3), (1, 0))
+
+
+def shift(x, pairs, axis="adapter"):
+    return lax.ppermute(x, axis, pairs)
+
+
+def swap(x, axis):
+    return lax.ppermute(x, axis, ((0, 1), (1, 0)))
+
+
+def both(x, axis, dim):
+    other = swap(x, axis)
+    first = lax.axis_index(axis) == 0
+    return jnp.concatenate([jnp.where(first, x, other), jnp.where(first, other, x)], dim)
+
+
+def after(x, *earlier):
+    return lax.optimization_barrier((x,) + earlier)[0]
+
+
+def place_kernel(where_ref, *refs):
+    step = pl.program_id(0)
+    for i, source in enumerate(refs[:-1]):
+
+        @pl.when(step == i)
+        def _(source=source):
+            refs[-1][...] = source[...]
+
+
+def place(where, blocks):
+    rows, width = blocks[0].shape
+    return pl.pallas_call(
+        place_kernel,
+        out_shape=jax.ShapeDtypeStruct((rows, len(blocks) * width), blocks[0].dtype),
+        grid_spec=pltpu.PrefetchScalarGridSpec(
+            num_scalar_prefetch=1,
+            grid=(len(blocks),),
+            in_specs=[pl.BlockSpec((rows, width), lambda i, where: (0, 0))] * len(blocks),
+            out_specs=pl.BlockSpec((rows, width), lambda i, where: (0, where[i])),
+        ),
+    )(where, *blocks)
+
+
+def dot(a, b):
+    return jnp.dot(a, b, preferred_element_type=F32)
+
+
+def gray(v):
+    return v ^ (v >> 1)
+
+
+def line_of_four(tokens, token_adapter_index, query_weight, shrink_weight, expand_weight):
+    me = lax.axis_index("adapter")
+    tp = lax.axis_index("tp")
+    planes = [me] + [gray((gray(me) + i) % 4) for i in range(1, 4)]
+    own = tokens[0]
+    rows = own.shape[0]
+    half = rows // 2
+    width = query_weight.shape[1]
+    shrink = shrink_weight[0]
+    rank = shrink.shape[1]
+    ids = token_adapter_index[0]
+
+    def rank_of(x, i):
+        named = lax.dynamic_slice_in_dim(ids, planes[i] * rows, rows) == me
+        return jnp.where(named, dot(x, shrink), 0.0).astype(BF16)
+
+    x1 = shift(own, FROM_NEXT)
+    x3 = shift(own, FROM_LAST)
+    x2a = shift(own, INNER)
+    x2b = shift(x1, RELAY)
+
+    peers = lax.axis_size("groups") * lax.axis_size("replica") * lax.axis_size("tp")
+    peer = (lax.axis_index("groups") * lax.axis_size("replica") + lax.axis_index("replica")) * lax.axis_size("tp") + tp
+    share = rank // peers
+    r0 = rank_of(own, 0)
+    part = lax.dynamic_slice_in_dim(after(expand_weight[0], x1), peer * share, share)
+
+    def columns(i):
+        return lax.dynamic_slice_in_dim(part, planes[i] * width, width, 1)
+
+    panels = jnp.stack(
+        [columns(0), shift(columns(3), FROM_NEXT), shift(columns(2), OPPOSITE), shift(columns(1), FROM_LAST)]
+    )
+    panels = both(both(both(panels, "tp", 1), "replica", 1), "groups", 1).reshape(4 * rank, width)
+
+    base0 = dot(own, query_weight)
+    r1 = rank_of(x1, 1)
+    base1 = dot(x1, query_weight)
+    x3, base0, base1 = lax.optimization_barrier((x3, base0, base1))
+    r3 = rank_of(x3, 3)
+    early = jnp.concatenate([r0, r1, r3])
+    early = [early, shift(early, FROM_NEXT), shift(early, OPPOSITE), shift(early, FROM_LAST)]
+    base3 = dot(x3, query_weight)
+    x2a, x2b, base3 = lax.optimization_barrier((x2a, x2b, base3))
+    x2 = jnp.where((me == 1) | (me == 2), x2a, x2b)
+    r2 = rank_of(x2, 2)
+    late = [r2, shift(r2, FROM_NEXT), shift(r2, OPPOSITE), shift(r2, FROM_LAST)]
+    base2 = dot(x2, query_weight)
+    base = [base0, base1, base2, base3]
+
+    def rank_at(j, k):
+        return late[j] if k == 2 else early[j][rows * (0, 1, None, 2)[k]:][:rows]
+
+    wide = [jnp.concatenate([rank_at(j, (i - j) % 4) for j in range(4)], 1) for i in range(4)]
+
+    def partial(side):
+        at = side * half
+        take = lambda x: lax.dynamic_slice_in_dim(x, at, half)
+        ranks = jnp.concatenate([take(x) for x in wide])
+        bases = jnp.concatenate([take(x) for x in base])
+        return bases + LOW_RANK_SCALE * dot(ranks, panels)
+
+    theirs = swap(partial(1 - tp).astype(BF16), "tp")
+    full = (partial(tp) + theirs).astype(BF16).reshape(4, half, width)
+    back = [full[0], shift(full[3], FROM_NEXT), shift(full[2], OPPOSITE), shift(full[1], FROM_LAST)]
+    return place(jnp.stack(planes).astype(jnp.int32), back)[None]
+
+
+def any_length(tokens, token_adapter_index, query_weight, shrink_weight, expand_weight):
     own_rows = tokens[0]
     tok_rows = own_rows.shape[0]
     features = own_rows.shape[1]
@@ -66,8 +193,9 @@
         P("adapter", "tp", None),
         P("adapter", None, None),
     )
+    four = mesh.shape["adapter"] == 4 and all(mesh.shape[a] == 2 for a in ("groups", "replica", "tp"))
     return jax.shard_map(
-        local,
+        line_of_four if four else any_length,
         mesh=mesh,
         in_specs=placed,
         out_specs=P(("groups", "replica"), ("adapter", "tp"), None),

time: 221 us -> 103 us (0.47)
  waiting for transfers between devices: 168 us -> 34.3 us
  starting transfers between devices: 11.6 us -> 28.9 us
  between operations: 13.5 us -> 0.51 us
  matrix products: 20.8 us -> 31.6 us
  blocking collectives: 3.62 us -> 0 us
  Pallas kernels: 0 us -> 3.18 us
    all_to_all x3 -> x0, waiting for transfers between devices: 117 us -> none  [the longest x1 48.9 us: local(): lax.all_to_all(low_rank_delta.reshape(neighbor_count, slot_capacity, -1),...]
    all_gather x1 -> x0, waiting for transfers between devices: 50.3 us -> none  [local(): lax.all_gather(own_rows, 'adapter', axis=0, tiled=True)]
    ppermute x0 -> x20, waiting for transfers between devices: none -> 34.3 us  [the longest x16 24.3 us: shift(): return lax.ppermute(x, axis, pairs)]
    ppermute x0 -> x20, starting transfers between devices: none -> 28.9 us  [the longest x16 25.6 us: shift(): return lax.ppermute(x, axis, pairs)]
    all_to_all x3 -> x0, starting transfers between devices: 11.6 us -> none  [the longest x1 4.26 us: local(): lax.all_to_all(outgoing, 'adapter', split_axis=0, concat_axis=0, tiled=True)]
    dot_general x5 -> x10, matrix products: 20.8 us -> 31.6 us  [dot(): return jnp.dot(a, b, preferred_element_type=F32)]
    psum x1 -> x0, blocking collectives: 3.62 us -> none  [local(): rank_activation = lax.psum(shrink_output, 'tp').astype(jnp.bfloat16)]
    pallas_call x0 -> x1, Pallas kernels: none -> 3.18 us  [place(): pl.pallas_call(place_kernel, out_shape=jax.ShapeDtypeStruct((rows, len(bl...]
  transfers between devices with their start and end apart: 5 -> 20, of which waited for: 4 -> 8; matrix products, arithmetic and copies ran while one was open for 4% -> 33% of each run, Pallas kernels for 0% -> 0%
where the time goes in v1:
time: 103 us
  waiting for transfers between devices  34.3 us (33%)
  matrix products  31.6 us (31%)
  starting transfers between devices  28.9 us (28%)
  Pallas kernels  3.18 us (3%)
  local copies, waits for them, and re-layouts  2.85 us (3%)
  other arithmetic  1.63 us (2%)
    dot_general x10, matrix products, dot(): return jnp.dot(a, b, preferred_element_type=F32)  31.6 us
    ppermute x16, starting transfers between devices, shift(): return lax.ppermute(x, axis, pairs)  25.6 us
    ppermute x16, waiting for transfers between devices, shift(): return lax.ppermute(x, axis, pairs)  24.3 us
    ppermute x4, waiting for transfers between devices, swap(): return lax.ppermute(x, axis, ((0, 1), (1, 0)))  10.1 us
    ppermute x4, starting transfers between devices, swap(): return lax.ppermute(x, axis, ((0, 1), (1, 0)))  3.29 us
    pallas_call x1, Pallas kernels, place(): pl.pallas_call(place_kernel, out_shape=jax.ShapeDtypeStruct((rows, len(bl...  3.18 us
  transfers between devices with their start and end apart: 20, of which 8 were waited for; matrix products, arithmetic and copies ran while one was open for 33% of the time, Pallas kernels for 0%

profile of v1, /device:TPU:0, one launch (start us, length us, event | category | flops | bytes accessed | tf_op | source)
XLA Modules:
  0.0 102.9 jit_solution(14882476020984440286)
XLA Ops:
  0.0 4.1 %collective-permute-start.1 = (bf16[64,4096]{1,0:T(8,128)(2,1)}, bf16[64,4096]{1,0:T(8,128)(2,1)S(1)}, u32[]{:S(2)}, u32[]{:S(2)}) collective-permute-start(bf16[64,4096]{1,0:T(8,128)(2,1)} %bitcast.46), channel_id=1, source_target_pairs={{4,0},{12,4},{8,12},{0,8},{5,1},{13,5},{9,13},{1,9},{6,2},{14,6},{... | collective-permute-start | bytes 1572872 | tf_op jit(solution)/shard_map/ppermute | solution.py:20
  4.1 0.7 collective-permute-start.2
  4.8 3.4 %collective-permute-start = (bf16[64,4096]{1,0:T(8,128)(2,1)}, bf16[64,4096]{1,0:T(8,128)(2,1)S(1)}, u32[]{:S(2)}, u32[]{:S(2)}) collective-permute-start(bf16[64,4096]{1,0:T(8,128)(2,1)} %bitcast.48), channel_id=1, source_target_pairs={{0,4},{4,12},{12,8},{8,0},{1,5},{5,13},{13,9},{9,1},{2,6},{6,14},{... | collective-permute-start | bytes 1572872 | tf_op jit(solution)/shard_map/ppermute | solution.py:20
  8.2 9.0 %fusion.31 = f32[64,2048]{1,0:T(8,128)S(1)} fusion(bf16[4096,2048]{1,0:T(8,128)(2,1)} %param.7, bf16[1,64,4096]{2,1,0:T(8,128)(2,1)} %param.5), kind=kOutput, calls=%fused_computation.79 | convolution fusion | flops 1073741824 | bytes 17825792 | tf_op jit(solution)/shard_map/dot_general | solution.py:61
  17.3 0.1 compare_bitcast_fusion
  17.4 0.3 fusion.5
  17.7 0.0 collective-permute-done.1
  17.7 1.1 %dynamic-slice_bitcast_fusion = (bf16[1,8,2048]{2,1,0:T(8,128)(2,1)S(1)}, bf16[8,2048]{1,0:T(8,128)(2,1)S(1)}, bf16[8,2048]{1,0:T(8,128)(2,1)S(1)}, bf16[8,2048]{1,0:T(8,128)(2,1)S(1)}) fusion(bf16[64,8192]{1,0:T(8,128)(2,1)} %bitcast.57, s32[]{:T(128)S(6)} %select_n.147, s32[]{:T(128)S(6)} %select_n.149, s32[]{:T(128)S(6)} %select_n.155, s32[]{:T(128)S(6)} %select_n.153, ...), kind=kLoop, calls=%fused_computation.50 | loop fusion | bytes 262164 | tf_op jit(solution)/shard_map/stack | solution.py:98
  18.8 1.4 %collective-permute-start.12 = (bf16[8,2048]{1,0:T(8,128)(2,1)S(1)}, bf16[8,2048]{1,0:T(8,128)(2,1)S(1)}, u32[]{:S(2)}, u32[]{:S(2)}) collective-permute-start(bf16[8,2048]{1,0:T(8,128)(2,1)S(1)} %get-tuple-element.22), channel_id=1, source_target_pairs={{0,4},{4,12},{12,8},{8,0},{1,5},{5,13},{13,9},{9,1},{2,6},{6,14},{... | collective-permute-start | bytes 98312 | tf_op jit(solution)/shard_map/ppermute | solution.py:20
  20.2 2.5 %collective-permute-start.11 = (bf16[8,2048]{1,0:T(8,128)(2,1)S(1)}, bf16[8,2048]{1,0:T(8,128)(2,1)S(1)}, u32[]{:S(2)}, u32[]{:S(2)}) collective-permute-start(bf16[8,2048]{1,0:T(8,128)(2,1)S(1)} %get-tuple-element.23), channel_id=1, source_target_pairs={{0,12},{12,0},{4,8},{8,4},{1,13},{13,1},{5,9},{9,5},{2,14},{14,2},... | collective-permute-start | bytes 98312 | tf_op jit(solution)/shard_map/ppermute | solution.py:20
  22.7 0.0 collective-permute-start.10
  22.7 8.9 %fusion.37 = f32[64,2048]{1,0:T(8,128)S(1)} fusion(bf16[64,4096]{1,0:T(8,128)(2,1)S(1)} %collective-permute-done.1, bf16[4096,2048]{1,0:T(8,128)(2,1)} %param.7), kind=kOutput, calls=%fused_computation.85 | convolution fusion | flops 1073741824 | bytes 17825792 | tf_op jit(solution)/shard_map/dot_general | solution.py:61
  31.6 0.0 slice-start.2
  31.6 0.0 slice-start.3
  31.6 9.6 %collective-permute-done = bf16[64,4096]{1,0:T(8,128)(2,1)S(1)} collective-permute-done((bf16[64,4096]{1,0:T(8,128)(2,1)}, bf16[64,4096]{1,0:T(8,128)(2,1)S(1)}, u32[]{:S(2)}, u32[]{:S(2)}) %collective-permute-start) | collective-permute-done | bytes 524320 | tf_op jit(solution)/shard_map/ppermute | solution.py:20
  41.3 8.8 %fusion.38 = f32[64,2048]{1,0:T(8,128)S(1)} fusion(bf16[64,4096]{1,0:T(8,128)(2,1)S(1)} %collective-permute-done, bf16[4096,2048]{1,0:T(8,128)(2,1)} %param.7), kind=kOutput, calls=%fused_computation.86 | convolution fusion | flops 1073741824 | bytes 17825792 | tf_op jit(solution)/shard_map/dot_general | solution.py:61
  50.1 0.3 fusion.7
  50.4 0.3 fusion.6
  50.7 2.5 %collective-permute-start.7 = (bf16[192,64]{1,0:T(8,128)(2,1)S(1)}, bf16[192,64]{1,0:T(8,128)(2,1)S(1)}, u32[]{:S(2)}, u32[]{:S(2)}) collective-permute-start(bf16[192,64]{1,0:T(8,128)(2,1)S(1)} %pad_maximum_fusion.4), channel_id=1, source_target_pairs={{0,12},{12,0},{4,8},{8,4},{1,13},{13,1},{5,9},{9,5},{2,14},{14,2},... | collective-permute-start | bytes 73736 | tf_op jit(solution)/shard_map/ppermute | solution.py:20
  53.2 0.1 constant_dynamic-slice_fusion.6
  53.3 0.0 collective-permute-done.12
  53.3 0.1 collective-permute-start.6
  53.4 0.0 collective-permute-done.11
  53.4 2.9 %collective-permute-start.4 = (bf16[192,64]{1,0:T(8,128)(2,1)S(1)}, bf16[192,64]{1,0:T(8,128)(2,1)S(1)}, u32[]{:S(2)}, u32[]{:S(2)}) collective-permute-start(bf16[192,64]{1,0:T(8,128)(2,1)S(1)} %pad_maximum_fusion.4), channel_id=1, source_target_pairs={{4,0},{12,4},{8,12},{0,8},{5,1},{13,5},{9,13},{1,9},{6,2},{14,6},{... | collective-permute-start | bytes 73736 | tf_op jit(solution)/shard_map/ppermute | solution.py:20
  56.3 0.0 collective-permute-done.10
  56.3 1.3 %collective-permute-start.3 = (bf16[64,4096]{1,0:T(8,128)(2,1)S(1)}, bf16[64,4096]{1,0:T(8,128)(2,1)S(1)}, u32[]{:S(2)}, u32[]{:S(2)}) collective-permute-start(bf16[64,4096]{1,0:T(8,128)(2,1)S(1)} %collective-permute-done.1), channel_id=1, source_target_pairs={{8,12},{4,0},{9,13},{5,1},{10,14},{6,2},{11,15},{7,3},{24,28},{20,... | collective-permute-start | bytes 1572872 | tf_op jit(solution)/shard_map/ppermute | solution.py:20
  57.6 0.0 collective-permute-done.7
  57.6 0.1 collective-permute-start.13
  57.7 1.3 %collective-permute-done.13 = bf16[4,8,2048]{2,1,0:T(8,128)(2,1)S(1)} collective-permute-done((bf16[4,8,2048]{2,1,0:T(8,128)(2,1)S(1)}, bf16[4,8,2048]{2,1,0:T(8,128)(2,1)S(1)}, u32[]{:S(2)}, u32[]{:S(2)}) %collective-permute-start.13) | collective-permute-done | bytes 131104 | tf_op jit(solution)/shard_map/ppermute | solution.py:24
  59.1 1.6 %collective-permute-start.14 = (bf16[4,16,2048]{2,1,0:T(8,128)(2,1)S(1)}, bf16[4,16,2048]{2,1,0:T(8,128)(2,1)S(1)}, u32[]{:S(2)}, u32[]{:S(2)}) collective-permute-start(bf16[4,16,2048]{2,1,0:T(8,128)(2,1)S(1)} %pad_maximum_fusion.2), channel_id=1, source_target_pairs={{0,2},{2,0},{1,3},{3,1},{4,6},{6,4},{5,7},{7,5},{8,10},{10,8},{9,1... | collective-permute-start | bytes 786440 | tf_op jit(solution)/shard_map/ppermute | solution.py:24
  60.7 0.0 collective-permute-done.4
  60.7 6.8 %collective-permute-done.14 = bf16[4,16,2048]{2,1,0:T(8,128)(2,1)S(1)} collective-permute-done((bf16[4,16,2048]{2,1,0:T(8,128)(2,1)S(1)}, bf16[4,16,2048]{2,1,0:T(8,128)(2,1)S(1)}, u32[]{:S(2)}, u32[]{:S(2)}) %collective-permute-start.14) | collective-permute-done | bytes 262176 | tf_op jit(solution)/shard_map/ppermute | solution.py:24
  67.5 0.1 broadcast_select_fusion.4
  67.7 1.6 %collective-permute-start.15 = (bf16[4,32,2048]{2,1,0:T(8,128)(2,1)S(1)}, bf16[4,32,2048]{2,1,0:T(8,128)(2,1)S(1)}, u32[]{:S(2)}, u32[]{:S(2)}) collective-permute-start(bf16[4,32,2048]{2,1,0:T(8,128)(2,1)S(1)} %pad_maximum_fusion.1), channel_id=1, source_target_pairs={{0,16},{16,0},{1,17},{17,1},{2,18},{18,2},{3,19},{19,3},{4,20},{20... | collective-permute-start | bytes 1572872 | tf_op jit(solution)/shard_map/ppermute | solution.py:24
  69.2 0.0 collective-permute-done.2
  69.3 1.8 %collective-permute-done.3 = bf16[64,4096]{1,0:T(8,128)(2,1)S(1)} collective-permute-done((bf16[64,4096]{1,0:T(8,128)(2,1)S(1)}, bf16[64,4096]{1,0:T(8,128)(2,1)S(1)}, u32[]{:S(2)}, u32[]{:S(2)}) %collective-permute-start.3) | collective-permute-done | bytes 524320 | tf_op jit(solution)/shard_map/ppermute | solution.py:20
  71.1 3.1 %fusion.13 = f32[64,2048]{1,0:T(8,128)S(1)} fusion(bf16[4096,2048]{1,0:T(8,128)(2,1)S(1)} %bitcast.45, bf16[64,4096]{1,0:T(8,128)(2,1)S(1)} %collective-permute-done.2, bf16[64,4096]{1,0:T(8,128)(2,1)S(1)} %collective-permute-done.3, pred[]{:T(512)S(6)} %or.3), kind=kOutput, calls=%fused_computation.27 | convolution fusion | flops 1074003968 | bytes 18350080 | tf_op jit(solution)/shard_map/dot_general | solution.py:61
  74.2 0.3 fusion.8
  74.5 0.8 collective-permute-start.9
  75.3 1.3 %collective-permute-start.8 = (bf16[64,64]{1,0:T(8,128)(2,1)S(1)}, bf16[64,64]{1,0:T(8,128)(2,1)S(1)}, u32[]{:S(2)}, u32[]{:S(2)}) collective-permute-start(bf16[64,64]{1,0:T(8,128)(2,1)S(1)} %fusion.8), channel_id=1, source_target_pairs={{0,4},{4,12},{12,8},{8,0},{1,5},{5,13},{13,9},{9,1},{2,6},{6,14},{... | collective-permute-start | bytes 24584 | tf_op jit(solution)/shard_map/ppermute | solution.py:20
  76.6 1.3 %collective-permute-start.5 = (bf16[64,64]{1,0:T(8,128)(2,1)S(1)}, bf16[64,64]{1,0:T(8,128)(2,1)S(1)}, u32[]{:S(2)}, u32[]{:S(2)}) collective-permute-start(bf16[64,64]{1,0:T(8,128)(2,1)S(1)} %fusion.8), channel_id=1, source_target_pairs={{0,12},{12,0},{4,8},{8,4},{1,13},{13,1},{5,9},{9,5},{2,14},{14,2},... | collective-permute-start | bytes 24584 | tf_op jit(solution)/shard_map/ppermute | solution.py:20
  77.9 0.1 constant_dynamic-slice_fusion.4
  78.0 0.1 pad_maximum_fusion.7
  78.1 0.2 collective-permute-done.9
  78.3 0.1 pad_maximum_fusion.8
  78.4 3.7 %collective-permute-done.5 = bf16[64,64]{1,0:T(8,128)(2,1)S(1)} collective-permute-done((bf16[64,64]{1,0:T(8,128)(2,1)S(1)}, bf16[64,64]{1,0:T(8,128)(2,1)S(1)}, u32[]{:S(2)}, u32[]{:S(2)}) %collective-permute-start.5) | collective-permute-done | bytes 8224 | tf_op jit(solution)/shard_map/ppermute | solution.py:20
  82.1 0.1 pad_maximum_fusion.5
  82.3 0.1 pad_maximum_fusion.6
  82.4 0.3 broadcast_select_fusion.1
  82.6 0.1 pad_maximum_fusion
  82.8 0.3 fusion.4
  83.1 0.1 collective-permute-start.16
  83.2 1.9 %collective-permute-done.16 = bf16[128,2048]{1,0:T(8,128)(2,1)S(1)} collective-permute-done((bf16[128,2048]{1,0:T(8,128)(2,1)S(1)}, bf16[128,2048]{1,0:T(8,128)(2,1)S(1)}, u32[]{:S(2)}, u32[]{:S(2)}) %collective-permute-start.16) | collective-permute-done | bytes 524320 | tf_op jit(solution)/shard_map/ppermute | solution.py:24
  85.1 0.3 fusion.3
  85.4 0.7 fusion.33
  86.1 1.2 %collective-permute-start.19 = (bf16[32,2048]{1,0:T(8,128)(2,1)S(1)}, bf16[32,2048]{1,0:T(8,128)(2,1)S(1)}, u32[]{:S(2)}, u32[]{:S(2)}) collective-permute-start(bf16[32,2048]{1,0:T(8,128)(2,1)S(1)} %get-tuple-element.25), channel_id=1, source_target_pairs={{0,4},{4,12},{12,8},{8,0},{1,5},{5,13},{13,9},{9,1},{2,6},{6,14},{... | collective-permute-start | bytes 393224 | tf_op jit(solution)/shard_map/ppermute | solution.py:20
  87.3 1.3 %collective-permute-start.18 = (bf16[32,2048]{1,0:T(8,128)(2,1)S(1)}, bf16[32,2048]{1,0:T(8,128)(2,1)S(1)}, u32[]{:S(2)}, u32[]{:S(2)}) collective-permute-start(bf16[32,2048]{1,0:T(8,128)(2,1)S(1)} %get-tuple-element.26), channel_id=1, source_target_pairs={{0,12},{12,0},{4,8},{8,4},{1,13},{13,1},{5,9},{9,5},{2,14},{14,2},... | collective-permute-start | bytes 393224 | tf_op jit(solution)/shard_map/ppermute | solution.py:20
  88.6 0.9 collective-permute-start.17
  89.5 0.6 pad_add_fusion.where_ref
  90.1 8.9 %collective-permute-done.19.refs_3_ = bf16[32,2048]{1,0:T(8,128)(2,1)S(1)} collective-permute-done((bf16[32,2048]{1,0:T(8,128)(2,1)S(1)}, bf16[32,2048]{1,0:T(8,128)(2,1)S(1)}, u32[]{:S(2)}, u32[]{:S(2)}) %collective-permute-start.19) | collective-permute-done | bytes 131104 | tf_op jit(solution)/shard_map/ppermute | solution.py:20
  99.0 0.6 copy-done.2
  99.6 0.1 copy-done.3
  99.7 0.1 copy-done.4
  99.7 3.2 %shard_map.55 = bf16[32,8192]{1,0:T(8,128)(2,1)} custom-call(s32[4]{0:T(128)} %pad_add_fusion.where_ref, bf16[32,2048]{1,0:T(8,128)(2,1)} %get-tuple-element.28.refs_0_, bf16[32,2048]{1,0:T(8,128)(2,1)} %copy-done.4, bf16[32,2048]{1,0:T(8,128)(2,1)} %copy-done.3, bf16[32,2048]{1,0:T(8,128)(2,1)} %copy-done.2), custom_call_target="tpu_custom_call" | custom-call | tf_op jit(solution)/shard_map/pallas_call | solution.py:48
  (33 shorter events, 0.2 us)
Async XLA Ops:
  0.0 17.4 %copy-start = (bf16[1,4096,64]{1,2,0:T(8,128)(2,1)S(1)}, bf16[1,4096,64]{1,2,0:T(8,128)(2,1)}, u32[]{:S(2)}) copy-start(bf16[1,4096,64]{1,2,0:T(8,128)(2,1)} %param.8) | copy-start | bytes 1572868
  0.0 17.4 %copy-start.1 = (bf16[1,64,4096]{2,1,0:T(8,128)(2,1)S(1)}, bf16[1,64,4096]{2,1,0:T(8,128)(2,1)}, u32[]{:S(2)}) copy-start(bf16[1,64,4096]{2,1,0:T(8,128)(2,1)} %param.5) | copy-start | bytes 1572868
  0.0 17.3 %copy-start.5 = (s32[1,256,1]{1,2,0:T(1,128)S(1)}, s32[1,256,1]{1,2,0:T(1,128)}, u32[]{:S(2)}) copy-start(s32[1,256,1]{1,2,0:T(1,128)} %param.6) | copy-start | bytes 3076
  0.0 17.7 %collective-permute-start.1 = (bf16[64,4096]{1,0:T(8,128)(2,1)}, bf16[64,4096]{1,0:T(8,128)(2,1)S(1)}, u32[]{:S(2)}, u32[]{:S(2)}) collective-permute-start(bf16[64,4096]{1,0:T(8,128)(2,1)} %bitcast.46), channel_id=1, source_target_pairs={{4,0},{12,4},{8,12},{0,8},{5,1},{13,5},{9,13},{1,9},{6,2},{14,6},{... | collective-permute-start | bytes 1572872 | tf_op jit(solution)/shard_map/ppermute | solution.py:20
  4.1 65.2 %collective-permute-start.2 = (bf16[64,4096]{1,0:T(8,128)(2,1)}, bf16[64,4096]{1,0:T(8,128)(2,1)S(1)}, u32[]{:S(2)}, u32[]{:S(2)}) collective-permute-start(bf16[64,4096]{1,0:T(8,128)(2,1)} %bitcast.47), channel_id=1, source_target_pairs={{4,8},{8,4},{5,9},{9,5},{6,10},{10,6},{7,11},{11,7},{20,24},{24,20... | collective-permute-start | bytes 1572872 | tf_op jit(solution)/shard_map/ppermute | solution.py:20
  4.8 36.5 %collective-permute-start = (bf16[64,4096]{1,0:T(8,128)(2,1)}, bf16[64,4096]{1,0:T(8,128)(2,1)S(1)}, u32[]{:S(2)}, u32[]{:S(2)}) collective-permute-start(bf16[64,4096]{1,0:T(8,128)(2,1)} %bitcast.48), channel_id=1, source_target_pairs={{0,4},{4,12},{12,8},{8,0},{1,5},{5,13},{13,9},{9,1},{2,6},{6,14},{... | collective-permute-start | bytes 1572872 | tf_op jit(solution)/shard_map/ppermute | solution.py:20
  18.8 34.5 %collective-permute-start.12 = (bf16[8,2048]{1,0:T(8,128)(2,1)S(1)}, bf16[8,2048]{1,0:T(8,128)(2,1)S(1)}, u32[]{:S(2)}, u32[]{:S(2)}) collective-permute-start(bf16[8,2048]{1,0:T(8,128)(2,1)S(1)} %get-tuple-element.22), channel_id=1, source_target_pairs={{0,4},{4,12},{12,8},{8,0},{1,5},{5,13},{13,9},{9,1},{2,6},{6,14},{... | collective-permute-start | bytes 98312 | tf_op jit(solution)/shard_map/ppermute | solution.py:20
  20.2 33.2 %collective-permute-start.11 = (bf16[8,2048]{1,0:T(8,128)(2,1)S(1)}, bf16[8,2048]{1,0:T(8,128)(2,1)S(1)}, u32[]{:S(2)}, u32[]{:S(2)}) collective-permute-start(bf16[8,2048]{1,0:T(8,128)(2,1)S(1)} %get-tuple-element.23), channel_id=1, source_target_pairs={{0,12},{12,0},{4,8},{8,4},{1,13},{13,1},{5,9},{9,5},{2,14},{14,2},... | collective-permute-start | bytes 98312 | tf_op jit(solution)/shard_map/ppermute | solution.py:20
  22.7 33.6 %collective-permute-start.10 = (bf16[8,2048]{1,0:T(8,128)(2,1)S(1)}, bf16[8,2048]{1,0:T(8,128)(2,1)S(1)}, u32[]{:S(2)}, u32[]{:S(2)}) collective-permute-start(bf16[8,2048]{1,0:T(8,128)(2,1)S(1)} %get-tuple-element.24), channel_id=1, source_target_pairs={{4,0},{12,4},{8,12},{0,8},{5,1},{13,5},{9,13},{1,9},{6,2},{14,6},{... | collective-permute-start | bytes 98312 | tf_op jit(solution)/shard_map/ppermute | solution.py:20
  22.7 48.4 %slice-start = ((s8[16777216]{0:T(1024)(128)(4,1)}), s8[4194304]{0:T(1024)(128)(4,1)S(1)}, s32[]{:S(2)}) async-start(s8[16777216]{0:T(1024)(128)(4,1)} %bitcast.44), calls=%async_computation | async-start | bytes 8388608
  22.7 48.4 %slice-start.1 = ((s8[16777216]{0:T(1024)(128)(4,1)}), s8[4194304]{0:T(1024)(128)(4,1)S(1)}, s32[]{:S(2)}) async-start(s8[16777216]{0:T(1024)(128)(4,1)} %bitcast.44), calls=%async_computation.1 | async-start | bytes 8388608
  31.6 39.5 %slice-start.2 = ((s8[16777216]{0:T(1024)(128)(4,1)}), s8[4194304]{0:T(1024)(128)(4,1)S(1)}, s32[]{:S(2)}) async-start(s8[16777216]{0:T(1024)(128)(4,1)} %bitcast.44), calls=%async_computation.2 | async-start | bytes 8388608
  31.6 39.5 %slice-start.3 = ((s8[16777216]{0:T(1024)(128)(4,1)}), s8[4194304]{0:T(1024)(128)(4,1)S(1)}, s32[]{:S(2)}) async-start(s8[16777216]{0:T(1024)(128)(4,1)} %bitcast.44), calls=%async_computation.3 | async-start | bytes 8388608
  50.7 6.9 %collective-permute-start.7 = (bf16[192,64]{1,0:T(8,128)(2,1)S(1)}, bf16[192,64]{1,0:T(8,128)(2,1)S(1)}, u32[]{:S(2)}, u32[]{:S(2)}) collective-permute-start(bf16[192,64]{1,0:T(8,128)(2,1)S(1)} %pad_maximum_fusion.4), channel_id=1, source_target_pairs={{0,12},{12,0},{4,8},{8,4},{1,13},{13,1},{5,9},{9,5},{2,14},{14,2},... | collective-permute-start | bytes 73736 | tf_op jit(solution)/shard_map/ppermute | solution.py:20
  53.3 7.4 %collective-permute-start.6 = (bf16[192,64]{1,0:T(8,128)(2,1)S(1)}, bf16[192,64]{1,0:T(8,128)(2,1)S(1)}, u32[]{:S(2)}, u32[]{:S(2)}) collective-permute-start(bf16[192,64]{1,0:T(8,128)(2,1)S(1)} %pad_maximum_fusion.4), channel_id=1, source_target_pairs={{0,4},{4,12},{12,8},{8,0},{1,5},{5,13},{13,9},{9,1},{2,6},{6,14},{... | collective-permute-start | bytes 73736 | tf_op jit(solution)/shard_map/ppermute | solution.py:20
  53.4 7.3 %collective-permute-start.4 = (bf16[192,64]{1,0:T(8,128)(2,1)S(1)}, bf16[192,64]{1,0:T(8,128)(2,1)S(1)}, u32[]{:S(2)}, u32[]{:S(2)}) collective-permute-start(bf16[192,64]{1,0:T(8,128)(2,1)S(1)} %pad_maximum_fusion.4), channel_id=1, source_target_pairs={{4,0},{12,4},{8,12},{0,8},{5,1},{13,5},{9,13},{1,9},{6,2},{14,6},{... | collective-permute-start | bytes 73736 | tf_op jit(solution)/shard_map/ppermute | solution.py:20
  56.3 14.8 %collective-permute-start.3 = (bf16[64,4096]{1,0:T(8,128)(2,1)S(1)}, bf16[64,4096]{1,0:T(8,128)(2,1)S(1)}, u32[]{:S(2)}, u32[]{:S(2)}) collective-permute-start(bf16[64,4096]{1,0:T(8,128)(2,1)S(1)} %collective-permute-done.1), channel_id=1, source_target_pairs={{8,12},{4,0},{9,13},{5,1},{10,14},{6,2},{11,15},{7,3},{24,28},{20,... | collective-permute-start | bytes 1572872 | tf_op jit(solution)/shard_map/ppermute | solution.py:20
  57.6 1.4 %collective-permute-start.13 = (bf16[4,8,2048]{2,1,0:T(8,128)(2,1)S(1)}, bf16[4,8,2048]{2,1,0:T(8,128)(2,1)S(1)}, u32[]{:S(2)}, u32[]{:S(2)}) collective-permute-start(bf16[4,8,2048]{2,1,0:T(8,128)(2,1)S(1)} %pad_maximum_fusion.3), channel_id=1, source_target_pairs={{0,1},{1,0},{2,3},{3,2},{4,5},{5,4},{6,7},{7,6},{8,9},{9,8},{10,11... | collective-permute-start | bytes 393224 | tf_op jit(solution)/shard_map/ppermute | solution.py:24
  59.1 8.4 %collective-permute-start.14 = (bf16[4,16,2048]{2,1,0:T(8,128)(2,1)S(1)}, bf16[4,16,2048]{2,1,0:T(8,128)(2,1)S(1)}, u32[]{:S(2)}, u32[]{:S(2)}) collective-permute-start(bf16[4,16,2048]{2,1,0:T(8,128)(2,1)S(1)} %pad_maximum_fusion.2), channel_id=1, source_target_pairs={{0,2},{2,0},{1,3},{3,1},{4,6},{6,4},{5,7},{7,5},{8,10},{10,8},{9,1... | collective-permute-start | bytes 786440 | tf_op jit(solution)/shard_map/ppermute | solution.py:24
  67.7 14.7 %collective-permute-start.15 = (bf16[4,32,2048]{2,1,0:T(8,128)(2,1)S(1)}, bf16[4,32,2048]{2,1,0:T(8,128)(2,1)S(1)}, u32[]{:S(2)}, u32[]{:S(2)}) collective-permute-start(bf16[4,32,2048]{2,1,0:T(8,128)(2,1)S(1)} %pad_maximum_fusion.1), channel_id=1, source_target_pairs={{0,16},{16,0},{1,17},{17,1},{2,18},{18,2},{3,19},{19,3},{4,20},{20... | collective-permute-start | bytes 1572872 | tf_op jit(solution)/shard_map/ppermute | solution.py:24
  74.5 3.8 %collective-permute-start.9 = (bf16[64,64]{1,0:T(8,128)(2,1)S(1)}, bf16[64,64]{1,0:T(8,128)(2,1)S(1)}, u32[]{:S(2)}, u32[]{:S(2)}) collective-permute-start(bf16[64,64]{1,0:T(8,128)(2,1)S(1)} %fusion.8), channel_id=1, source_target_pairs={{4,0},{12,4},{8,12},{0,8},{5,1},{13,5},{9,13},{1,9},{6,2},{14,6},{... | collective-permute-start | bytes 24584 | tf_op jit(solution)/shard_map/ppermute | solution.py:20
  75.3 6.9 %collective-permute-start.8 = (bf16[64,64]{1,0:T(8,128)(2,1)S(1)}, bf16[64,64]{1,0:T(8,128)(2,1)S(1)}, u32[]{:S(2)}, u32[]{:S(2)}) collective-permute-start(bf16[64,64]{1,0:T(8,128)(2,1)S(1)} %fusion.8), channel_id=1, source_target_pairs={{0,4},{4,12},{12,8},{8,0},{1,5},{5,13},{13,9},{9,1},{2,6},{6,14},{... | collective-permute-start | bytes 24584 | tf_op jit(solution)/shard_map/ppermute | solution.py:20
  76.6 5.5 %collective-permute-start.5 = (bf16[64,64]{1,0:T(8,128)(2,1)S(1)}, bf16[64,64]{1,0:T(8,128)(2,1)S(1)}, u32[]{:S(2)}, u32[]{:S(2)}) collective-permute-start(bf16[64,64]{1,0:T(8,128)(2,1)S(1)} %fusion.8), channel_id=1, source_target_pairs={{0,12},{12,0},{4,8},{8,4},{1,13},{13,1},{5,9},{9,5},{2,14},{14,2},... | collective-permute-start | bytes 24584 | tf_op jit(solution)/shard_map/ppermute | solution.py:20
  83.1 2.0 %collective-permute-start.16 = (bf16[128,2048]{1,0:T(8,128)(2,1)S(1)}, bf16[128,2048]{1,0:T(8,128)(2,1)S(1)}, u32[]{:S(2)}, u32[]{:S(2)}) collective-permute-start(bf16[128,2048]{1,0:T(8,128)(2,1)S(1)} %fusion.4), channel_id=1, source_target_pairs={{0,1},{1,0},{2,3},{3,2},{4,5},{5,4},{6,7},{7,6},{8,9},{9,8},{10,11... | collective-permute-start | bytes 1572872 | tf_op jit(solution)/shard_map/ppermute | solution.py:24
  86.1 12.9 %collective-permute-start.19 = (bf16[32,2048]{1,0:T(8,128)(2,1)S(1)}, bf16[32,2048]{1,0:T(8,128)(2,1)S(1)}, u32[]{:S(2)}, u32[]{:S(2)}) collective-permute-start(bf16[32,2048]{1,0:T(8,128)(2,1)S(1)} %get-tuple-element.25), channel_id=1, source_target_pairs={{0,4},{4,12},{12,8},{8,0},{1,5},{5,13},{13,9},{9,1},{2,6},{6,14},{... | collective-permute-start | bytes 393224 | tf_op jit(solution)/shard_map/ppermute | solution.py:20
  87.3 11.7 %collective-permute-start.18 = (bf16[32,2048]{1,0:T(8,128)(2,1)S(1)}, bf16[32,2048]{1,0:T(8,128)(2,1)S(1)}, u32[]{:S(2)}, u32[]{:S(2)}) collective-permute-start(bf16[32,2048]{1,0:T(8,128)(2,1)S(1)} %get-tuple-element.26), channel_id=1, source_target_pairs={{0,12},{12,0},{4,8},{8,4},{1,13},{13,1},{5,9},{9,5},{2,14},{14,2},... | collective-permute-start | bytes 393224 | tf_op jit(solution)/shard_map/ppermute | solution.py:20
  88.6 10.4 %collective-permute-start.17 = (bf16[32,2048]{1,0:T(8,128)(2,1)S(1)}, bf16[32,2048]{1,0:T(8,128)(2,1)S(1)}, u32[]{:S(2)}, u32[]{:S(2)}) collective-permute-start(bf16[32,2048]{1,0:T(8,128)(2,1)S(1)} %get-tuple-element.27), channel_id=1, source_target_pairs={{4,0},{12,4},{8,12},{0,8},{5,1},{13,5},{9,13},{1,9},{6,2},{14,6},{... | collective-permute-start | bytes 393224 | tf_op jit(solution)/shard_map/ppermute | solution.py:20
  99.0 0.7 copy-start.2
  99.0 0.7 copy-start.3
  99.0 0.8 copy-start.4

commit v2 on v1

--- a/solution.py
+++ b/solution.py
@@ -8,6 +8,7 @@
 LOW_RANK_SCALE = 2.0
 F32 = jnp.float32
 BF16 = jnp.bfloat16
+VMEM_LIMIT = 44 * 2**20
 
 FROM_NEXT = ((1, 0), (3, 1), (2, 3), (0, 2))
 FROM_LAST = ((0, 1), (1, 3), (3, 2), (2, 0))
@@ -35,12 +36,9 @@
 
 
 def place_kernel(where_ref, *refs):
-    step = pl.program_id(0)
+    width = refs[0].shape[1]
     for i, source in enumerate(refs[:-1]):
-
-        @pl.when(step == i)
-        def _(source=source):
-            refs[-1][...] = source[...]
+        refs[-1][:, pl.ds(pl.multiple_of(where_ref[i] * width, 128), width)] = source[...]
 
 
 def place(where, blocks):
@@ -48,13 +46,64 @@
     return pl.pallas_call(
         place_kernel,
         out_shape=jax.ShapeDtypeStruct((rows, len(blocks) * width), blocks[0].dtype),
-        grid_spec=pltpu.PrefetchScalarGridSpec(
-            num_scalar_prefetch=1,
-            grid=(len(blocks),),
-            in_specs=[pl.BlockSpec((rows, width), lambda i, where: (0, 0))] * len(blocks),
-            out_specs=pl.BlockSpec((rows, width), lambda i, where: (0, where[i])),
+        in_specs=[pl.BlockSpec(memory_space=pltpu.SMEM)] + [pl.BlockSpec(memory_space=pltpu.VMEM)] * len(blocks),
+        out_specs=pl.BlockSpec(memory_space=pltpu.VMEM),
+        compiler_params=pltpu.CompilerParams(vmem_limit_bytes=4 * 2**20),
+    )(where, *blocks)
+
+
+def base_kernel(inner_ref, *refs):
+    *x_refs, weight_ref, out_ref, x_ref, held_ref, sems = refs
+    count, depth, _ = held_ref.shape
+
+    def part(k):
+        return pltpu.make_async_copy(weight_ref.at[pl.ds(k * depth, depth)], held_ref.at[k], sems.at[k])
+
+    for k in range(count):
+        part(k).start()
+    rows = x_refs[0].shape[0]
+    for i, block in enumerate(x_refs):
+        at = pl.ds(min(i, 2) * rows, rows)
+        if i < 2:
+            x_ref[at] = block[...]
+        else:
+
+            @pl.when(inner_ref[0] == 3 - i)
+            def _(at=at, block=block):
+                x_ref[at] = block[...]
+
+    for k in range(count):
+        part(k).wait()
+        term = dot(x_ref[:, k * depth : (k + 1) * depth], held_ref[k])
+        if k == 0:
+            out_ref[...] = term
+        else:
+            out_ref[...] += term
+
+
+def base_of(inner, blocks, weight):
+    rows, depth = blocks[0].shape
+    count = min(len(blocks), 3)
+    width = weight.shape[1]
+    parts = 8
+    vmem = pl.BlockSpec(memory_space=pltpu.VMEM)
+    return pl.pallas_call(
+        base_kernel,
+        out_shape=jax.ShapeDtypeStruct((count * rows, width), F32),
+        in_specs=[pl.BlockSpec(memory_space=pltpu.SMEM)]
+        + [vmem] * len(blocks)
+        + [pl.BlockSpec(memory_space=pl.ANY)],
+        out_specs=vmem,
+        scratch_shapes=[
+            pltpu.VMEM((count * rows, depth), weight.dtype),
+            pltpu.VMEM((parts, depth // parts, width), weight.dtype),
+            pltpu.SemaphoreType.DMA((parts,)),
+        ],
+        compiler_params=pltpu.CompilerParams(vmem_limit_bytes=VMEM_LIMIT),
+        cost_estimate=pl.CostEstimate(
+            flops=2 * count * rows * depth * width, bytes_accessed=weight.size * 2, transcendentals=0
         ),
-    )(where, *blocks)
+    )(inner, *blocks, weight)
 
 
 def dot(a, b):
@@ -77,46 +126,46 @@
     rank = shrink.shape[1]
     ids = token_adapter_index[0]
 
-    def rank_of(x, i):
-        named = lax.dynamic_slice_in_dim(ids, planes[i] * rows, rows) == me
-        return jnp.where(named, dot(x, shrink), 0.0).astype(BF16)
-
     x1 = shift(own, FROM_NEXT)
+    inner = (me == 1) | (me == 2)
+    base0 = base_of(jnp.ones((1,), jnp.int32), [own], query_weight)
+    own, base0 = lax.optimization_barrier((own, base0))
     x3 = shift(own, FROM_LAST)
     x2a = shift(own, INNER)
-    x2b = shift(x1, RELAY)
-
-    peers = lax.axis_size("groups") * lax.axis_size("replica") * lax.axis_size("tp")
-    peer = (lax.axis_index("groups") * lax.axis_size("replica") + lax.axis_index("replica")) * lax.axis_size("tp") + tp
+
+    inside = ("replica", "tp")
+    peers = lax.axis_size(inside)
+    peer = lax.axis_index(inside)
     share = rank // peers
-    r0 = rank_of(own, 0)
-    part = lax.dynamic_slice_in_dim(after(expand_weight[0], x1), peer * share, share)
+    part = lax.dynamic_slice_in_dim(after(expand_weight[0], base0), peer * share, share)
 
     def columns(i):
         return lax.dynamic_slice_in_dim(part, planes[i] * width, width, 1)
 
-    panels = jnp.stack(
+    part = jnp.stack(
         [columns(0), shift(columns(3), FROM_NEXT), shift(columns(2), OPPOSITE), shift(columns(1), FROM_LAST)]
-    )
-    panels = both(both(both(panels, "tp", 1), "replica", 1), "groups", 1).reshape(4 * rank, width)
-
-    base0 = dot(own, query_weight)
-    r1 = rank_of(x1, 1)
-    base1 = dot(x1, query_weight)
-    x3, base0, base1 = lax.optimization_barrier((x3, base0, base1))
-    r3 = rank_of(x3, 3)
-    early = jnp.concatenate([r0, r1, r3])
-    early = [early, shift(early, FROM_NEXT), shift(early, OPPOSITE), shift(early, FROM_LAST)]
-    base3 = dot(x3, query_weight)
-    x2a, x2b, base3 = lax.optimization_barrier((x2a, x2b, base3))
-    x2 = jnp.where((me == 1) | (me == 2), x2a, x2b)
-    r2 = rank_of(x2, 2)
-    late = [r2, shift(r2, FROM_NEXT), shift(r2, OPPOSITE), shift(r2, FROM_LAST)]
-    base2 = dot(x2, query_weight)
-    base = [base0, base1, base2, base3]
+    ).reshape(4 * share, width)
+    x1, part = lax.optimization_barrier((x1, part))
+    x2b = shift(x1, RELAY)
+    x3, x2a, x2b = lax.optimization_barrier((x3, x2a, x2b))
+    parts = [part] + [shift(part, [(i, i ^ k) for i in range(peers)], inside) for k in range(1, peers)]
+    to = jnp.arange(4 * rank)[:, None]
+    at = jnp.arange(4 * rank)[None, :]
+    picked = at == ((to % rank // share) ^ peer) * (4 * share) + to // rank * share + to % share
+    panels = dot(picked.astype(BF16), jnp.concatenate(parts)).astype(BF16)
+
+    x2 = jnp.where(inner, x2a, x2b)
+    ranks = []
+    for i, x in enumerate((own, x1, x2, x3)):
+        named = lax.dynamic_slice_in_dim(ids, planes[i] * rows, rows) == me
+        ranks.append(jnp.where(named, dot(x, shrink), 0.0).astype(BF16))
+    ranks = jnp.concatenate(ranks)
+    ranks = [ranks, shift(ranks, FROM_NEXT), shift(ranks, OPPOSITE), shift(ranks, FROM_LAST)]
+    base = base_of(inner.astype(jnp.int32)[None], [x1, x3, x2a, x2b], query_weight)
+    base = [base0, base[:rows], base[2 * rows :], base[rows : 2 * rows]]
 
     def rank_at(j, k):
-        return late[j] if k == 2 else early[j][rows * (0, 1, None, 2)[k]:][:rows]
+        return ranks[j][k * rows:][:rows]
 
     wide = [jnp.concatenate([rank_at(j, (i - j) % 4) for j in range(4)], 1) for i in range(4)]
 

time: 103 us -> 77.5 us (0.75)
  matrix products: 31.6 us -> 3.47 us
  Pallas kernels: 3.18 us -> 14.3 us
  starting transfers between devices: 28.9 us -> 20.8 us
    dot_general x10 -> x7, matrix products: 31.6 us -> 3.47 us  [dot(): return jnp.dot(a, b, preferred_element_type=F32)]
    pallas_call x0 -> x2, Pallas kernels: none -> 13 us  [base_of(): pl.pallas_call(base_kernel, out_shape=jax.ShapeDtypeStruct((count * rows,...]
    ppermute x4 -> x1, waiting for transfers between devices: 10.1 us -> 1.9 us  [swap(): return lax.ppermute(x, axis, ((0, 1), (1, 0)))]
    ppermute x16, waiting for transfers between devices: 24.3 us -> 31.4 us  [shift(): return lax.ppermute(x, axis, pairs)]
    ppermute x16, starting transfers between devices: 25.6 us -> 20.7 us  [shift(): return lax.ppermute(x, axis, pairs)]
    ppermute x4 -> x1, starting transfers between devices: 3.29 us -> 0.07 us  [swap(): return lax.ppermute(x, axis, ((0, 1), (1, 0)))]
    pallas_call x1, Pallas kernels: 3.18 us -> 1.37 us  [place(): pl.pallas_call(place_kernel, out_shape=jax.ShapeDtypeStruct((rows, len(bl...]
  transfers between devices with their start and end apart: 20 -> 17, of which waited for: 8 -> 9; matrix products, arithmetic and copies ran while one was open for 33% -> 7% of each run, Pallas kernels for 0% -> 17%
where the time goes in v2:
time: 77.5 us; the launch traced here: 77.2 us
  waiting for transfers between devices  33.3 us (43%)
  starting transfers between devices  20.8 us (27%)
  Pallas kernels  14.3 us (18%)
  local copies, waits for them, and re-layouts  3.71 us (5%)
  matrix products  3.47 us (4%)
  other arithmetic  1.29 us (2%)
    ppermute x16, waiting for transfers between devices, shift(): return lax.ppermute(x, axis, pairs)  31.4 us
    ppermute x16, starting transfers between devices, shift(): return lax.ppermute(x, axis, pairs)  20.7 us
    pallas_call x2, Pallas kernels, base_of(): pl.pallas_call(base_kernel, out_shape=jax.ShapeDtypeStruct((count * rows,...  13 us
    dot_general x7, matrix products, dot(): return jnp.dot(a, b, preferred_element_type=F32)  3.47 us
    ppermute x1, waiting for transfers between devices, swap(): return lax.ppermute(x, axis, ((0, 1), (1, 0)))  1.9 us
  transfers between devices with their start and end apart: 17, of which 9 were waited for; matrix products, arithmetic and copies ran while one was open for 7% of the time, Pallas kernels for 17%

profile of v2, /device:TPU:0, one launch (start us, length us, event | category | flops | bytes accessed | tf_op | source)
XLA Modules:
  0.0 77.2 jit_solution(17201559000167836746)
XLA Ops:
  0.0 0.0 copy-start
  0.0 4.0 %collective-permute-start = (bf16[64,4096]{1,0:T(8,128)(2,1)}, bf16[64,4096]{1,0:T(8,128)(2,1)S(1)}, u32[]{:S(2)}, u32[]{:S(2)}) collective-permute-start(bf16[64,4096]{1,0:T(8,128)(2,1)} %bitcast.36), channel_id=1, source_target_pairs={{4,0},{12,4},{8,12},{0,8},{5,1},{13,5},{9,13},{1,9},{6,2},{14,6},{... | collective-permute-start | bytes 1572872 | tf_op jit(solution)/shard_map/ppermute | solution.py:21
  4.0 0.0 copy-start.1
  4.0 1.1 %copy-done.1 = bf16[1,64,4096]{2,1,0:T(8,128)(2,1)S(1)} copy-done((bf16[1,64,4096]{2,1,0:T(8,128)(2,1)S(1)}, bf16[1,64,4096]{2,1,0:T(8,128)(2,1)}, u32[]{:S(2)}) %copy-start.1) | copy-done | bytes 524312
  5.1 6.5 %shard_map.55 = f32[64,2048]{1,0:T(8,128)S(1)} custom-call(s32[1]{0:T(128)} %constant.133.clone.1.inner_ref, bf16[64,4096]{1,0:T(8,128)(2,1)S(1)} %bitcast.37, bf16[4096,2048]{1,0:T(8,128)(2,1)} %refs_4_.1), custom_call_target="tpu_custom_call" | custom-call | flops 1073741824 | bytes 16777216 | tf_op jit(solution)/shard_map/pallas_call | solution.py:90
  11.6 0.0 copy-start.4
  11.6 1.2 %dynamic-slice_bitcast_fusion = (bf16[1,16,2048]{2,1,0:T(8,128)(2,1)S(1)}, bf16[16,2048]{1,0:T(8,128)(2,1)S(1)}, bf16[16,2048]{1,0:T(8,128)(2,1)S(1)}, bf16[16,2048]{1,0:T(8,128)(2,1)S(1)}) fusion(bf16[64,8192]{1,0:T(8,128)(2,1)} %bitcast.41, s32[]{:T(128)S(6)} %select_n.136, s32[]{:T(128)S(6)} %select_n.138, s32[]{:T(128)S(6)} %select_n.144, ...), kind=kLoop, calls=%fused_computation.46 | loop fusion | bytes 524308 | tf_op jit(solution)/shard_map/stack | solution.py:145
  12.8 0.1 collective-permute-start.3
  12.9 2.9 %collective-permute-start.1 = (bf16[16,2048]{1,0:T(8,128)(2,1)S(1)}, bf16[16,2048]{1,0:T(8,128)(2,1)S(1)}, u32[]{:S(2)}, u32[]{:S(2)}) collective-permute-start(bf16[16,2048]{1,0:T(8,128)(2,1)S(1)} %get-tuple-element.27), channel_id=1, source_target_pairs={{4,0},{12,4},{8,12},{0,8},{5,1},{13,5},{9,13},{1,9},{6,2},{14,6},{... | collective-permute-start | bytes 196616 | tf_op jit(solution)/shard_map/ppermute | solution.py:21
  15.8 1.3 %collective-permute-start.2 = (bf16[16,2048]{1,0:T(8,128)(2,1)S(1)}, bf16[16,2048]{1,0:T(8,128)(2,1)S(1)}, u32[]{:S(2)}, u32[]{:S(2)}) collective-permute-start(bf16[16,2048]{1,0:T(8,128)(2,1)S(1)} %get-tuple-element.26), channel_id=1, source_target_pairs={{0,12},{12,0},{4,8},{8,4},{1,13},{13,1},{5,9},{9,5},{2,14},{14,2},... | collective-permute-start | bytes 196616 | tf_op jit(solution)/shard_map/ppermute | solution.py:21
  17.2 0.0 copy-done.2
  17.2 0.0 collective-permute-start.4
  17.2 0.7 constant_dynamic-slice_fusion.19
  17.9 3.7 %collective-permute-done.3 = bf16[16,2048]{1,0:T(8,128)(2,1)S(1)} collective-permute-done((bf16[16,2048]{1,0:T(8,128)(2,1)S(1)}, bf16[16,2048]{1,0:T(8,128)(2,1)S(1)}, u32[]{:S(2)}, u32[]{:S(2)}) %collective-permute-start.3) | collective-permute-done | bytes 65568 | tf_op jit(solution)/shard_map/ppermute | solution.py:21
  21.6 0.7 collective-permute-start.5
  22.3 0.0 collective-permute-done.1
  22.3 0.3 collective-permute-done.2
  22.6 0.7 pad_maximum_fusion
  23.4 0.0 collective-permute-done.refs_0_
  23.4 0.0 collective-permute-start.10
  23.4 0.0 copy-done.4
  23.4 0.1 compare_bitcast_fusion.3
  23.5 0.0 copy-done
  23.5 0.3 fusion.3
  23.8 1.6 %collective-permute-start.11 = (bf16[64,2048]{1,0:T(8,128)(2,1)}, bf16[64,2048]{1,0:T(8,128)(2,1)}, u32[]{:S(2)}, u32[]{:S(2)}) collective-permute-start(bf16[64,2048]{1,0:T(8,128)(2,1)} %bitcast.11), channel_id=1, source_target_pairs={{0,2},{1,3},{2,0},{3,1},{4,6},{5,7},{6,4},{7,5},{8,10},{9,11},{10,... | collective-permute-start | bytes 786440 | tf_op jit(solution)/shard_map/ppermute | solution.py:21
  25.3 0.4 collective-permute-start.12
  25.7 0.0 collective-permute-done.10
  25.7 1.3 %collective-permute-start.6 = (bf16[64,4096]{1,0:T(8,128)(2,1)S(1)}, bf16[64,4096]{1,0:T(8,128)(2,1)S(1)}, u32[]{:S(2)}, u32[]{:S(2)}) collective-permute-start(bf16[64,4096]{1,0:T(8,128)(2,1)S(1)} %collective-permute-done.refs_0_), channel_id=1, source_target_pairs={{8,12},{4,0},{9,13},{5,1},{10,14},{6,2},{11,15},{7,3},{24,28},{20,... | collective-permute-start | bytes 1572872 | tf_op jit(solution)/shard_map/ppermute | solution.py:21
  27.0 0.3 fusion.4
  27.3 6.0 %collective-permute-done.11 = bf16[64,2048]{1,0:T(8,128)(2,1)} collective-permute-done((bf16[64,2048]{1,0:T(8,128)(2,1)}, bf16[64,2048]{1,0:T(8,128)(2,1)}, u32[]{:S(2)}, u32[]{:S(2)}) %collective-permute-start.11) | collective-permute-done | bytes 262176 | tf_op jit(solution)/shard_map/ppermute | solution.py:21
  33.3 4.8 %collective-permute-done.12 = bf16[64,2048]{1,0:T(8,128)(2,1)} collective-permute-done((bf16[64,2048]{1,0:T(8,128)(2,1)}, bf16[64,2048]{1,0:T(8,128)(2,1)}, u32[]{:S(2)}, u32[]{:S(2)}) %collective-permute-start.12) | collective-permute-done | bytes 262176 | tf_op jit(solution)/shard_map/ppermute | solution.py:21
  38.1 1.7 %convolution_convert_fusion = bf16[256,2048]{1,0:T(8,128)(2,1)S(1)} fusion(bf16[64,2048]{1,0:T(8,128)(2,1)} %collective-permute-done.12, bf16[64,2048]{1,0:T(8,128)(2,1)} %collective-permute-done.11, bf16[64,2048]{1,0:T(8,128)(2,1)} %collective-permute-done.10, bf16[64,2048]{1,0:T(8,128)(2,1)} %bitcast.11, s32[256]{0:T(256)S(1)} %fusion.35), kind=kOutput, calls=%fused_computation | convolution fusion | flops 273219584 | bytes 2098176 | tf_op jit(solution)/shard_map/dot_general | solution.py:110
  39.8 0.0 collective-permute-done.4.refs_1_
  39.8 0.0 collective-permute-done.5.refs_2_
  39.8 5.5 %collective-permute-done.6.refs_3_ = bf16[64,4096]{1,0:T(8,128)(2,1)S(1)} collective-permute-done((bf16[64,4096]{1,0:T(8,128)(2,1)S(1)}, bf16[64,4096]{1,0:T(8,128)(2,1)S(1)}, u32[]{:S(2)}, u32[]{:S(2)}) %collective-permute-start.6) | collective-permute-done | bytes 524320 | tf_op jit(solution)/shard_map/ppermute | solution.py:21
  45.3 0.3 fusion.6
  45.6 0.3 fusion.5
  45.9 1.7 %collective-permute-start.7 = (bf16[256,64]{1,0:T(8,128)(2,1)S(1)}, bf16[256,64]{1,0:T(8,128)(2,1)S(1)}, u32[]{:S(2)}, u32[]{:S(2)}) collective-permute-start(bf16[256,64]{1,0:T(8,128)(2,1)S(1)} %pad_maximum_fusion.1), channel_id=1, source_target_pairs={{4,0},{12,4},{8,12},{0,8},{5,1},{13,5},{9,13},{1,9},{6,2},{14,6},{... | collective-permute-start | bytes 98312 | tf_op jit(solution)/shard_map/ppermute | solution.py:21
  47.6 1.3 %collective-permute-start.8 = (bf16[256,64]{1,0:T(8,128)(2,1)S(1)}, bf16[256,64]{1,0:T(8,128)(2,1)S(1)}, u32[]{:S(2)}, u32[]{:S(2)}) collective-permute-start(bf16[256,64]{1,0:T(8,128)(2,1)S(1)} %pad_maximum_fusion.1), channel_id=1, source_target_pairs={{0,12},{12,0},{4,8},{8,4},{1,13},{13,1},{5,9},{9,5},{2,14},{14,2},... | collective-permute-start | bytes 98312 | tf_op jit(solution)/shard_map/ppermute | solution.py:21
  49.0 0.6 collective-permute-start.9
  49.6 6.5 %shard_map.56 = f32[192,2048]{1,0:T(8,128)S(1)} custom-call(s32[1]{0:T(128)} %bitcast.5.inner_ref, bf16[64,4096]{1,0:T(8,128)(2,1)S(1)} %collective-permute-done.refs_0_, bf16[64,4096]{1,0:T(8,128)(2,1)S(1)} %collective-permute-done.4.refs_1_, bf16[64,4096]{1,0:T(8,128)(2,1)S(1)} %collective-permute-done.5.refs_2_, ...), custom_call_target="tpu_custom_call" | custom-call | flops 3221225472 | bytes 16777216 | tf_op jit(solution)/shard_map/pallas_call | solution.py:90
  56.1 0.1 fusion.41
  56.3 0.0 copy-start.3
  56.3 0.1 constant_dynamic-slice_fusion.16
  56.4 0.0 collective-permute-done.7
  56.4 0.0 collective-permute-done.8
  56.5 0.0 collective-permute-done.9
  56.5 0.1 pad_maximum_fusion.2
  56.6 0.1 pad_maximum_fusion.3
  56.7 0.1 pad_maximum_fusion.4
  56.8 0.1 pad_maximum_fusion.5
  56.9 0.3 copy-done.3
  57.2 0.3 fusion.2
  57.5 0.1 collective-permute-start.13
  57.6 1.9 %collective-permute-done.13 = bf16[128,2048]{1,0:T(8,128)(2,1)S(1)} collective-permute-done((bf16[128,2048]{1,0:T(8,128)(2,1)S(1)}, bf16[128,2048]{1,0:T(8,128)(2,1)S(1)}, u32[]{:S(2)}, u32[]{:S(2)}) %collective-permute-start.13) | collective-permute-done | bytes 524320 | tf_op jit(solution)/shard_map/ppermute | solution.py:25
  59.5 0.3 add_convert_fusion
  59.9 2.4 %collective-permute-start.14 = (bf16[32,2048]{1,0:T(8,128)(2,1)S(1)}, bf16[32,2048]{1,0:T(8,128)(2,1)S(1)}, u32[]{:S(2)}, u32[]{:S(2)}) collective-permute-start(bf16[32,2048]{1,0:T(8,128)(2,1)S(1)} %get-tuple-element.30), channel_id=1, source_target_pairs={{4,0},{12,4},{8,12},{0,8},{5,1},{13,5},{9,13},{1,9},{6,2},{14,6},{... | collective-permute-start | bytes 393224 | tf_op jit(solution)/shard_map/ppermute | solution.py:21
  62.3 2.5 %collective-permute-start.15 = (bf16[32,2048]{1,0:T(8,128)(2,1)S(1)}, bf16[32,2048]{1,0:T(8,128)(2,1)S(1)}, u32[]{:S(2)}, u32[]{:S(2)}) collective-permute-start(bf16[32,2048]{1,0:T(8,128)(2,1)S(1)} %get-tuple-element.29), channel_id=1, source_target_pairs={{0,12},{12,0},{4,8},{8,4},{1,13},{13,1},{5,9},{9,5},{2,14},{14,2},... | collective-permute-start | bytes 393224 | tf_op jit(solution)/shard_map/ppermute | solution.py:21
  64.7 0.0 collective-permute-start.16
  64.7 0.1 pad_add_fusion.where_ref
  64.8 1.4 %collective-permute-done.14.refs_1_ = bf16[32,2048]{1,0:T(8,128)(2,1)S(1)} collective-permute-done((bf16[32,2048]{1,0:T(8,128)(2,1)S(1)}, bf16[32,2048]{1,0:T(8,128)(2,1)S(1)}, u32[]{:S(2)}, u32[]{:S(2)}) %collective-permute-start.14) | collective-permute-done | bytes 131104 | tf_op jit(solution)/shard_map/ppermute | solution.py:21
  66.2 5.7 %collective-permute-done.15.refs_2_ = bf16[32,2048]{1,0:T(8,128)(2,1)S(1)} collective-permute-done((bf16[32,2048]{1,0:T(8,128)(2,1)S(1)}, bf16[32,2048]{1,0:T(8,128)(2,1)S(1)}, u32[]{:S(2)}, u32[]{:S(2)}) %collective-permute-start.15) | collective-permute-done | bytes 131104 | tf_op jit(solution)/shard_map/ppermute | solution.py:21
  71.9 4.0 %collective-permute-done.16.refs_3_ = bf16[32,2048]{1,0:T(8,128)(2,1)S(1)} collective-permute-done((bf16[32,2048]{1,0:T(8,128)(2,1)S(1)}, bf16[32,2048]{1,0:T(8,128)(2,1)S(1)}, u32[]{:S(2)}, u32[]{:S(2)}) %collective-permute-start.16) | collective-permute-done | bytes 131104 | tf_op jit(solution)/shard_map/ppermute | solution.py:21
  75.9 1.4 %shard_map.57 = bf16[32,8192]{1,0:T(8,128)(2,1)} custom-call(s32[4]{0:T(128)S(1)} %pad_add_fusion.where_ref, bf16[32,2048]{1,0:T(8,128)(2,1)S(1)} %get-tuple-element.31.refs_0_, bf16[32,2048]{1,0:T(8,128)(2,1)S(1)} %collective-permute-done.14.refs_1_, bf16[32,2048]{1,0:T(8,128)(2,1)S(1)} %collective-permute-done.15.refs_2_, ...), custom_call_target="tpu_custom_call" | custom-call | tf_op jit(solution)/shard_map/pallas_call | solution.py:46
  (10 shorter events, 0.2 us)
Async XLA Ops:
  0.0 23.5 %copy-start = (bf16[1,4096,64]{1,2,0:T(8,128)(2,1)S(1)}, bf16[1,4096,64]{1,2,0:T(8,128)(2,1)}, u32[]{:S(2)}) copy-start(bf16[1,4096,64]{1,2,0:T(8,128)(2,1)} %param.8) | copy-start | bytes 1572868
  0.0 23.4 %collective-permute-start = (bf16[64,4096]{1,0:T(8,128)(2,1)}, bf16[64,4096]{1,0:T(8,128)(2,1)S(1)}, u32[]{:S(2)}, u32[]{:S(2)}) collective-permute-start(bf16[64,4096]{1,0:T(8,128)(2,1)} %bitcast.36), channel_id=1, source_target_pairs={{4,0},{12,4},{8,12},{0,8},{5,1},{13,5},{9,13},{1,9},{6,2},{14,6},{... | collective-permute-start | bytes 1572872 | tf_op jit(solution)/shard_map/ppermute | solution.py:21
  4.0 1.1 %copy-start.1 = (bf16[1,64,4096]{2,1,0:T(8,128)(2,1)S(1)}, bf16[1,64,4096]{2,1,0:T(8,128)(2,1)}, u32[]{:S(2)}) copy-start(bf16[1,64,4096]{2,1,0:T(8,128)(2,1)} %param.5) | copy-start | bytes 1572868
  5.1 12.0 %copy-start.2 = (bf16[1,64,4096]{2,1,0:T(8,128)(2,1)S(1)}, bf16[1,64,4096]{2,1,0:T(8,128)(2,1)}, u32[]{:S(2)}) copy-start(bf16[1,64,4096]{2,1,0:T(8,128)(2,1)} %param.5) | copy-start | bytes 1572868
  11.6 11.8 %copy-start.4 = (s32[1,256,1]{1,2,0:T(1,128)S(1)}, s32[1,256,1]{1,2,0:T(1,128)}, u32[]{:S(2)}) copy-start(s32[1,256,1]{1,2,0:T(1,128)} %param.6) | copy-start | bytes 3076
  12.8 8.8 %collective-permute-start.3 = (bf16[16,2048]{1,0:T(8,128)(2,1)S(1)}, bf16[16,2048]{1,0:T(8,128)(2,1)S(1)}, u32[]{:S(2)}, u32[]{:S(2)}) collective-permute-start(bf16[16,2048]{1,0:T(8,128)(2,1)S(1)} %get-tuple-element.25), channel_id=1, source_target_pairs={{0,4},{4,12},{12,8},{8,0},{1,5},{5,13},{13,9},{9,1},{2,6},{6,14},{... | collective-permute-start | bytes 196616 | tf_op jit(solution)/shard_map/ppermute | solution.py:21
  12.9 9.4 %collective-permute-start.1 = (bf16[16,2048]{1,0:T(8,128)(2,1)S(1)}, bf16[16,2048]{1,0:T(8,128)(2,1)S(1)}, u32[]{:S(2)}, u32[]{:S(2)}) collective-permute-start(bf16[16,2048]{1,0:T(8,128)(2,1)S(1)} %get-tuple-element.27), channel_id=1, source_target_pairs={{4,0},{12,4},{8,12},{0,8},{5,1},{13,5},{9,13},{1,9},{6,2},{14,6},{... | collective-permute-start | bytes 196616 | tf_op jit(solution)/shard_map/ppermute | solution.py:21
  15.8 6.8 %collective-permute-start.2 = (bf16[16,2048]{1,0:T(8,128)(2,1)S(1)}, bf16[16,2048]{1,0:T(8,128)(2,1)S(1)}, u32[]{:S(2)}, u32[]{:S(2)}) collective-permute-start(bf16[16,2048]{1,0:T(8,128)(2,1)S(1)} %get-tuple-element.26), channel_id=1, source_target_pairs={{0,12},{12,0},{4,8},{8,4},{1,13},{13,1},{5,9},{9,5},{2,14},{14,2},... | collective-permute-start | bytes 196616 | tf_op jit(solution)/shard_map/ppermute | solution.py:21
  17.2 22.6 %collective-permute-start.4 = (bf16[64,4096]{1,0:T(8,128)(2,1)S(1)}, bf16[64,4096]{1,0:T(8,128)(2,1)S(1)}, u32[]{:S(2)}, u32[]{:S(2)}) collective-permute-start(bf16[64,4096]{1,0:T(8,128)(2,1)S(1)} %bitcast.38), channel_id=1, source_target_pairs={{0,4},{4,12},{12,8},{8,0},{1,5},{5,13},{13,9},{9,1},{2,6},{6,14},{... | collective-permute-start | bytes 1572872 | tf_op jit(solution)/shard_map/ppermute | solution.py:21
  21.6 18.2 %collective-permute-start.5 = (bf16[64,4096]{1,0:T(8,128)(2,1)S(1)}, bf16[64,4096]{1,0:T(8,128)(2,1)S(1)}, u32[]{:S(2)}, u32[]{:S(2)}) collective-permute-start(bf16[64,4096]{1,0:T(8,128)(2,1)S(1)} %bitcast.39), channel_id=1, source_target_pairs={{4,8},{8,4},{5,9},{9,5},{6,10},{10,6},{7,11},{11,7},{20,24},{24,20... | collective-permute-start | bytes 1572872 | tf_op jit(solution)/shard_map/ppermute | solution.py:21
  23.4 2.3 %collective-permute-start.10 = (bf16[64,2048]{1,0:T(8,128)(2,1)}, bf16[64,2048]{1,0:T(8,128)(2,1)}, u32[]{:S(2)}, u32[]{:S(2)}) collective-permute-start(bf16[64,2048]{1,0:T(8,128)(2,1)} %bitcast.11), channel_id=1, source_target_pairs={{0,1},{1,0},{2,3},{3,2},{4,5},{5,4},{6,7},{7,6},{8,9},{9,8},{10,11... | collective-permute-start | bytes 786440 | tf_op jit(solution)/shard_map/ppermute | solution.py:21
  23.8 9.5 %collective-permute-start.11 = (bf16[64,2048]{1,0:T(8,128)(2,1)}, bf16[64,2048]{1,0:T(8,128)(2,1)}, u32[]{:S(2)}, u32[]{:S(2)}) collective-permute-start(bf16[64,2048]{1,0:T(8,128)(2,1)} %bitcast.11), channel_id=1, source_target_pairs={{0,2},{1,3},{2,0},{3,1},{4,6},{5,7},{6,4},{7,5},{8,10},{9,11},{10,... | collective-permute-start | bytes 786440 | tf_op jit(solution)/shard_map/ppermute | solution.py:21
  25.3 12.7 %collective-permute-start.12 = (bf16[64,2048]{1,0:T(8,128)(2,1)}, bf16[64,2048]{1,0:T(8,128)(2,1)}, u32[]{:S(2)}, u32[]{:S(2)}) collective-permute-start(bf16[64,2048]{1,0:T(8,128)(2,1)} %bitcast.11), channel_id=1, source_target_pairs={{0,3},{1,2},{2,1},{3,0},{4,7},{5,6},{6,5},{7,4},{8,11},{9,10},{10,... | collective-permute-start | bytes 786440 | tf_op jit(solution)/shard_map/ppermute | solution.py:21
  25.7 19.6 %collective-permute-start.6 = (bf16[64,4096]{1,0:T(8,128)(2,1)S(1)}, bf16[64,4096]{1,0:T(8,128)(2,1)S(1)}, u32[]{:S(2)}, u32[]{:S(2)}) collective-permute-start(bf16[64,4096]{1,0:T(8,128)(2,1)S(1)} %collective-permute-done.refs_0_), channel_id=1, source_target_pairs={{8,12},{4,0},{9,13},{5,1},{10,14},{6,2},{11,15},{7,3},{24,28},{20,... | collective-permute-start | bytes 1572872 | tf_op jit(solution)/shard_map/ppermute | solution.py:21
  45.9 10.5 %collective-permute-start.7 = (bf16[256,64]{1,0:T(8,128)(2,1)S(1)}, bf16[256,64]{1,0:T(8,128)(2,1)S(1)}, u32[]{:S(2)}, u32[]{:S(2)}) collective-permute-start(bf16[256,64]{1,0:T(8,128)(2,1)S(1)} %pad_maximum_fusion.1), channel_id=1, source_target_pairs={{4,0},{12,4},{8,12},{0,8},{5,1},{13,5},{9,13},{1,9},{6,2},{14,6},{... | collective-permute-start | bytes 98312 | tf_op jit(solution)/shard_map/ppermute | solution.py:21
  47.6 8.8 %collective-permute-start.8 = (bf16[256,64]{1,0:T(8,128)(2,1)S(1)}, bf16[256,64]{1,0:T(8,128)(2,1)S(1)}, u32[]{:S(2)}, u32[]{:S(2)}) collective-permute-start(bf16[256,64]{1,0:T(8,128)(2,1)S(1)} %pad_maximum_fusion.1), channel_id=1, source_target_pairs={{0,12},{12,0},{4,8},{8,4},{1,13},{13,1},{5,9},{9,5},{2,14},{14,2},... | collective-permute-start | bytes 98312 | tf_op jit(solution)/shard_map/ppermute | solution.py:21
  49.0 7.5 %collective-permute-start.9 = (bf16[256,64]{1,0:T(8,128)(2,1)S(1)}, bf16[256,64]{1,0:T(8,128)(2,1)S(1)}, u32[]{:S(2)}, u32[]{:S(2)}) collective-permute-start(bf16[256,64]{1,0:T(8,128)(2,1)S(1)} %pad_maximum_fusion.1), channel_id=1, source_target_pairs={{0,4},{4,12},{12,8},{8,0},{1,5},{5,13},{13,9},{9,1},{2,6},{6,14},{... | collective-permute-start | bytes 98312 | tf_op jit(solution)/shard_map/ppermute | solution.py:21
  56.3 1.0 %copy-start.3 = (f32[32,2048]{1,0:T(8,128)S(1)}, f32[32,2048]{1,0:T(8,128)}, u32[]{:S(2)}) copy-start(f32[32,2048]{1,0:T(8,128)} %get-tuple-element.33) | copy-start | bytes 786436
  57.5 2.0 %collective-permute-start.13 = (bf16[128,2048]{1,0:T(8,128)(2,1)S(1)}, bf16[128,2048]{1,0:T(8,128)(2,1)S(1)}, u32[]{:S(2)}, u32[]{:S(2)}) collective-permute-start(bf16[128,2048]{1,0:T(8,128)(2,1)S(1)} %fusion.2), channel_id=1, source_target_pairs={{0,1},{1,0},{2,3},{3,2},{4,5},{5,4},{6,7},{7,6},{8,9},{9,8},{10,11... | collective-permute-start | bytes 1572872 | tf_op jit(solution)/shard_map/ppermute | solution.py:25
  59.9 6.3 %collective-permute-start.14 = (bf16[32,2048]{1,0:T(8,128)(2,1)S(1)}, bf16[32,2048]{1,0:T(8,128)(2,1)S(1)}, u32[]{:S(2)}, u32[]{:S(2)}) collective-permute-start(bf16[32,2048]{1,0:T(8,128)(2,1)S(1)} %get-tuple-element.30), channel_id=1, source_target_pairs={{4,0},{12,4},{8,12},{0,8},{5,1},{13,5},{9,13},{1,9},{6,2},{14,6},{... | collective-permute-start | bytes 393224 | tf_op jit(solution)/shard_map/ppermute | solution.py:21
  62.3 9.6 %collective-permute-start.15 = (bf16[32,2048]{1,0:T(8,128)(2,1)S(1)}, bf16[32,2048]{1,0:T(8,128)(2,1)S(1)}, u32[]{:S(2)}, u32[]{:S(2)}) collective-permute-start(bf16[32,2048]{1,0:T(8,128)(2,1)S(1)} %get-tuple-element.29), channel_id=1, source_target_pairs={{0,12},{12,0},{4,8},{8,4},{1,13},{13,1},{5,9},{9,5},{2,14},{14,2},... | collective-permute-start | bytes 393224 | tf_op jit(solution)/shard_map/ppermute | solution.py:21
  64.7 11.1 %collective-permute-start.16 = (bf16[32,2048]{1,0:T(8,128)(2,1)S(1)}, bf16[32,2048]{1,0:T(8,128)(2,1)S(1)}, u32[]{:S(2)}, u32[]{:S(2)}) collective-permute-start(bf16[32,2048]{1,0:T(8,128)(2,1)S(1)} %get-tuple-element.28), channel_id=1, source_target_pairs={{0,4},{4,12},{12,8},{8,0},{1,5},{5,13},{13,9},{9,1},{2,6},{6,14},{... | collective-permute-start | bytes 393224 | tf_op jit(solution)/shard_map/ppermute | solution.py:21

commit v3 on v2

--- a/solution.py
+++ b/solution.py
@@ -1,3 +1,5 @@
+import functools
+
 import jax
 import jax.numpy as jnp
 from jax import lax
@@ -52,15 +54,16 @@
     )(where, *blocks)
 
 
-def base_kernel(inner_ref, *refs):
-    *x_refs, weight_ref, out_ref, x_ref, held_ref, sems = refs
+def base_kernel(inner_ref, *refs, blocks, parts):
+    x_refs, part_refs, weight_ref = refs[:blocks], refs[blocks : blocks + parts], refs[blocks + parts]
+    out_ref, *panel_refs, x_ref, held_ref, sems = refs[blocks + parts + 1 :]
     count, depth, _ = held_ref.shape
 
-    def part(k):
+    def piece(k):
         return pltpu.make_async_copy(weight_ref.at[pl.ds(k * depth, depth)], held_ref.at[k], sems.at[k])
 
     for k in range(count):
-        part(k).start()
+        piece(k).start()
     rows = x_refs[0].shape[0]
     for i, block in enumerate(x_refs):
         at = pl.ds(min(i, 2) * rows, rows)
@@ -72,8 +75,23 @@
             def _(at=at, block=block):
                 x_ref[at] = block[...]
 
+    for k, part_ref in enumerate(part_refs):
+        share = part_ref.shape[0] // 8
+        for slot in range(4):
+            first = part_ref[slot * share : (slot + 1) * share]
+            second = part_ref[(4 + slot) * share : (5 + slot) * share]
+            at = pl.multiple_of((slot * parts + (inner_ref[1] ^ k)) * 2 * share, 16)
+
+            @pl.when(inner_ref[2] == 0)
+            def _(at=at, first=first, second=second):
+                panel_refs[0][pl.ds(at, 2 * share)] = jnp.concatenate([first, second])
+
+            @pl.when(inner_ref[2] == 1)
+            def _(at=at, first=first, second=second):
+                panel_refs[0][pl.ds(at, 2 * share)] = jnp.concatenate([second, first])
+
     for k in range(count):
-        part(k).wait()
+        piece(k).wait()
         term = dot(x_ref[:, k * depth : (k + 1) * depth], held_ref[k])
         if k == 0:
             out_ref[...] = term
@@ -81,29 +99,32 @@
             out_ref[...] += term
 
 
-def base_of(inner, blocks, weight):
+def base_of(facts, blocks, parts, weight):
     rows, depth = blocks[0].shape
     count = min(len(blocks), 3)
     width = weight.shape[1]
-    parts = 8
+    pieces = 8
     vmem = pl.BlockSpec(memory_space=pltpu.VMEM)
+    shapes = [jax.ShapeDtypeStruct((count * rows, width), F32)]
+    if parts:
+        shapes.append(jax.ShapeDtypeStruct((len(parts) * parts[0].shape[0], width), parts[0].dtype))
     return pl.pallas_call(
-        base_kernel,
-        out_shape=jax.ShapeDtypeStruct((count * rows, width), F32),
+        functools.partial(base_kernel, blocks=len(blocks), parts=len(parts)),
+        out_shape=shapes,
         in_specs=[pl.BlockSpec(memory_space=pltpu.SMEM)]
-        + [vmem] * len(blocks)
+        + [vmem] * (len(blocks) + len(parts))
         + [pl.BlockSpec(memory_space=pl.ANY)],
-        out_specs=vmem,
+        out_specs=[vmem] * len(shapes),
         scratch_shapes=[
             pltpu.VMEM((count * rows, depth), weight.dtype),
-            pltpu.VMEM((parts, depth // parts, width), weight.dtype),
-            pltpu.SemaphoreType.DMA((parts,)),
+            pltpu.VMEM((pieces, depth // pieces, width), weight.dtype),
+            pltpu.SemaphoreType.DMA((pieces,)),
         ],
         compiler_params=pltpu.CompilerParams(vmem_limit_bytes=VMEM_LIMIT),
         cost_estimate=pl.CostEstimate(
             flops=2 * count * rows * depth * width, bytes_accessed=weight.size * 2, transcendentals=0
         ),
-    )(inner, *blocks, weight)
+    )(facts, *blocks, *parts, weight)
 
 
 def dot(a, b):
@@ -128,7 +149,7 @@
 
     x1 = shift(own, FROM_NEXT)
     inner = (me == 1) | (me == 2)
-    base0 = base_of(jnp.ones((1,), jnp.int32), [own], query_weight)
+    [base0] = base_of(jnp.ones((3,), jnp.int32), [own], [], query_weight)
     own, base0 = lax.optimization_barrier((own, base0))
     x3 = shift(own, FROM_LAST)
     x2a = shift(own, INNER)
@@ -136,23 +157,21 @@
     inside = ("replica", "tp")
     peers = lax.axis_size(inside)
     peer = lax.axis_index(inside)
-    share = rank // peers
-    part = lax.dynamic_slice_in_dim(after(expand_weight[0], base0), peer * share, share)
+    group = lax.axis_index("groups")
+    share = rank // peers // 2
+    part = lax.dynamic_slice_in_dim(after(expand_weight[0], base0), (peer * 2 + group) * share, share)
 
     def columns(i):
         return lax.dynamic_slice_in_dim(part, planes[i] * width, width, 1)
 
     part = jnp.stack(
         [columns(0), shift(columns(3), FROM_NEXT), shift(columns(2), OPPOSITE), shift(columns(1), FROM_LAST)]
-    ).reshape(4 * share, width)
+    )
     x1, part = lax.optimization_barrier((x1, part))
     x2b = shift(x1, RELAY)
     x3, x2a, x2b = lax.optimization_barrier((x3, x2a, x2b))
+    part = jnp.concatenate([part.reshape(4 * share, width), swap(part, "groups").reshape(4 * share, width)])
     parts = [part] + [shift(part, [(i, i ^ k) for i in range(peers)], inside) for k in range(1, peers)]
-    to = jnp.arange(4 * rank)[:, None]
-    at = jnp.arange(4 * rank)[None, :]
-    picked = at == ((to % rank // share) ^ peer) * (4 * share) + to // rank * share + to % share
-    panels = dot(picked.astype(BF16), jnp.concatenate(parts)).astype(BF16)
 
     x2 = jnp.where(inner, x2a, x2b)
     ranks = []
@@ -161,7 +180,8 @@
         ranks.append(jnp.where(named, dot(x, shrink), 0.0).astype(BF16))
     ranks = jnp.concatenate(ranks)
     ranks = [ranks, shift(ranks, FROM_NEXT), shift(ranks, OPPOSITE), shift(ranks, FROM_LAST)]
-    base = base_of(inner.astype(jnp.int32)[None], [x1, x3, x2a, x2b], query_weight)
+    facts = jnp.stack([inner.astype(jnp.int32), peer.astype(jnp.int32), group.astype(jnp.int32)])
+    base, panels = base_of(facts, [x1, x3, x2a, x2b], parts, query_weight)
     base = [base0, base[:rows], base[2 * rows :], base[rows : 2 * rows]]
 
     def rank_at(j, k):

time: 77.5 us -> 76.8 us (level)
  starting transfers between devices: 20.8 us -> 23.1 us
  matrix products: 3.47 us -> 1.85 us
  Pallas kernels: 14.3 us -> 15.4 us
  local copies, waits for them, and re-layouts: 3.71 us -> 2.64 us
    ppermute x16, waiting for transfers between devices: 31.4 us -> 27.5 us  [shift(): return lax.ppermute(x, axis, pairs)]
    ppermute x1 -> x2, waiting for transfers between devices: 1.9 us -> 5.05 us  [swap(): return lax.ppermute(x, axis, ((0, 1), (1, 0)))]
    dot_general x7 -> x6, matrix products: 3.47 us -> 1.85 us  [dot(): return jnp.dot(a, b, preferred_element_type=F32)]
    ppermute x1 -> x2, starting transfers between devices: 0.07 us -> 1.6 us  [swap(): return lax.ppermute(x, axis, ((0, 1), (1, 0)))]
    pallas_call x2, Pallas kernels: 13 us -> 14 us  [base_of(): pl.pallas_call(functools.partial(base_kernel, blocks=len(blocks), parts=l...]
  transfers between devices with their start and end apart: 17 -> 18, of which waited for: 9 -> 6; matrix products, arithmetic and copies ran while one was open for 7% -> 4% of each run, Pallas kernels for 17% -> 18%
where the time goes in v3:
time: 76.8 us; the launch traced here: 76.5 us
  waiting for transfers between devices  32.6 us (42%)
  starting transfers between devices  23.1 us (30%)
  Pallas kernels  15.4 us (20%)
  local copies, waits for them, and re-layouts  2.64 us (3%)
  matrix products  1.85 us (2%)
    ppermute x16, waiting for transfers between devices, shift(): return lax.ppermute(x, axis, pairs)  27.5 us
    ppermute x16, starting transfers between devices, shift(): return lax.ppermute(x, axis, pairs)  21.5 us
    pallas_call x2, Pallas kernels, base_of(): pl.pallas_call(functools.partial(base_kernel, blocks=len(blocks), parts=l...  14 us
    ppermute x2, waiting for transfers between devices, swap(): return lax.ppermute(x, axis, ((0, 1), (1, 0)))  5.05 us
    dot_general x6, matrix products, dot(): return jnp.dot(a, b, preferred_element_type=F32)  1.85 us
    ppermute x2, starting transfers between devices, swap(): return lax.ppermute(x, axis, ((0, 1), (1, 0)))  1.6 us
  transfers between devices with their start and end apart: 18, of which 6 were waited for; matrix products, arithmetic and copies ran while one was open for 4% of the time, Pallas kernels for 18%

profile of v3, /device:TPU:0, one launch (start us, length us, event | category | flops | bytes accessed | tf_op | source)
XLA Modules:
  0.0 76.5 jit_solution(13785442120433886071)
XLA Ops:
  0.0 0.0 copy-start
  0.0 4.0 %collective-permute-start = (bf16[64,4096]{1,0:T(8,128)(2,1)}, bf16[64,4096]{1,0:T(8,128)(2,1)S(1)}, u32[]{:S(2)}, u32[]{:S(2)}) collective-permute-start(bf16[64,4096]{1,0:T(8,128)(2,1)} %bitcast.39), channel_id=1, source_target_pairs={{4,0},{12,4},{8,12},{0,8},{5,1},{13,5},{9,13},{1,9},{6,2},{14,6},{... | collective-permute-start | bytes 1572872 | tf_op jit(solution)/shard_map/ppermute | solution.py:23
  4.0 0.0 copy-start.1
  4.0 1.1 %copy-done.1 = bf16[1,64,4096]{2,1,0:T(8,128)(2,1)S(1)} copy-done((bf16[1,64,4096]{2,1,0:T(8,128)(2,1)S(1)}, bf16[1,64,4096]{2,1,0:T(8,128)(2,1)}, u32[]{:S(2)}) %copy-start.1) | copy-done | bytes 524312
  5.1 0.0 copy-start.2
  5.1 0.0 copy-start.3
  5.1 6.9 %shard_map.55 = f32[64,2048]{1,0:T(8,128)S(1)} custom-call(s32[3]{0:T(128)S(1)} %broadcast_3_inner_ref.2.inner_ref, bf16[64,4096]{1,0:T(8,128)(2,1)S(1)} %bitcast.40, bf16[4096,2048]{1,0:T(8,128)(2,1)} %refs_8_.1), custom_call_target="tpu_custom_call" | custom-call | flops 1073741824 | bytes 16777216 | tf_op jit(solution)/shard_map/pallas_call | solution.py:111
  12.1 1.1 %dynamic-slice_bitcast_fusion = (bf16[1,8,2048]{2,1,0:T(8,128)(2,1)S(1)}, bf16[8,2048]{1,0:T(8,128)(2,1)S(1)}, bf16[8,2048]{1,0:T(8,128)(2,1)S(1)}, bf16[8,2048]{1,0:T(8,128)(2,1)S(1)}) fusion(bf16[64,8192]{1,0:T(8,128)(2,1)} %bitcast.49, s32[]{:T(128)S(6)} %select_n.98, s32[]{:T(128)S(6)} %select_n.100, s32[]{:T(128)S(6)} %select_n.106, s32[]{:T(128)S(6)} %select_n.104, ...), kind=kLoop, calls=%fused_computation.42 | loop fusion | bytes 262164 | tf_op jit(solution)/shard_map/stack | solution.py:167
  13.2 0.1 collective-permute-start.3
  13.3 3.0 %collective-permute-start.2 = (bf16[8,2048]{1,0:T(8,128)(2,1)S(1)}, bf16[8,2048]{1,0:T(8,128)(2,1)S(1)}, u32[]{:S(2)}, u32[]{:S(2)}) collective-permute-start(bf16[8,2048]{1,0:T(8,128)(2,1)S(1)} %get-tuple-element.30), channel_id=1, source_target_pairs={{0,12},{12,0},{4,8},{8,4},{1,13},{13,1},{5,9},{9,5},{2,14},{14,2},... | collective-permute-start | bytes 98312 | tf_op jit(solution)/shard_map/ppermute | solution.py:23
  16.3 0.4 collective-permute-start.1
  16.6 0.0 copy-done.2
  16.6 0.7 collective-permute-start.5
  17.4 0.0 copy-done.3
  17.4 0.1 compare_bitcast_fusion.3
  17.5 0.0 copy-done
  17.5 0.3 fusion.5
  17.8 0.8 %collective-permute-done.3 = bf16[8,2048]{1,0:T(8,128)(2,1)S(1)} collective-permute-done((bf16[8,2048]{1,0:T(8,128)(2,1)S(1)}, bf16[8,2048]{1,0:T(8,128)(2,1)S(1)}, u32[]{:S(2)}, u32[]{:S(2)}) %collective-permute-start.3) | collective-permute-done | bytes 32800 | tf_op jit(solution)/shard_map/ppermute | solution.py:23
  18.7 2.1 %collective-permute-start.4 = (bf16[64,4096]{1,0:T(8,128)(2,1)S(1)}, bf16[64,4096]{1,0:T(8,128)(2,1)S(1)}, u32[]{:S(2)}, u32[]{:S(2)}) collective-permute-start(bf16[64,4096]{1,0:T(8,128)(2,1)S(1)} %bitcast.43), channel_id=1, source_target_pairs={{0,4},{4,12},{12,8},{8,0},{1,5},{5,13},{13,9},{9,1},{2,6},{6,14},{... | collective-permute-start | bytes 1572872 | tf_op jit(solution)/shard_map/ppermute | solution.py:23
  20.8 0.0 collective-permute-done.2
  20.8 0.0 collective-permute-done.1
  20.8 0.0 collective-permute-done.refs_0_
  20.8 1.3 %collective-permute-start.6 = (bf16[64,4096]{1,0:T(8,128)(2,1)S(1)}, bf16[64,4096]{1,0:T(8,128)(2,1)S(1)}, u32[]{:S(2)}, u32[]{:S(2)}) collective-permute-start(bf16[64,4096]{1,0:T(8,128)(2,1)S(1)} %collective-permute-done.refs_0_), channel_id=1, source_target_pairs={{8,12},{4,0},{9,13},{5,1},{10,14},{6,2},{11,15},{7,3},{24,28},{20,... | collective-permute-start | bytes 1572872 | tf_op jit(solution)/shard_map/ppermute | solution.py:23
  22.1 0.1 pad_add_fusion.1.inner_ref
  22.2 1.5 %collective-permute-start.7 = (bf16[4,8,2048]{2,1,0:T(8,128)(2,1)S(1)}, bf16[4,8,2048]{2,1,0:T(8,128)(2,1)S(1)}, u32[]{:S(2)}, u32[]{:S(2)}) collective-permute-start(bf16[4,8,2048]{2,1,0:T(8,128)(2,1)S(1)} %pad_maximum_fusion.1), channel_id=1, source_target_pairs={{0,16},{16,0},{1,17},{17,1},{2,18},{18,2},{3,19},{19,3},{4,20},{20... | collective-permute-start | bytes 393224 | tf_op jit(solution)/shard_map/ppermute | solution.py:27
  23.7 0.3 fusion.6
  24.0 3.2 %collective-permute-done.7 = bf16[4,8,2048]{2,1,0:T(8,128)(2,1)S(1)} collective-permute-done((bf16[4,8,2048]{2,1,0:T(8,128)(2,1)S(1)}, bf16[4,8,2048]{2,1,0:T(8,128)(2,1)S(1)}, u32[]{:S(2)}, u32[]{:S(2)}) %collective-permute-start.7) | collective-permute-done | bytes 131104 | tf_op jit(solution)/shard_map/ppermute | solution.py:27
  27.2 0.1 collective-permute-start.10
  27.3 1.6 %collective-permute-start.9 = (bf16[64,2048]{1,0:T(8,128)(2,1)S(1)}, bf16[64,2048]{1,0:T(8,128)(2,1)S(1)}, u32[]{:S(2)}, u32[]{:S(2)}) collective-permute-start(bf16[64,2048]{1,0:T(8,128)(2,1)S(1)} %pad_maximum_fusion.refs_4_), channel_id=1, source_target_pairs={{0,2},{1,3},{2,0},{3,1},{4,6},{5,7},{6,4},{7,5},{8,10},{9,11},{10,... | collective-permute-start | bytes 786440 | tf_op jit(solution)/shard_map/ppermute | solution.py:23
  28.8 0.0 collective-permute-done.5.refs_2_
  28.8 0.3 collective-permute-start.8
  29.1 14.4 %collective-permute-done.4.refs_1_ = bf16[64,4096]{1,0:T(8,128)(2,1)S(1)} collective-permute-done((bf16[64,4096]{1,0:T(8,128)(2,1)S(1)}, bf16[64,4096]{1,0:T(8,128)(2,1)S(1)}, u32[]{:S(2)}, u32[]{:S(2)}) %collective-permute-start.4) | collective-permute-done | bytes 524320 | tf_op jit(solution)/shard_map/ppermute | solution.py:23
  43.6 2.6 %collective-permute-done.6.refs_3_ = bf16[64,4096]{1,0:T(8,128)(2,1)S(1)} collective-permute-done((bf16[64,4096]{1,0:T(8,128)(2,1)S(1)}, bf16[64,4096]{1,0:T(8,128)(2,1)S(1)}, u32[]{:S(2)}, u32[]{:S(2)}) %collective-permute-start.6) | collective-permute-done | bytes 524320 | tf_op jit(solution)/shard_map/ppermute | solution.py:23
  46.2 0.3 fusion.7
  46.5 0.3 fusion.8
  46.9 0.1 collective-permute-start.13
  46.9 2.7 %collective-permute-start.12 = (bf16[256,64]{1,0:T(8,128)(2,1)S(1)}, bf16[256,64]{1,0:T(8,128)(2,1)S(1)}, u32[]{:S(2)}, u32[]{:S(2)}) collective-permute-start(bf16[256,64]{1,0:T(8,128)(2,1)S(1)} %pad_maximum_fusion.2), channel_id=1, source_target_pairs={{0,12},{12,0},{4,8},{8,4},{1,13},{13,1},{5,9},{9,5},{2,14},{14,2},... | collective-permute-start | bytes 98312 | tf_op jit(solution)/shard_map/ppermute | solution.py:23
  49.6 0.0 collective-permute-done.10.refs_7_
  49.7 1.9 %collective-permute-start.11 = (bf16[256,64]{1,0:T(8,128)(2,1)S(1)}, bf16[256,64]{1,0:T(8,128)(2,1)S(1)}, u32[]{:S(2)}, u32[]{:S(2)}) collective-permute-start(bf16[256,64]{1,0:T(8,128)(2,1)S(1)} %pad_maximum_fusion.2), channel_id=1, source_target_pairs={{4,0},{12,4},{8,12},{0,8},{5,1},{13,5},{9,13},{1,9},{6,2},{14,6},{... | collective-permute-start | bytes 98312 | tf_op jit(solution)/shard_map/ppermute | solution.py:23
  51.6 0.0 collective-permute-done.9.refs_6_
  51.6 0.0 collective-permute-done.8.refs_5_
  51.6 7.1 %shard_map.56 = (f32[192,2048]{1,0:T(8,128)S(1)}, bf16[256,2048]{1,0:T(8,128)(2,1)S(1)}) custom-call(s32[3]{0:T(128)S(1)} %pad_add_fusion.1.inner_ref, bf16[64,4096]{1,0:T(8,128)(2,1)S(1)} %collective-permute-done.refs_0_, bf16[64,4096]{1,0:T(8,128)(2,1)S(1)} %collective-permute-done.4.refs_1_, bf16[64,4096]{1,0:T(8,128)(2,1)S(1)} %collective-permute-done.5.refs_2_, ...), custom_call_target="tpu_custom_call" | custom-call | flops 3221225472 | bytes 16777216 | tf_op jit(solution)/shard_map/pallas_call | solution.py:111
  58.7 0.1 fusion.31
  58.8 0.1 constant_dynamic-slice_fusion.4
  59.0 0.0 collective-permute-done.13
  59.0 0.0 collective-permute-done.12
  59.0 0.0 collective-permute-done.11
  59.1 0.1 pad_maximum_fusion.5
  59.2 0.1 pad_maximum_fusion.6
  59.3 0.1 pad_maximum_fusion.4
  59.4 0.1 pad_maximum_fusion.3
  59.5 0.3 fusion.4
  59.8 0.1 collective-permute-start.14
  59.9 1.9 %collective-permute-done.14 = bf16[128,2048]{1,0:T(8,128)(2,1)S(1)} collective-permute-done((bf16[128,2048]{1,0:T(8,128)(2,1)S(1)}, bf16[128,2048]{1,0:T(8,128)(2,1)S(1)}, u32[]{:S(2)}, u32[]{:S(2)}) %collective-permute-start.14) | collective-permute-done | bytes 524320 | tf_op jit(solution)/shard_map/ppermute | solution.py:27
  61.8 0.3 fusion.3
  62.2 0.1 collective-permute-start.17
  62.3 1.4 %collective-permute-start.16 = (bf16[32,2048]{1,0:T(8,128)(2,1)S(1)}, bf16[32,2048]{1,0:T(8,128)(2,1)S(1)}, u32[]{:S(2)}, u32[]{:S(2)}) collective-permute-start(bf16[32,2048]{1,0:T(8,128)(2,1)S(1)} %get-tuple-element.33), channel_id=1, source_target_pairs={{0,12},{12,0},{4,8},{8,4},{1,13},{13,1},{5,9},{9,5},{2,14},{14,2},... | collective-permute-start | bytes 393224 | tf_op jit(solution)/shard_map/ppermute | solution.py:23
  63.7 1.7 %collective-permute-start.15 = (bf16[32,2048]{1,0:T(8,128)(2,1)S(1)}, bf16[32,2048]{1,0:T(8,128)(2,1)S(1)}, u32[]{:S(2)}, u32[]{:S(2)}) collective-permute-start(bf16[32,2048]{1,0:T(8,128)(2,1)S(1)} %get-tuple-element.34), channel_id=1, source_target_pairs={{4,0},{12,4},{8,12},{0,8},{5,1},{13,5},{9,13},{1,9},{6,2},{14,6},{... | collective-permute-start | bytes 393224 | tf_op jit(solution)/shard_map/ppermute | solution.py:23
  65.5 0.1 pad_add_fusion.where_ref
  65.5 9.6 %collective-permute-done.17.refs_3_ = bf16[32,2048]{1,0:T(8,128)(2,1)S(1)} collective-permute-done((bf16[32,2048]{1,0:T(8,128)(2,1)S(1)}, bf16[32,2048]{1,0:T(8,128)(2,1)S(1)}, u32[]{:S(2)}, u32[]{:S(2)}) %collective-permute-start.17) | collective-permute-done | bytes 131104 | tf_op jit(solution)/shard_map/ppermute | solution.py:23
  75.1 0.0 collective-permute-done.16.refs_2_
  75.1 0.0 collective-permute-done.15.refs_1_
  75.1 1.4 %shard_map.57 = bf16[32,8192]{1,0:T(8,128)(2,1)} custom-call(s32[4]{0:T(128)S(1)} %pad_add_fusion.where_ref, bf16[32,2048]{1,0:T(8,128)(2,1)S(1)} %get-tuple-element.35.refs_0_, bf16[32,2048]{1,0:T(8,128)(2,1)S(1)} %collective-permute-done.15.refs_1_, bf16[32,2048]{1,0:T(8,128)(2,1)S(1)} %collective-permute-done.16.refs_2_, ...), custom_call_target="tpu_custom_call" | custom-call | tf_op jit(solution)/shard_map/pallas_call | solution.py:48
  (12 shorter events, 0.2 us)
Async XLA Ops:
  0.0 17.5 %copy-start = (bf16[1,4096,64]{1,2,0:T(8,128)(2,1)S(1)}, bf16[1,4096,64]{1,2,0:T(8,128)(2,1)}, u32[]{:S(2)}) copy-start(bf16[1,4096,64]{1,2,0:T(8,128)(2,1)} %param.8) | copy-start | bytes 1572868
  0.0 20.8 %collective-permute-start = (bf16[64,4096]{1,0:T(8,128)(2,1)}, bf16[64,4096]{1,0:T(8,128)(2,1)S(1)}, u32[]{:S(2)}, u32[]{:S(2)}) collective-permute-start(bf16[64,4096]{1,0:T(8,128)(2,1)} %bitcast.39), channel_id=1, source_target_pairs={{4,0},{12,4},{8,12},{0,8},{5,1},{13,5},{9,13},{1,9},{6,2},{14,6},{... | collective-permute-start | bytes 1572872 | tf_op jit(solution)/shard_map/ppermute | solution.py:23
  4.0 1.1 %copy-start.1 = (bf16[1,64,4096]{2,1,0:T(8,128)(2,1)S(1)}, bf16[1,64,4096]{2,1,0:T(8,128)(2,1)}, u32[]{:S(2)}) copy-start(bf16[1,64,4096]{2,1,0:T(8,128)(2,1)} %param.5) | copy-start | bytes 1572868
  5.1 11.5 %copy-start.2 = (bf16[1,64,4096]{2,1,0:T(8,128)(2,1)S(1)}, bf16[1,64,4096]{2,1,0:T(8,128)(2,1)}, u32[]{:S(2)}) copy-start(bf16[1,64,4096]{2,1,0:T(8,128)(2,1)} %param.5) | copy-start | bytes 1572868
  5.1 12.2 %copy-start.3 = (s32[1,256,1]{1,2,0:T(1,128)S(1)}, s32[1,256,1]{1,2,0:T(1,128)}, u32[]{:S(2)}) copy-start(s32[1,256,1]{1,2,0:T(1,128)} %param.6) | copy-start | bytes 3076
  13.2 5.4 %collective-permute-start.3 = (bf16[8,2048]{1,0:T(8,128)(2,1)S(1)}, bf16[8,2048]{1,0:T(8,128)(2,1)S(1)}, u32[]{:S(2)}, u32[]{:S(2)}) collective-permute-start(bf16[8,2048]{1,0:T(8,128)(2,1)S(1)} %get-tuple-element.29), channel_id=1, source_target_pairs={{0,4},{4,12},{12,8},{8,0},{1,5},{5,13},{13,9},{9,1},{2,6},{6,14},{... | collective-permute-start | bytes 98312 | tf_op jit(solution)/shard_map/ppermute | solution.py:23
  13.3 7.5 %collective-permute-start.2 = (bf16[8,2048]{1,0:T(8,128)(2,1)S(1)}, bf16[8,2048]{1,0:T(8,128)(2,1)S(1)}, u32[]{:S(2)}, u32[]{:S(2)}) collective-permute-start(bf16[8,2048]{1,0:T(8,128)(2,1)S(1)} %get-tuple-element.30), channel_id=1, source_target_pairs={{0,12},{12,0},{4,8},{8,4},{1,13},{13,1},{5,9},{9,5},{2,14},{14,2},... | collective-permute-start | bytes 98312 | tf_op jit(solution)/shard_map/ppermute | solution.py:23
  16.3 4.5 %collective-permute-start.1 = (bf16[8,2048]{1,0:T(8,128)(2,1)S(1)}, bf16[8,2048]{1,0:T(8,128)(2,1)S(1)}, u32[]{:S(2)}, u32[]{:S(2)}) collective-permute-start(bf16[8,2048]{1,0:T(8,128)(2,1)S(1)} %get-tuple-element.31), channel_id=1, source_target_pairs={{4,0},{12,4},{8,12},{0,8},{5,1},{13,5},{9,13},{1,9},{6,2},{14,6},{... | collective-permute-start | bytes 98312 | tf_op jit(solution)/shard_map/ppermute | solution.py:23
  16.6 12.2 %collective-permute-start.5 = (bf16[64,4096]{1,0:T(8,128)(2,1)S(1)}, bf16[64,4096]{1,0:T(8,128)(2,1)S(1)}, u32[]{:S(2)}, u32[]{:S(2)}) collective-permute-start(bf16[64,4096]{1,0:T(8,128)(2,1)S(1)} %bitcast.41), channel_id=1, source_target_pairs={{4,8},{8,4},{5,9},{9,5},{6,10},{10,6},{7,11},{11,7},{20,24},{24,20... | collective-permute-start | bytes 1572872 | tf_op jit(solution)/shard_map/ppermute | solution.py:23
  18.7 24.9 %collective-permute-start.4 = (bf16[64,4096]{1,0:T(8,128)(2,1)S(1)}, bf16[64,4096]{1,0:T(8,128)(2,1)S(1)}, u32[]{:S(2)}, u32[]{:S(2)}) collective-permute-start(bf16[64,4096]{1,0:T(8,128)(2,1)S(1)} %bitcast.43), channel_id=1, source_target_pairs={{0,4},{4,12},{12,8},{8,0},{1,5},{5,13},{13,9},{9,1},{2,6},{6,14},{... | collective-permute-start | bytes 1572872 | tf_op jit(solution)/shard_map/ppermute | solution.py:23
  20.8 25.4 %collective-permute-start.6 = (bf16[64,4096]{1,0:T(8,128)(2,1)S(1)}, bf16[64,4096]{1,0:T(8,128)(2,1)S(1)}, u32[]{:S(2)}, u32[]{:S(2)}) collective-permute-start(bf16[64,4096]{1,0:T(8,128)(2,1)S(1)} %collective-permute-done.refs_0_), channel_id=1, source_target_pairs={{8,12},{4,0},{9,13},{5,1},{10,14},{6,2},{11,15},{7,3},{24,28},{20,... | collective-permute-start | bytes 1572872 | tf_op jit(solution)/shard_map/ppermute | solution.py:23
  22.2 5.0 %collective-permute-start.7 = (bf16[4,8,2048]{2,1,0:T(8,128)(2,1)S(1)}, bf16[4,8,2048]{2,1,0:T(8,128)(2,1)S(1)}, u32[]{:S(2)}, u32[]{:S(2)}) collective-permute-start(bf16[4,8,2048]{2,1,0:T(8,128)(2,1)S(1)} %pad_maximum_fusion.1), channel_id=1, source_target_pairs={{0,16},{16,0},{1,17},{17,1},{2,18},{18,2},{3,19},{19,3},{4,20},{20... | collective-permute-start | bytes 393224 | tf_op jit(solution)/shard_map/ppermute | solution.py:27
  27.2 22.4 %collective-permute-start.10 = (bf16[64,2048]{1,0:T(8,128)(2,1)S(1)}, bf16[64,2048]{1,0:T(8,128)(2,1)S(1)}, u32[]{:S(2)}, u32[]{:S(2)}) collective-permute-start(bf16[64,2048]{1,0:T(8,128)(2,1)S(1)} %pad_maximum_fusion.refs_4_), channel_id=1, source_target_pairs={{0,3},{1,2},{2,1},{3,0},{4,7},{5,6},{6,5},{7,4},{8,11},{9,10},{10,... | collective-permute-start | bytes 786440 | tf_op jit(solution)/shard_map/ppermute | solution.py:23
  27.3 24.3 %collective-permute-start.9 = (bf16[64,2048]{1,0:T(8,128)(2,1)S(1)}, bf16[64,2048]{1,0:T(8,128)(2,1)S(1)}, u32[]{:S(2)}, u32[]{:S(2)}) collective-permute-start(bf16[64,2048]{1,0:T(8,128)(2,1)S(1)} %pad_maximum_fusion.refs_4_), channel_id=1, source_target_pairs={{0,2},{1,3},{2,0},{3,1},{4,6},{5,7},{6,4},{7,5},{8,10},{9,11},{10,... | collective-permute-start | bytes 786440 | tf_op jit(solution)/shard_map/ppermute | solution.py:23
  28.8 22.8 %collective-permute-start.8 = (bf16[64,2048]{1,0:T(8,128)(2,1)S(1)}, bf16[64,2048]{1,0:T(8,128)(2,1)S(1)}, u32[]{:S(2)}, u32[]{:S(2)}) collective-permute-start(bf16[64,2048]{1,0:T(8,128)(2,1)S(1)} %pad_maximum_fusion.refs_4_), channel_id=1, source_target_pairs={{0,1},{1,0},{2,3},{3,2},{4,5},{5,4},{6,7},{7,6},{8,9},{9,8},{10,11... | collective-permute-start | bytes 786440 | tf_op jit(solution)/shard_map/ppermute | solution.py:23
  46.9 12.1 %collective-permute-start.13 = (bf16[256,64]{1,0:T(8,128)(2,1)S(1)}, bf16[256,64]{1,0:T(8,128)(2,1)S(1)}, u32[]{:S(2)}, u32[]{:S(2)}) collective-permute-start(bf16[256,64]{1,0:T(8,128)(2,1)S(1)} %pad_maximum_fusion.2), channel_id=1, source_target_pairs={{0,4},{4,12},{12,8},{8,0},{1,5},{5,13},{13,9},{9,1},{2,6},{6,14},{... | collective-permute-start | bytes 98312 | tf_op jit(solution)/shard_map/ppermute | solution.py:23
  46.9 12.1 %collective-permute-start.12 = (bf16[256,64]{1,0:T(8,128)(2,1)S(1)}, bf16[256,64]{1,0:T(8,128)(2,1)S(1)}, u32[]{:S(2)}, u32[]{:S(2)}) collective-permute-start(bf16[256,64]{1,0:T(8,128)(2,1)S(1)} %pad_maximum_fusion.2), channel_id=1, source_target_pairs={{0,12},{12,0},{4,8},{8,4},{1,13},{13,1},{5,9},{9,5},{2,14},{14,2},... | collective-permute-start | bytes 98312 | tf_op jit(solution)/shard_map/ppermute | solution.py:23
  49.7 9.4 %collective-permute-start.11 = (bf16[256,64]{1,0:T(8,128)(2,1)S(1)}, bf16[256,64]{1,0:T(8,128)(2,1)S(1)}, u32[]{:S(2)}, u32[]{:S(2)}) collective-permute-start(bf16[256,64]{1,0:T(8,128)(2,1)S(1)} %pad_maximum_fusion.2), channel_id=1, source_target_pairs={{4,0},{12,4},{8,12},{0,8},{5,1},{13,5},{9,13},{1,9},{6,2},{14,6},{... | collective-permute-start | bytes 98312 | tf_op jit(solution)/shard_map/ppermute | solution.py:23
  59.8 2.0 %collective-permute-start.14 = (bf16[128,2048]{1,0:T(8,128)(2,1)S(1)}, bf16[128,2048]{1,0:T(8,128)(2,1)S(1)}, u32[]{:S(2)}, u32[]{:S(2)}) collective-permute-start(bf16[128,2048]{1,0:T(8,128)(2,1)S(1)} %fusion.4), channel_id=1, source_target_pairs={{0,1},{1,0},{2,3},{3,2},{4,5},{5,4},{6,7},{7,6},{8,9},{9,8},{10,11... | collective-permute-start | bytes 1572872 | tf_op jit(solution)/shard_map/ppermute | solution.py:27
  62.2 13.0 %collective-permute-start.17 = (bf16[32,2048]{1,0:T(8,128)(2,1)S(1)}, bf16[32,2048]{1,0:T(8,128)(2,1)S(1)}, u32[]{:S(2)}, u32[]{:S(2)}) collective-permute-start(bf16[32,2048]{1,0:T(8,128)(2,1)S(1)} %get-tuple-element.32), channel_id=1, source_target_pairs={{0,4},{4,12},{12,8},{8,0},{1,5},{5,13},{13,9},{9,1},{2,6},{6,14},{... | collective-permute-start | bytes 393224 | tf_op jit(solution)/shard_map/ppermute | solution.py:23
  62.3 12.8 %collective-permute-start.16 = (bf16[32,2048]{1,0:T(8,128)(2,1)S(1)}, bf16[32,2048]{1,0:T(8,128)(2,1)S(1)}, u32[]{:S(2)}, u32[]{:S(2)}) collective-permute-start(bf16[32,2048]{1,0:T(8,128)(2,1)S(1)} %get-tuple-element.33), channel_id=1, source_target_pairs={{0,12},{12,0},{4,8},{8,4},{1,13},{13,1},{5,9},{9,5},{2,14},{14,2},... | collective-permute-start | bytes 393224 | tf_op jit(solution)/shard_map/ppermute | solution.py:23
  63.7 11.4 %collective-permute-start.15 = (bf16[32,2048]{1,0:T(8,128)(2,1)S(1)}, bf16[32,2048]{1,0:T(8,128)(2,1)S(1)}, u32[]{:S(2)}, u32[]{:S(2)}) collective-permute-start(bf16[32,2048]{1,0:T(8,128)(2,1)S(1)} %get-tuple-element.34), channel_id=1, source_target_pairs={{4,0},{12,4},{8,12},{0,8},{5,1},{13,5},{9,13},{1,9},{6,2},{14,6},{... | collective-permute-start | bytes 393224 | tf_op jit(solution)/shard_map/ppermute | solution.py:23

commit v4 on v3

--- a/solution.py
+++ b/solution.py
@@ -1,5 +1,3 @@
-import functools
-
 import jax
 import jax.numpy as jnp
 from jax import lax
@@ -10,7 +8,9 @@
 LOW_RANK_SCALE = 2.0
 F32 = jnp.float32
 BF16 = jnp.bfloat16
-VMEM_LIMIT = 44 * 2**20
+FIRST_LIMIT = 44 * 2**20
+NEXT_LIMIT = 20 * 2**20
+LAST_LIMIT = 12 * 2**20
 
 FROM_NEXT = ((1, 0), (3, 1), (2, 3), (0, 2))
 FROM_LAST = ((0, 1), (1, 3), (3, 2), (2, 0))
@@ -54,9 +54,15 @@
     )(where, *blocks)
 
 
-def base_kernel(inner_ref, *refs, blocks, parts):
-    x_refs, part_refs, weight_ref = refs[:blocks], refs[blocks : blocks + parts], refs[blocks + parts]
-    out_ref, *panel_refs, x_ref, held_ref, sems = refs[blocks + parts + 1 :]
+VMEM = pl.BlockSpec(memory_space=pltpu.VMEM)
+SMEM = pl.BlockSpec(memory_space=pltpu.SMEM)
+
+
+def cost(rows, weight):
+    return pl.CostEstimate(flops=2 * rows * weight.size, bytes_accessed=weight.size * 2, transcendentals=0)
+
+
+def stream_kernel(x_ref, weight_ref, out_ref, held_ref, sems):
     count, depth, _ = held_ref.shape
 
     def piece(k):
@@ -64,32 +70,6 @@
 
     for k in range(count):
         piece(k).start()
-    rows = x_refs[0].shape[0]
-    for i, block in enumerate(x_refs):
-        at = pl.ds(min(i, 2) * rows, rows)
-        if i < 2:
-            x_ref[at] = block[...]
-        else:
-
-            @pl.when(inner_ref[0] == 3 - i)
-            def _(at=at, block=block):
-                x_ref[at] = block[...]
-
-    for k, part_ref in enumerate(part_refs):
-        share = part_ref.shape[0] // 8
-        for slot in range(4):
-            first = part_ref[slot * share : (slot + 1) * share]
-            second = part_ref[(4 + slot) * share : (5 + slot) * share]
-            at = pl.multiple_of((slot * parts + (inner_ref[1] ^ k)) * 2 * share, 16)
-
-            @pl.when(inner_ref[2] == 0)
-            def _(at=at, first=first, second=second):
-                panel_refs[0][pl.ds(at, 2 * share)] = jnp.concatenate([first, second])
-
-            @pl.when(inner_ref[2] == 1)
-            def _(at=at, first=first, second=second):
-                panel_refs[0][pl.ds(at, 2 * share)] = jnp.concatenate([second, first])
-
     for k in range(count):
         piece(k).wait()
         term = dot(x_ref[:, k * depth : (k + 1) * depth], held_ref[k])
@@ -99,32 +79,75 @@
             out_ref[...] += term
 
 
-def base_of(facts, blocks, parts, weight):
-    rows, depth = blocks[0].shape
-    count = min(len(blocks), 3)
+def stream(x, weight, limit):
+    rows, depth = x.shape
     width = weight.shape[1]
     pieces = 8
-    vmem = pl.BlockSpec(memory_space=pltpu.VMEM)
-    shapes = [jax.ShapeDtypeStruct((count * rows, width), F32)]
-    if parts:
-        shapes.append(jax.ShapeDtypeStruct((len(parts) * parts[0].shape[0], width), parts[0].dtype))
     return pl.pallas_call(
-        functools.partial(base_kernel, blocks=len(blocks), parts=len(parts)),
-        out_shape=shapes,
-        in_specs=[pl.BlockSpec(memory_space=pltpu.SMEM)]
-        + [vmem] * (len(blocks) + len(parts))
-        + [pl.BlockSpec(memory_space=pl.ANY)],
-        out_specs=[vmem] * len(shapes),
+        stream_kernel,
+        out_shape=jax.ShapeDtypeStruct((rows, width), F32),
+        in_specs=[VMEM, pl.BlockSpec(memory_space=pl.ANY)],
+        out_specs=VMEM,
         scratch_shapes=[
-            pltpu.VMEM((count * rows, depth), weight.dtype),
             pltpu.VMEM((pieces, depth // pieces, width), weight.dtype),
             pltpu.SemaphoreType.DMA((pieces,)),
         ],
-        compiler_params=pltpu.CompilerParams(vmem_limit_bytes=VMEM_LIMIT),
-        cost_estimate=pl.CostEstimate(
-            flops=2 * count * rows * depth * width, bytes_accessed=weight.size * 2, transcendentals=0
-        ),
-    )(facts, *blocks, *parts, weight)
+        compiler_params=pltpu.CompilerParams(vmem_limit_bytes=limit),
+        cost_estimate=cost(rows, weight),
+    )(x, weight)
+
+
+def last_kernel(facts_ref, x3_ref, x2a_ref, x2b_ref, *refs):
+    part_refs, (weight_ref, out_ref, panel_ref, x_ref) = refs[:-4], refs[-4:]
+    rows = x3_ref.shape[0]
+    x_ref[rows:] = x3_ref[...]
+
+    @pl.when(facts_ref[0] == 1)
+    def _():
+        x_ref[:rows] = x2a_ref[...]
+
+    @pl.when(facts_ref[0] == 0)
+    def _():
+        x_ref[:rows] = x2b_ref[...]
+
+    for k, part_ref in enumerate(part_refs):
+        share = part_ref.shape[0] // 8
+        for slot in range(4):
+            first = part_ref[slot * share : (slot + 1) * share]
+            second = part_ref[(4 + slot) * share : (5 + slot) * share]
+            at = pl.multiple_of((slot * len(part_refs) + (facts_ref[1] ^ k)) * 2 * share, 16)
+
+            @pl.when(facts_ref[2] == 0)
+            def _(at=at, first=first, second=second):
+                panel_ref[pl.ds(at, 2 * share)] = jnp.concatenate([first, second])
+
+            @pl.when(facts_ref[2] == 1)
+            def _(at=at, first=first, second=second):
+                panel_ref[pl.ds(at, 2 * share)] = jnp.concatenate([second, first])
+
+    tile = 256
+
+    @pl.loop(0, out_ref.shape[1] // tile)
+    def _(n):
+        at = pl.ds(pl.multiple_of(n * tile, tile), tile)
+        out_ref[:, at] = dot(x_ref[...], weight_ref[:, at])
+
+
+def last(facts, x3, x2a, x2b, parts, weight):
+    rows, depth = x3.shape
+    width = weight.shape[1]
+    return pl.pallas_call(
+        last_kernel,
+        out_shape=[
+            jax.ShapeDtypeStruct((2 * rows, width), F32),
+            jax.ShapeDtypeStruct((len(parts) * parts[0].shape[0], width), parts[0].dtype),
+        ],
+        in_specs=[SMEM] + [VMEM] * (4 + len(parts)),
+        out_specs=[VMEM, VMEM],
+        scratch_shapes=[pltpu.VMEM((2 * rows, depth), weight.dtype)],
+        compiler_params=pltpu.CompilerParams(vmem_limit_bytes=LAST_LIMIT),
+        cost_estimate=cost(2 * rows, weight),
+    )(facts, x3, x2a, x2b, *parts, weight)
 
 
 def dot(a, b):
@@ -149,7 +172,7 @@
 
     x1 = shift(own, FROM_NEXT)
     inner = (me == 1) | (me == 2)
-    [base0] = base_of(jnp.ones((3,), jnp.int32), [own], [], query_weight)
+    base0 = stream(own, query_weight, FIRST_LIMIT)
     own, base0 = lax.optimization_barrier((own, base0))
     x3 = shift(own, FROM_LAST)
     x2a = shift(own, INNER)
@@ -169,7 +192,8 @@
     )
     x1, part = lax.optimization_barrier((x1, part))
     x2b = shift(x1, RELAY)
-    x3, x2a, x2b = lax.optimization_barrier((x3, x2a, x2b))
+    base1 = stream(x1, query_weight, NEXT_LIMIT)
+    x3, x2a, x2b, base1 = lax.optimization_barrier((x3, x2a, x2b, base1))
     part = jnp.concatenate([part.reshape(4 * share, width), swap(part, "groups").reshape(4 * share, width)])
     parts = [part] + [shift(part, [(i, i ^ k) for i in range(peers)], inside) for k in range(1, peers)]
 
@@ -181,8 +205,8 @@
     ranks = jnp.concatenate(ranks)
     ranks = [ranks, shift(ranks, FROM_NEXT), shift(ranks, OPPOSITE), shift(ranks, FROM_LAST)]
     facts = jnp.stack([inner.astype(jnp.int32), peer.astype(jnp.int32), group.astype(jnp.int32)])
-    base, panels = base_of(facts, [x1, x3, x2a, x2b], parts, query_weight)
-    base = [base0, base[:rows], base[2 * rows :], base[rows : 2 * rows]]
+    base23, panels = last(facts, x3, x2a, x2b, parts, query_weight)
+    base = [base0, base1, base23[:rows], base23[rows:]]
 
     def rank_at(j, k):
         return ranks[j][k * rows:][:rows]

time: 76.8 us -> 75.5 us (0.983)
  waiting for transfers between devices: 32.6 us -> 24.9 us
  local copies, waits for them, and re-layouts: 2.64 us -> 8.32 us
  Pallas kernels: 15.4 us -> 17.1 us
  starting transfers between devices: 23.1 us -> 21.9 us
    unnamed x8 -> x12, local copies, waits for them, and re-layouts: 1.08 us -> 6.85 us
    ppermute x16, waiting for transfers between devices: 27.5 us -> 23 us  [shift(): return lax.ppermute(x, axis, pairs)]
    ppermute x2, waiting for transfers between devices: 5.05 us -> 1.9 us  [swap(): return lax.ppermute(x, axis, ((0, 1), (1, 0)))]
    pallas_call x2 -> x3, Pallas kernels: 14 us -> 15.8 us  [the longest x2 10.8 us: stream(): pl.pallas_call(stream_kernel, out_shape=jax.ShapeDtypeStruct((rows, width...]
    ppermute x16, starting transfers between devices: 21.5 us -> 20.3 us  [shift(): return lax.ppermute(x, axis, pairs)]
  transfers between devices with their start and end apart: 18 -> 18, of which waited for: 6 -> 5; matrix products, arithmetic and copies ran while one was open for 4% -> 4% of each run, Pallas kernels for 18% -> 21%
where the time goes in v4:
time: 75.5 us; the launch traced here: 75.2 us
  waiting for transfers between devices  24.9 us (33%)
  starting transfers between devices  21.9 us (29%)
  Pallas kernels  17.1 us (23%)
  local copies, waits for them, and re-layouts  8.32 us (11%)
  matrix products  1.86 us (2%)
    ppermute x16, waiting for transfers between devices, shift(): return lax.ppermute(x, axis, pairs)  23 us
    ppermute x16, starting transfers between devices, shift(): return lax.ppermute(x, axis, pairs)  20.3 us
    pallas_call x2, Pallas kernels, stream(): pl.pallas_call(stream_kernel, out_shape=jax.ShapeDtypeStruct((rows, width...  10.8 us
    unnamed x12, local copies, waits for them, and re-layouts  6.85 us
    pallas_call x1, Pallas kernels, last(): pl.pallas_call(last_kernel, out_shape=[jax.ShapeDtypeStruct((2 * rows, wi...  5 us
    ppermute x2, waiting for transfers between devices, swap(): return lax.ppermute(x, axis, ((0, 1), (1, 0)))  1.9 us
    dot_general x6, matrix products, dot(): return jnp.dot(a, b, preferred_element_type=F32)  1.86 us
    ppermute x2, starting transfers between devices, swap(): return lax.ppermute(x, axis, ((0, 1), (1, 0)))  1.66 us
  transfers between devices with their start and end apart: 18, of which 5 were waited for; matrix products, arithmetic and copies ran while one was open for 4% of the time, Pallas kernels for 21%

profile of v4, /device:TPU:0, one launch (start us, length us, event | category | flops | bytes accessed | tf_op | source)
XLA Modules:
  0.0 75.2 jit_solution(195007413115450721)
XLA Ops:
  0.0 0.0 copy-start
  0.0 4.0 %collective-permute-start.2 = (bf16[64,4096]{1,0:T(8,128)(2,1)}, bf16[64,4096]{1,0:T(8,128)(2,1)S(1)}, u32[]{:S(2)}, u32[]{:S(2)}) collective-permute-start(bf16[64,4096]{1,0:T(8,128)(2,1)} %bitcast.39), channel_id=1, source_target_pairs={{4,0},{12,4},{8,12},{0,8},{5,1},{13,5},{9,13},{1,9},{6,2},{14,6},{... | collective-permute-start | bytes 1572872 | tf_op jit(solution)/shard_map/ppermute | solution.py:23
  4.0 1.1 %copy-done.3 = bf16[1,64,4096]{2,1,0:T(8,128)(2,1)S(1)} copy-done((bf16[1,64,4096]{2,1,0:T(8,128)(2,1)S(1)}, bf16[1,64,4096]{2,1,0:T(8,128)(2,1)}, u32[]{:S(2)}) %copy-start.3) | copy-done | bytes 524312
  5.1 6.5 %shard_map.55 = f32[64,2048]{1,0:T(8,128)S(1)} custom-call(bf16[64,4096]{1,0:T(8,128)(2,1)S(1)} %bitcast.40, bf16[4096,2048]{1,0:T(8,128)(2,1)} %refs_4_.1), custom_call_target="tpu_custom_call" | custom-call | flops 1073741824 | bytes 16777216 | tf_op jit(solution)/shard_map/pallas_call | solution.py:86
  11.6 1.1 %dynamic-slice_bitcast_fusion = (bf16[1,8,2048]{2,1,0:T(8,128)(2,1)S(1)}, bf16[8,2048]{1,0:T(8,128)(2,1)S(1)}, bf16[8,2048]{1,0:T(8,128)(2,1)S(1)}, bf16[8,2048]{1,0:T(8,128)(2,1)S(1)}) fusion(bf16[64,8192]{1,0:T(8,128)(2,1)} %bitcast.49, s32[]{:T(128)S(6)} %select_n.98, s32[]{:T(128)S(6)} %select_n.100, s32[]{:T(128)S(6)} %select_n.106, s32[]{:T(128)S(6)} %select_n.104, ...), kind=kLoop, calls=%fused_computation.42 | loop fusion | bytes 262164 | tf_op jit(solution)/shard_map/stack | solution.py:190
  12.7 0.1 collective-permute-start.5
  12.8 3.0 %collective-permute-start.4 = (bf16[8,2048]{1,0:T(8,128)(2,1)S(1)}, bf16[8,2048]{1,0:T(8,128)(2,1)S(1)}, u32[]{:S(2)}, u32[]{:S(2)}) collective-permute-start(bf16[8,2048]{1,0:T(8,128)(2,1)S(1)} %get-tuple-element.31), channel_id=1, source_target_pairs={{0,12},{12,0},{4,8},{8,4},{1,13},{13,1},{5,9},{9,5},{2,14},{14,2},... | collective-permute-start | bytes 98312 | tf_op jit(solution)/shard_map/ppermute | solution.py:23
  15.8 0.4 collective-permute-start.3
  16.1 0.0 copy-done.4
  16.1 0.7 collective-permute-start.1
  16.9 0.0 copy-done.5
  16.9 0.1 compare_bitcast_fusion.3
  17.0 0.0 copy-done
  17.0 0.3 fusion.5
  17.3 0.1 pad_add_fusion.1.facts_ref
  17.4 1.9 %collective-permute-done.5 = bf16[8,2048]{1,0:T(8,128)(2,1)S(1)} collective-permute-done((bf16[8,2048]{1,0:T(8,128)(2,1)S(1)}, bf16[8,2048]{1,0:T(8,128)(2,1)S(1)}, u32[]{:S(2)}, u32[]{:S(2)}) %collective-permute-start.5) | collective-permute-done | bytes 32800 | tf_op jit(solution)/shard_map/ppermute | solution.py:23
  19.3 1.0 %collective-permute-start = (bf16[64,4096]{1,0:T(8,128)(2,1)S(1)}, bf16[64,4096]{1,0:T(8,128)(2,1)S(1)}, u32[]{:S(2)}, u32[]{:S(2)}) collective-permute-start(bf16[64,4096]{1,0:T(8,128)(2,1)S(1)} %bitcast.43), channel_id=1, source_target_pairs={{0,4},{4,12},{12,8},{8,0},{1,5},{5,13},{13,9},{9,1},{2,6},{6,14},{... | collective-permute-start | bytes 1572872 | tf_op jit(solution)/shard_map/ppermute | solution.py:23
  20.3 0.0 collective-permute-done.4
  20.3 0.0 collective-permute-done.3
  20.3 0.0 collective-permute-done.2.x_ref
  20.4 1.6 %collective-permute-start.7 = (bf16[4,8,2048]{2,1,0:T(8,128)(2,1)S(1)}, bf16[4,8,2048]{2,1,0:T(8,128)(2,1)S(1)}, u32[]{:S(2)}, u32[]{:S(2)}) collective-permute-start(bf16[4,8,2048]{2,1,0:T(8,128)(2,1)S(1)} %pad_maximum_fusion.1), channel_id=1, source_target_pairs={{0,16},{16,0},{1,17},{17,1},{2,18},{18,2},{3,19},{19,3},{4,20},{20... | collective-permute-start | bytes 393224 | tf_op jit(solution)/shard_map/ppermute | solution.py:27
  21.9 1.3 %collective-permute-start.6 = (bf16[64,4096]{1,0:T(8,128)(2,1)S(1)}, bf16[64,4096]{1,0:T(8,128)(2,1)S(1)}, u32[]{:S(2)}, u32[]{:S(2)}) collective-permute-start(bf16[64,4096]{1,0:T(8,128)(2,1)S(1)} %collective-permute-done.2.x_ref), channel_id=1, source_target_pairs={{8,12},{4,0},{9,13},{5,1},{10,14},{6,2},{11,15},{7,3},{24,28},{20,... | collective-permute-start | bytes 1572872 | tf_op jit(solution)/shard_map/ppermute | solution.py:23
  23.2 0.3 fusion.6
  23.5 0.0 copy-start.1
  23.5 5.8 %copy-done.1 = bf16[4096,2048]{1,0:T(8,128)(2,1)S(1)} copy-done((bf16[4096,2048]{1,0:T(8,128)(2,1)S(1)}, bf16[4096,2048]{1,0:T(8,128)(2,1)}, u32[]{:S(2)}) %copy-start.1) | copy-done | bytes 16777240
  29.3 4.3 %shard_map.56 = f32[64,2048]{1,0:T(8,128)S(1)} custom-call(bf16[64,4096]{1,0:T(8,128)(2,1)S(1)} %collective-permute-done.2.x_ref, bf16[4096,2048]{1,0:T(8,128)(2,1)S(1)} %copy-done.1), custom_call_target="tpu_custom_call" | custom-call | flops 1073741824 | bytes 16777216 | tf_op jit(solution)/shard_map/pallas_call | solution.py:86
  33.6 0.0 collective-permute-done.7
  33.7 0.1 collective-permute-start.10
  33.7 1.5 %collective-permute-start.9 = (bf16[64,2048]{1,0:T(8,128)(2,1)S(1)}, bf16[64,2048]{1,0:T(8,128)(2,1)S(1)}, u32[]{:S(2)}, u32[]{:S(2)}) collective-permute-start(bf16[64,2048]{1,0:T(8,128)(2,1)S(1)} %pad_maximum_fusion.refs_0_), channel_id=1, source_target_pairs={{0,2},{1,3},{2,0},{3,1},{4,6},{5,7},{6,4},{7,5},{8,10},{9,11},{10,... | collective-permute-start | bytes 786440 | tf_op jit(solution)/shard_map/ppermute | solution.py:23
  35.3 0.0 collective-permute-done.1.x2a_ref
  35.3 0.3 collective-permute-start.8
  35.6 7.5 %collective-permute-done.x3_ref = bf16[64,4096]{1,0:T(8,128)(2,1)S(1)} collective-permute-done((bf16[64,4096]{1,0:T(8,128)(2,1)S(1)}, bf16[64,4096]{1,0:T(8,128)(2,1)S(1)}, u32[]{:S(2)}, u32[]{:S(2)}) %collective-permute-start) | collective-permute-done | bytes 524320 | tf_op jit(solution)/shard_map/ppermute | solution.py:23
  43.1 4.3 %collective-permute-done.6.x2b_ref = bf16[64,4096]{1,0:T(8,128)(2,1)S(1)} collective-permute-done((bf16[64,4096]{1,0:T(8,128)(2,1)S(1)}, bf16[64,4096]{1,0:T(8,128)(2,1)S(1)}, u32[]{:S(2)}, u32[]{:S(2)}) %collective-permute-start.6) | collective-permute-done | bytes 524320 | tf_op jit(solution)/shard_map/ppermute | solution.py:23
  47.4 0.3 fusion.7
  47.7 0.3 fusion.8
  48.0 0.1 collective-permute-start.13
  48.1 2.4 %collective-permute-start.12 = (bf16[256,64]{1,0:T(8,128)(2,1)S(1)}, bf16[256,64]{1,0:T(8,128)(2,1)S(1)}, u32[]{:S(2)}, u32[]{:S(2)}) collective-permute-start(bf16[256,64]{1,0:T(8,128)(2,1)S(1)} %pad_maximum_fusion.2), channel_id=1, source_target_pairs={{0,12},{12,0},{4,8},{8,4},{1,13},{13,1},{5,9},{9,5},{2,14},{14,2},... | collective-permute-start | bytes 98312 | tf_op jit(solution)/shard_map/ppermute | solution.py:23
  50.5 0.0 collective-permute-done.10.refs_3_
  50.5 1.9 %collective-permute-start.11 = (bf16[256,64]{1,0:T(8,128)(2,1)S(1)}, bf16[256,64]{1,0:T(8,128)(2,1)S(1)}, u32[]{:S(2)}, u32[]{:S(2)}) collective-permute-start(bf16[256,64]{1,0:T(8,128)(2,1)S(1)} %pad_maximum_fusion.2), channel_id=1, source_target_pairs={{4,0},{12,4},{8,12},{0,8},{5,1},{13,5},{9,13},{1,9},{6,2},{14,6},{... | collective-permute-start | bytes 98312 | tf_op jit(solution)/shard_map/ppermute | solution.py:23
  52.4 0.0 collective-permute-done.9.refs_2_
  52.4 0.0 collective-permute-done.8.refs_1_
  52.4 0.0 copy-done.2
  52.5 5.0 %shard_map.57 = (f32[128,2048]{1,0:T(8,128)S(1)}, bf16[256,2048]{1,0:T(8,128)(2,1)S(1)}) custom-call(s32[3]{0:T(128)S(1)} %pad_add_fusion.1.facts_ref, bf16[64,4096]{1,0:T(8,128)(2,1)S(1)} %collective-permute-done.x3_ref, bf16[64,4096]{1,0:T(8,128)(2,1)S(1)} %collective-permute-done.1.x2a_ref, bf16[64,4096]{1,0:T(8,128)(2,1)S(1)} %collective-permute-done.6.x2b_ref, ...), custom_call_target="tpu_custom_call" | custom-call | flops 2147483648 | bytes 16777216 | tf_op jit(solution)/shard_map/pallas_call | solution.py:139
  57.5 0.1 fusion.31
  57.5 0.1 constant_dynamic-slice_fusion.4
  57.7 0.0 collective-permute-done.13
  57.7 0.0 collective-permute-done.12
  57.7 0.0 collective-permute-done.11
  57.8 0.1 pad_maximum_fusion.5
  57.9 0.1 pad_maximum_fusion.6
  58.0 0.1 pad_maximum_fusion.4
  58.1 0.1 pad_maximum_fusion.3
  58.2 0.3 fusion.4
  58.5 0.1 collective-permute-start.14
  58.6 1.9 %collective-permute-done.14 = bf16[128,2048]{1,0:T(8,128)(2,1)S(1)} collective-permute-done((bf16[128,2048]{1,0:T(8,128)(2,1)S(1)}, bf16[128,2048]{1,0:T(8,128)(2,1)S(1)}, u32[]{:S(2)}, u32[]{:S(2)}) %collective-permute-start.14) | collective-permute-done | bytes 524320 | tf_op jit(solution)/shard_map/ppermute | solution.py:27
  60.5 0.3 fusion.3
  60.9 0.1 collective-permute-start.17
  61.0 1.5 %collective-permute-start.16 = (bf16[32,2048]{1,0:T(8,128)(2,1)S(1)}, bf16[32,2048]{1,0:T(8,128)(2,1)S(1)}, u32[]{:S(2)}, u32[]{:S(2)}) collective-permute-start(bf16[32,2048]{1,0:T(8,128)(2,1)S(1)} %get-tuple-element.34), channel_id=1, source_target_pairs={{0,12},{12,0},{4,8},{8,4},{1,13},{13,1},{5,9},{9,5},{2,14},{14,2},... | collective-permute-start | bytes 393224 | tf_op jit(solution)/shard_map/ppermute | solution.py:23
  62.5 1.9 %collective-permute-start.15 = (bf16[32,2048]{1,0:T(8,128)(2,1)S(1)}, bf16[32,2048]{1,0:T(8,128)(2,1)S(1)}, u32[]{:S(2)}, u32[]{:S(2)}) collective-permute-start(bf16[32,2048]{1,0:T(8,128)(2,1)S(1)} %get-tuple-element.35), channel_id=1, source_target_pairs={{4,0},{12,4},{8,12},{0,8},{5,1},{13,5},{9,13},{1,9},{6,2},{14,6},{... | collective-permute-start | bytes 393224 | tf_op jit(solution)/shard_map/ppermute | solution.py:23
  64.4 0.1 pad_add_fusion.where_ref
  64.5 9.3 %collective-permute-done.17.refs_3_ = bf16[32,2048]{1,0:T(8,128)(2,1)S(1)} collective-permute-done((bf16[32,2048]{1,0:T(8,128)(2,1)S(1)}, bf16[32,2048]{1,0:T(8,128)(2,1)S(1)}, u32[]{:S(2)}, u32[]{:S(2)}) %collective-permute-start.17) | collective-permute-done | bytes 131104 | tf_op jit(solution)/shard_map/ppermute | solution.py:23
  73.8 0.0 collective-permute-done.16.refs_2_
  73.8 0.0 collective-permute-done.15.refs_1_
  73.8 1.4 %shard_map.58 = bf16[32,8192]{1,0:T(8,128)(2,1)} custom-call(s32[4]{0:T(128)S(1)} %pad_add_fusion.where_ref, bf16[32,2048]{1,0:T(8,128)(2,1)S(1)} %get-tuple-element.36.refs_0_, bf16[32,2048]{1,0:T(8,128)(2,1)S(1)} %collective-permute-done.15.refs_1_, bf16[32,2048]{1,0:T(8,128)(2,1)S(1)} %collective-permute-done.16.refs_2_, ...), custom_call_target="tpu_custom_call" | custom-call | tf_op jit(solution)/shard_map/pallas_call | solution.py:48
  (15 shorter events, 0.2 us)
Async XLA Ops:
  0.0 17.0 %copy-start = (bf16[1,4096,64]{1,2,0:T(8,128)(2,1)S(1)}, bf16[1,4096,64]{1,2,0:T(8,128)(2,1)}, u32[]{:S(2)}) copy-start(bf16[1,4096,64]{1,2,0:T(8,128)(2,1)} %param.8) | copy-start | bytes 1572868
  0.0 16.9 %copy-start.5 = (s32[1,256,1]{1,2,0:T(1,128)S(1)}, s32[1,256,1]{1,2,0:T(1,128)}, u32[]{:S(2)}) copy-start(s32[1,256,1]{1,2,0:T(1,128)} %param.6) | copy-start | bytes 3076
  0.0 20.3 %collective-permute-start.2 = (bf16[64,4096]{1,0:T(8,128)(2,1)}, bf16[64,4096]{1,0:T(8,128)(2,1)S(1)}, u32[]{:S(2)}, u32[]{:S(2)}) collective-permute-start(bf16[64,4096]{1,0:T(8,128)(2,1)} %bitcast.39), channel_id=1, source_target_pairs={{4,0},{12,4},{8,12},{0,8},{5,1},{13,5},{9,13},{1,9},{6,2},{14,6},{... | collective-permute-start | bytes 1572872 | tf_op jit(solution)/shard_map/ppermute | solution.py:23
  4.0 1.1 %copy-start.3 = (bf16[1,64,4096]{2,1,0:T(8,128)(2,1)S(1)}, bf16[1,64,4096]{2,1,0:T(8,128)(2,1)}, u32[]{:S(2)}) copy-start(bf16[1,64,4096]{2,1,0:T(8,128)(2,1)} %param.5) | copy-start | bytes 1572868
  5.1 11.0 %copy-start.4 = (bf16[1,64,4096]{2,1,0:T(8,128)(2,1)S(1)}, bf16[1,64,4096]{2,1,0:T(8,128)(2,1)}, u32[]{:S(2)}) copy-start(bf16[1,64,4096]{2,1,0:T(8,128)(2,1)} %param.5) | copy-start | bytes 1572868
  12.7 6.6 %collective-permute-start.5 = (bf16[8,2048]{1,0:T(8,128)(2,1)S(1)}, bf16[8,2048]{1,0:T(8,128)(2,1)S(1)}, u32[]{:S(2)}, u32[]{:S(2)}) collective-permute-start(bf16[8,2048]{1,0:T(8,128)(2,1)S(1)} %get-tuple-element.30), channel_id=1, source_target_pairs={{0,4},{4,12},{12,8},{8,0},{1,5},{5,13},{13,9},{9,1},{2,6},{6,14},{... | collective-permute-start | bytes 98312 | tf_op jit(solution)/shard_map/ppermute | solution.py:23
  12.8 7.5 %collective-permute-start.4 = (bf16[8,2048]{1,0:T(8,128)(2,1)S(1)}, bf16[8,2048]{1,0:T(8,128)(2,1)S(1)}, u32[]{:S(2)}, u32[]{:S(2)}) collective-permute-start(bf16[8,2048]{1,0:T(8,128)(2,1)S(1)} %get-tuple-element.31), channel_id=1, source_target_pairs={{0,12},{12,0},{4,8},{8,4},{1,13},{13,1},{5,9},{9,5},{2,14},{14,2},... | collective-permute-start | bytes 98312 | tf_op jit(solution)/shard_map/ppermute | solution.py:23
  15.8 4.5 %collective-permute-start.3 = (bf16[8,2048]{1,0:T(8,128)(2,1)S(1)}, bf16[8,2048]{1,0:T(8,128)(2,1)S(1)}, u32[]{:S(2)}, u32[]{:S(2)}) collective-permute-start(bf16[8,2048]{1,0:T(8,128)(2,1)S(1)} %get-tuple-element.32), channel_id=1, source_target_pairs={{4,0},{12,4},{8,12},{0,8},{5,1},{13,5},{9,13},{1,9},{6,2},{14,6},{... | collective-permute-start | bytes 98312 | tf_op jit(solution)/shard_map/ppermute | solution.py:23
  16.1 19.1 %collective-permute-start.1 = (bf16[64,4096]{1,0:T(8,128)(2,1)S(1)}, bf16[64,4096]{1,0:T(8,128)(2,1)S(1)}, u32[]{:S(2)}, u32[]{:S(2)}) collective-permute-start(bf16[64,4096]{1,0:T(8,128)(2,1)S(1)} %bitcast.41), channel_id=1, source_target_pairs={{4,8},{8,4},{5,9},{9,5},{6,10},{10,6},{7,11},{11,7},{20,24},{24,20... | collective-permute-start | bytes 1572872 | tf_op jit(solution)/shard_map/ppermute | solution.py:23
  19.3 23.7 %collective-permute-start = (bf16[64,4096]{1,0:T(8,128)(2,1)S(1)}, bf16[64,4096]{1,0:T(8,128)(2,1)S(1)}, u32[]{:S(2)}, u32[]{:S(2)}) collective-permute-start(bf16[64,4096]{1,0:T(8,128)(2,1)S(1)} %bitcast.43), channel_id=1, source_target_pairs={{0,4},{4,12},{12,8},{8,0},{1,5},{5,13},{13,9},{9,1},{2,6},{6,14},{... | collective-permute-start | bytes 1572872 | tf_op jit(solution)/shard_map/ppermute | solution.py:23
  20.4 13.3 %collective-permute-start.7 = (bf16[4,8,2048]{2,1,0:T(8,128)(2,1)S(1)}, bf16[4,8,2048]{2,1,0:T(8,128)(2,1)S(1)}, u32[]{:S(2)}, u32[]{:S(2)}) collective-permute-start(bf16[4,8,2048]{2,1,0:T(8,128)(2,1)S(1)} %pad_maximum_fusion.1), channel_id=1, source_target_pairs={{0,16},{16,0},{1,17},{17,1},{2,18},{18,2},{3,19},{19,3},{4,20},{20... | collective-permute-start | bytes 393224 | tf_op jit(solution)/shard_map/ppermute | solution.py:27
  21.9 25.4 %collective-permute-start.6 = (bf16[64,4096]{1,0:T(8,128)(2,1)S(1)}, bf16[64,4096]{1,0:T(8,128)(2,1)S(1)}, u32[]{:S(2)}, u32[]{:S(2)}) collective-permute-start(bf16[64,4096]{1,0:T(8,128)(2,1)S(1)} %collective-permute-done.2.x_ref), channel_id=1, source_target_pairs={{8,12},{4,0},{9,13},{5,1},{10,14},{6,2},{11,15},{7,3},{24,28},{20,... | collective-permute-start | bytes 1572872 | tf_op jit(solution)/shard_map/ppermute | solution.py:23
  23.5 5.8 %copy-start.1 = (bf16[4096,2048]{1,0:T(8,128)(2,1)S(1)}, bf16[4096,2048]{1,0:T(8,128)(2,1)}, u32[]{:S(2)}) copy-start(bf16[4096,2048]{1,0:T(8,128)(2,1)} %refs_4_.1) | copy-start | bytes 50331652
  29.3 23.1 %copy-start.2 = (bf16[4096,2048]{1,0:T(8,128)(2,1)S(1)}, bf16[4096,2048]{1,0:T(8,128)(2,1)}, u32[]{:S(2)}) copy-start(bf16[4096,2048]{1,0:T(8,128)(2,1)} %refs_4_.1) | copy-start | bytes 50331652
  33.7 16.8 %collective-permute-start.10 = (bf16[64,2048]{1,0:T(8,128)(2,1)S(1)}, bf16[64,2048]{1,0:T(8,128)(2,1)S(1)}, u32[]{:S(2)}, u32[]{:S(2)}) collective-permute-start(bf16[64,2048]{1,0:T(8,128)(2,1)S(1)} %pad_maximum_fusion.refs_0_), channel_id=1, source_target_pairs={{0,3},{1,2},{2,1},{3,0},{4,7},{5,6},{6,5},{7,4},{8,11},{9,10},{10,... | collective-permute-start | bytes 786440 | tf_op jit(solution)/shard_map/ppermute | solution.py:23
  33.7 18.7 %collective-permute-start.9 = (bf16[64,2048]{1,0:T(8,128)(2,1)S(1)}, bf16[64,2048]{1,0:T(8,128)(2,1)S(1)}, u32[]{:S(2)}, u32[]{:S(2)}) collective-permute-start(bf16[64,2048]{1,0:T(8,128)(2,1)S(1)} %pad_maximum_fusion.refs_0_), channel_id=1, source_target_pairs={{0,2},{1,3},{2,0},{3,1},{4,6},{5,7},{6,4},{7,5},{8,10},{9,11},{10,... | collective-permute-start | bytes 786440 | tf_op jit(solution)/shard_map/ppermute | solution.py:23
  35.3 17.2 %collective-permute-start.8 = (bf16[64,2048]{1,0:T(8,128)(2,1)S(1)}, bf16[64,2048]{1,0:T(8,128)(2,1)S(1)}, u32[]{:S(2)}, u32[]{:S(2)}) collective-permute-start(bf16[64,2048]{1,0:T(8,128)(2,1)S(1)} %pad_maximum_fusion.refs_0_), channel_id=1, source_target_pairs={{0,1},{1,0},{2,3},{3,2},{4,5},{5,4},{6,7},{7,6},{8,9},{9,8},{10,11... | collective-permute-start | bytes 786440 | tf_op jit(solution)/shard_map/ppermute | solution.py:23
  48.0 9.7 %collective-permute-start.13 = (bf16[256,64]{1,0:T(8,128)(2,1)S(1)}, bf16[256,64]{1,0:T(8,128)(2,1)S(1)}, u32[]{:S(2)}, u32[]{:S(2)}) collective-permute-start(bf16[256,64]{1,0:T(8,128)(2,1)S(1)} %pad_maximum_fusion.2), channel_id=1, source_target_pairs={{0,4},{4,12},{12,8},{8,0},{1,5},{5,13},{13,9},{9,1},{2,6},{6,14},{... | collective-permute-start | bytes 98312 | tf_op jit(solution)/shard_map/ppermute | solution.py:23
  48.1 9.6 %collective-permute-start.12 = (bf16[256,64]{1,0:T(8,128)(2,1)S(1)}, bf16[256,64]{1,0:T(8,128)(2,1)S(1)}, u32[]{:S(2)}, u32[]{:S(2)}) collective-permute-start(bf16[256,64]{1,0:T(8,128)(2,1)S(1)} %pad_maximum_fusion.2), channel_id=1, source_target_pairs={{0,12},{12,0},{4,8},{8,4},{1,13},{13,1},{5,9},{9,5},{2,14},{14,2},... | collective-permute-start | bytes 98312 | tf_op jit(solution)/shard_map/ppermute | solution.py:23
  50.5 7.2 %collective-permute-start.11 = (bf16[256,64]{1,0:T(8,128)(2,1)S(1)}, bf16[256,64]{1,0:T(8,128)(2,1)S(1)}, u32[]{:S(2)}, u32[]{:S(2)}) collective-permute-start(bf16[256,64]{1,0:T(8,128)(2,1)S(1)} %pad_maximum_fusion.2), channel_id=1, source_target_pairs={{4,0},{12,4},{8,12},{0,8},{5,1},{13,5},{9,13},{1,9},{6,2},{14,6},{... | collective-permute-start | bytes 98312 | tf_op jit(solution)/shard_map/ppermute | solution.py:23
  58.5 2.0 %collective-permute-start.14 = (bf16[128,2048]{1,0:T(8,128)(2,1)S(1)}, bf16[128,2048]{1,0:T(8,128)(2,1)S(1)}, u32[]{:S(2)}, u32[]{:S(2)}) collective-permute-start(bf16[128,2048]{1,0:T(8,128)(2,1)S(1)} %fusion.4), channel_id=1, source_target_pairs={{0,1},{1,0},{2,3},{3,2},{4,5},{5,4},{6,7},{7,6},{8,9},{9,8},{10,11... | collective-permute-start | bytes 1572872 | tf_op jit(solution)/shard_map/ppermute | solution.py:27
  60.9 13.0 %collective-permute-start.17 = (bf16[32,2048]{1,0:T(8,128)(2,1)S(1)}, bf16[32,2048]{1,0:T(8,128)(2,1)S(1)}, u32[]{:S(2)}, u32[]{:S(2)}) collective-permute-start(bf16[32,2048]{1,0:T(8,128)(2,1)S(1)} %get-tuple-element.33), channel_id=1, source_target_pairs={{0,4},{4,12},{12,8},{8,0},{1,5},{5,13},{13,9},{9,1},{2,6},{6,14},{... | collective-permute-start | bytes 393224 | tf_op jit(solution)/shard_map/ppermute | solution.py:23
  61.0 12.8 %collective-permute-start.16 = (bf16[32,2048]{1,0:T(8,128)(2,1)S(1)}, bf16[32,2048]{1,0:T(8,128)(2,1)S(1)}, u32[]{:S(2)}, u32[]{:S(2)}) collective-permute-start(bf16[32,2048]{1,0:T(8,128)(2,1)S(1)} %get-tuple-element.34), channel_id=1, source_target_pairs={{0,12},{12,0},{4,8},{8,4},{1,13},{13,1},{5,9},{9,5},{2,14},{14,2},... | collective-permute-start | bytes 393224 | tf_op jit(solution)/shard_map/ppermute | solution.py:23
  62.5 11.3 %collective-permute-start.15 = (bf16[32,2048]{1,0:T(8,128)(2,1)S(1)}, bf16[32,2048]{1,0:T(8,128)(2,1)S(1)}, u32[]{:S(2)}, u32[]{:S(2)}) collective-permute-start(bf16[32,2048]{1,0:T(8,128)(2,1)S(1)} %get-tuple-element.35), channel_id=1, source_target_pairs={{4,0},{12,4},{8,12},{0,8},{5,1},{13,5},{9,13},{1,9},{6,2},{14,6},{... | collective-permute-start | bytes 393224 | tf_op jit(solution)/shard_map/ppermute | solution.py:23

commit v5 on v4

--- a/solution.py
+++ b/solution.py
@@ -175,7 +175,6 @@
     base0 = stream(own, query_weight, FIRST_LIMIT)
     own, base0 = lax.optimization_barrier((own, base0))
     x3 = shift(own, FROM_LAST)
-    x2a = shift(own, INNER)
 
     inside = ("replica", "tp")
     peers = lax.axis_size(inside)
@@ -190,7 +189,8 @@
     part = jnp.stack(
         [columns(0), shift(columns(3), FROM_NEXT), shift(columns(2), OPPOSITE), shift(columns(1), FROM_LAST)]
     )
-    x1, part = lax.optimization_barrier((x1, part))
+    x1, part, own = lax.optimization_barrier((x1, part, own))
+    x2a = shift(own, INNER)
     x2b = shift(x1, RELAY)
     base1 = stream(x1, query_weight, NEXT_LIMIT)
     x3, x2a, x2b, base1 = lax.optimization_barrier((x3, x2a, x2b, base1))

time: 75.5 us -> 72.7 us (0.963)
  waiting for transfers between devices: 24.9 us -> 19.2 us
  starting transfers between devices: 21.9 us -> 24.8 us
    ppermute x16, waiting for transfers between devices: 23 us -> 17.3 us  [shift(): return lax.ppermute(x, axis, pairs)]
    ppermute x16, starting transfers between devices: 20.3 us -> 23.1 us  [shift(): return lax.ppermute(x, axis, pairs)]
  transfers between devices with their start and end apart: 18 -> 18, of which waited for: 5 -> 8; matrix products, arithmetic and copies ran while one was open for 4% -> 4% of each run, Pallas kernels for 21% -> 22%
where the time goes in v5:
time: 72.7 us; the launch traced here: 72.2 us
  starting transfers between devices  24.8 us (34%)
  waiting for transfers between devices  19.2 us (26%)
  Pallas kernels  17.1 us (24%)
  local copies, waits for them, and re-layouts  8.32 us (11%)
  matrix products  1.84 us (3%)
    ppermute x16, starting transfers between devices, shift(): return lax.ppermute(x, axis, pairs)  23.1 us
    ppermute x16, waiting for transfers between devices, shift(): return lax.ppermute(x, axis, pairs)  17.3 us
    pallas_call x2, Pallas kernels, stream(): pl.pallas_call(stream_kernel, out_shape=jax.ShapeDtypeStruct((rows, width...  10.8 us
    unnamed x12, local copies, waits for them, and re-layouts  6.85 us
    pallas_call x1, Pallas kernels, last(): pl.pallas_call(last_kernel, out_shape=[jax.ShapeDtypeStruct((2 * rows, wi...  4.99 us
    ppermute x2, waiting for transfers between devices, swap(): return lax.ppermute(x, axis, ((0, 1), (1, 0)))  1.87 us
    dot_general x6, matrix products, dot(): return jnp.dot(a, b, preferred_element_type=F32)  1.84 us
    ppermute x2, starting transfers between devices, swap(): return lax.ppermute(x, axis, ((0, 1), (1, 0)))  1.7 us
  transfers between devices with their start and end apart: 18, of which 8 were waited for; matrix products, arithmetic and copies ran while one was open for 4% of the time, Pallas kernels for 22%

profile of v5, /device:TPU:0, one launch (start us, length us, event | category | flops | bytes accessed | tf_op | source)
XLA Modules:
  0.0 72.2 jit_solution(11317779753523535161)
XLA Ops:
  0.0 0.0 copy-start
  0.0 4.0 %collective-permute-start.1 = (bf16[64,4096]{1,0:T(8,128)(2,1)}, bf16[64,4096]{1,0:T(8,128)(2,1)S(1)}, u32[]{:S(2)}, u32[]{:S(2)}) collective-permute-start(bf16[64,4096]{1,0:T(8,128)(2,1)} %bitcast.39), channel_id=1, source_target_pairs={{4,0},{12,4},{8,12},{0,8},{5,1},{13,5},{9,13},{1,9},{6,2},{14,6},{... | collective-permute-start | bytes 1572872 | tf_op jit(solution)/shard_map/ppermute | solution.py:23
  4.0 1.1 %copy-done.3 = bf16[1,64,4096]{2,1,0:T(8,128)(2,1)S(1)} copy-done((bf16[1,64,4096]{2,1,0:T(8,128)(2,1)S(1)}, bf16[1,64,4096]{2,1,0:T(8,128)(2,1)}, u32[]{:S(2)}) %copy-start.3) | copy-done | bytes 524312
  5.1 6.5 %shard_map.55 = f32[64,2048]{1,0:T(8,128)S(1)} custom-call(bf16[64,4096]{1,0:T(8,128)(2,1)S(1)} %bitcast.40, bf16[4096,2048]{1,0:T(8,128)(2,1)} %refs_4_.1), custom_call_target="tpu_custom_call" | custom-call | flops 1073741824 | bytes 16777216 | tf_op jit(solution)/shard_map/pallas_call | solution.py:86
  11.6 1.1 %dynamic-slice_bitcast_fusion = (bf16[1,8,2048]{2,1,0:T(8,128)(2,1)S(1)}, bf16[8,2048]{1,0:T(8,128)(2,1)S(1)}, bf16[8,2048]{1,0:T(8,128)(2,1)S(1)}, bf16[8,2048]{1,0:T(8,128)(2,1)S(1)}) fusion(bf16[64,8192]{1,0:T(8,128)(2,1)} %bitcast.49, s32[]{:T(128)S(6)} %select_n.98, s32[]{:T(128)S(6)} %select_n.100, s32[]{:T(128)S(6)} %select_n.106, s32[]{:T(128)S(6)} %select_n.104, ...), kind=kLoop, calls=%fused_computation.42 | loop fusion | bytes 262164 | tf_op jit(solution)/shard_map/stack | solution.py:189
  12.7 0.1 collective-permute-start.4
  12.8 3.0 %collective-permute-start.3 = (bf16[8,2048]{1,0:T(8,128)(2,1)S(1)}, bf16[8,2048]{1,0:T(8,128)(2,1)S(1)}, u32[]{:S(2)}, u32[]{:S(2)}) collective-permute-start(bf16[8,2048]{1,0:T(8,128)(2,1)S(1)} %get-tuple-element.33), channel_id=1, source_target_pairs={{0,12},{12,0},{4,8},{8,4},{1,13},{13,1},{5,9},{9,5},{2,14},{14,2},... | collective-permute-start | bytes 98312 | tf_op jit(solution)/shard_map/ppermute | solution.py:23
  15.8 0.4 collective-permute-start.2
  16.1 0.0 copy-done.4
  16.1 1.7 %collective-permute-start = (bf16[64,4096]{1,0:T(8,128)(2,1)S(1)}, bf16[64,4096]{1,0:T(8,128)(2,1)S(1)}, u32[]{:S(2)}, u32[]{:S(2)}) collective-permute-start(bf16[64,4096]{1,0:T(8,128)(2,1)S(1)} %bitcast.41), channel_id=1, source_target_pairs={{0,4},{4,12},{12,8},{8,0},{1,5},{5,13},{13,9},{9,1},{2,6},{6,14},{... | collective-permute-start | bytes 1572872 | tf_op jit(solution)/shard_map/ppermute | solution.py:23
  17.8 0.0 copy-done.5
  17.8 0.1 compare_bitcast_fusion.3
  18.0 0.1 pad_add_fusion.1.facts_ref
  18.0 1.4 %collective-permute-done.4 = bf16[8,2048]{1,0:T(8,128)(2,1)S(1)} collective-permute-done((bf16[8,2048]{1,0:T(8,128)(2,1)S(1)}, bf16[8,2048]{1,0:T(8,128)(2,1)S(1)}, u32[]{:S(2)}, u32[]{:S(2)}) %collective-permute-start.4) | collective-permute-done | bytes 32800 | tf_op jit(solution)/shard_map/ppermute | solution.py:23
  19.4 0.0 collective-permute-done.3
  19.4 0.7 collective-permute-done.2
  20.2 0.0 collective-permute-done.1.x_ref
  20.2 1.6 %collective-permute-start.7 = (bf16[4,8,2048]{2,1,0:T(8,128)(2,1)S(1)}, bf16[4,8,2048]{2,1,0:T(8,128)(2,1)S(1)}, u32[]{:S(2)}, u32[]{:S(2)}) collective-permute-start(bf16[4,8,2048]{2,1,0:T(8,128)(2,1)S(1)} %pad_maximum_fusion.1), channel_id=1, source_target_pairs={{0,16},{16,0},{1,17},{17,1},{2,18},{18,2},{3,19},{19,3},{4,20},{20... | collective-permute-start | bytes 393224 | tf_op jit(solution)/shard_map/ppermute | solution.py:27
  21.8 0.7 collective-permute-start.5
  22.4 1.3 %collective-permute-start.6 = (bf16[64,4096]{1,0:T(8,128)(2,1)S(1)}, bf16[64,4096]{1,0:T(8,128)(2,1)S(1)}, u32[]{:S(2)}, u32[]{:S(2)}) collective-permute-start(bf16[64,4096]{1,0:T(8,128)(2,1)S(1)} %collective-permute-done.1.x_ref), channel_id=1, source_target_pairs={{8,12},{4,0},{9,13},{5,1},{10,14},{6,2},{11,15},{7,3},{24,28},{20,... | collective-permute-start | bytes 1572872 | tf_op jit(solution)/shard_map/ppermute | solution.py:23
  23.7 0.0 copy-done
  23.8 0.3 fusion.5
  24.1 0.3 fusion.6
  24.3 0.0 copy-start.1
  24.4 5.8 %copy-done.1 = bf16[4096,2048]{1,0:T(8,128)(2,1)S(1)} copy-done((bf16[4096,2048]{1,0:T(8,128)(2,1)S(1)}, bf16[4096,2048]{1,0:T(8,128)(2,1)}, u32[]{:S(2)}) %copy-start.1) | copy-done | bytes 16777240
  30.1 4.3 %shard_map.56 = f32[64,2048]{1,0:T(8,128)S(1)} custom-call(bf16[64,4096]{1,0:T(8,128)(2,1)S(1)} %collective-permute-done.1.x_ref, bf16[4096,2048]{1,0:T(8,128)(2,1)S(1)} %copy-done.1), custom_call_target="tpu_custom_call" | custom-call | flops 1073741824 | bytes 16777216 | tf_op jit(solution)/shard_map/pallas_call | solution.py:86
  34.4 0.0 collective-permute-done.7
  34.5 0.1 collective-permute-start.10
  34.6 1.6 %collective-permute-start.9 = (bf16[64,2048]{1,0:T(8,128)(2,1)S(1)}, bf16[64,2048]{1,0:T(8,128)(2,1)S(1)}, u32[]{:S(2)}, u32[]{:S(2)}) collective-permute-start(bf16[64,2048]{1,0:T(8,128)(2,1)S(1)} %pad_maximum_fusion.refs_0_), channel_id=1, source_target_pairs={{0,2},{1,3},{2,0},{3,1},{4,6},{5,7},{6,4},{7,5},{8,10},{9,11},{10,... | collective-permute-start | bytes 786440 | tf_op jit(solution)/shard_map/ppermute | solution.py:23
  36.1 0.0 collective-permute-done.x3_ref
  36.1 0.3 collective-permute-start.8
  36.4 0.0 collective-permute-done.5.x2a_ref
  36.4 6.1 %collective-permute-done.6.x2b_ref = bf16[64,4096]{1,0:T(8,128)(2,1)S(1)} collective-permute-done((bf16[64,4096]{1,0:T(8,128)(2,1)S(1)}, bf16[64,4096]{1,0:T(8,128)(2,1)S(1)}, u32[]{:S(2)}, u32[]{:S(2)}) %collective-permute-start.6) | collective-permute-done | bytes 524320 | tf_op jit(solution)/shard_map/ppermute | solution.py:23
  42.5 0.3 fusion.7
  42.9 0.3 fusion.8
  43.2 0.6 collective-permute-start.13
  43.8 2.5 %collective-permute-start.12 = (bf16[256,64]{1,0:T(8,128)(2,1)S(1)}, bf16[256,64]{1,0:T(8,128)(2,1)S(1)}, u32[]{:S(2)}, u32[]{:S(2)}) collective-permute-start(bf16[256,64]{1,0:T(8,128)(2,1)S(1)} %pad_maximum_fusion.2), channel_id=1, source_target_pairs={{0,12},{12,0},{4,8},{8,4},{1,13},{13,1},{5,9},{9,5},{2,14},{14,2},... | collective-permute-start | bytes 98312 | tf_op jit(solution)/shard_map/ppermute | solution.py:23
  46.3 0.0 collective-permute-done.10.refs_3_
  46.3 1.4 %collective-permute-start.11 = (bf16[256,64]{1,0:T(8,128)(2,1)S(1)}, bf16[256,64]{1,0:T(8,128)(2,1)S(1)}, u32[]{:S(2)}, u32[]{:S(2)}) collective-permute-start(bf16[256,64]{1,0:T(8,128)(2,1)S(1)} %pad_maximum_fusion.2), channel_id=1, source_target_pairs={{4,0},{12,4},{8,12},{0,8},{5,1},{13,5},{9,13},{1,9},{6,2},{14,6},{... | collective-permute-start | bytes 98312 | tf_op jit(solution)/shard_map/ppermute | solution.py:23
  47.7 1.0 %collective-permute-done.9.refs_2_ = bf16[64,2048]{1,0:T(8,128)(2,1)S(1)} collective-permute-done((bf16[64,2048]{1,0:T(8,128)(2,1)S(1)}, bf16[64,2048]{1,0:T(8,128)(2,1)S(1)}, u32[]{:S(2)}, u32[]{:S(2)}) %collective-permute-start.9) | collective-permute-done | bytes 262176 | tf_op jit(solution)/shard_map/ppermute | solution.py:23
  48.8 0.0 collective-permute-done.8.refs_1_
  48.8 0.0 copy-done.2
  48.8 5.0 %shard_map.57 = (f32[128,2048]{1,0:T(8,128)S(1)}, bf16[256,2048]{1,0:T(8,128)(2,1)S(1)}) custom-call(s32[3]{0:T(128)S(1)} %pad_add_fusion.1.facts_ref, bf16[64,4096]{1,0:T(8,128)(2,1)S(1)} %collective-permute-done.x3_ref, bf16[64,4096]{1,0:T(8,128)(2,1)S(1)} %collective-permute-done.5.x2a_ref, bf16[64,4096]{1,0:T(8,128)(2,1)S(1)} %collective-permute-done.6.x2b_ref, ...), custom_call_target="tpu_custom_call" | custom-call | flops 2147483648 | bytes 16777216 | tf_op jit(solution)/shard_map/pallas_call | solution.py:139
  53.8 0.1 fusion.31
  53.9 0.1 constant_dynamic-slice_fusion.4
  54.0 0.0 collective-permute-done.13
  54.0 0.0 collective-permute-done.12
  54.1 0.0 collective-permute-done.11
  54.1 0.1 pad_maximum_fusion.5
  54.2 0.1 pad_maximum_fusion.6
  54.3 0.1 pad_maximum_fusion.4
  54.4 0.1 pad_maximum_fusion.3
  54.5 0.3 fusion.4
  54.8 0.1 collective-permute-start.14
  54.9 1.9 %collective-permute-done.14 = bf16[128,2048]{1,0:T(8,128)(2,1)S(1)} collective-permute-done((bf16[128,2048]{1,0:T(8,128)(2,1)S(1)}, bf16[128,2048]{1,0:T(8,128)(2,1)S(1)}, u32[]{:S(2)}, u32[]{:S(2)}) %collective-permute-start.14) | collective-permute-done | bytes 524320 | tf_op jit(solution)/shard_map/ppermute | solution.py:27
  56.8 0.3 fusion.3
  57.2 3.5 %collective-permute-start.17 = (bf16[32,2048]{1,0:T(8,128)(2,1)S(1)}, bf16[32,2048]{1,0:T(8,128)(2,1)S(1)}, u32[]{:S(2)}, u32[]{:S(2)}) collective-permute-start(bf16[32,2048]{1,0:T(8,128)(2,1)S(1)} %get-tuple-element.35), channel_id=1, source_target_pairs={{0,4},{4,12},{12,8},{8,0},{1,5},{5,13},{13,9},{9,1},{2,6},{6,14},{... | collective-permute-start | bytes 393224 | tf_op jit(solution)/shard_map/ppermute | solution.py:23
  60.6 2.1 %collective-permute-start.16 = (bf16[32,2048]{1,0:T(8,128)(2,1)S(1)}, bf16[32,2048]{1,0:T(8,128)(2,1)S(1)}, u32[]{:S(2)}, u32[]{:S(2)}) collective-permute-start(bf16[32,2048]{1,0:T(8,128)(2,1)S(1)} %get-tuple-element.36), channel_id=1, source_target_pairs={{0,12},{12,0},{4,8},{8,4},{1,13},{13,1},{5,9},{9,5},{2,14},{14,2},... | collective-permute-start | bytes 393224 | tf_op jit(solution)/shard_map/ppermute | solution.py:23
  62.7 0.0 collective-permute-start.15
  62.7 0.1 pad_add_fusion.where_ref
  62.8 2.9 %collective-permute-done.17.refs_3_ = bf16[32,2048]{1,0:T(8,128)(2,1)S(1)} collective-permute-done((bf16[32,2048]{1,0:T(8,128)(2,1)S(1)}, bf16[32,2048]{1,0:T(8,128)(2,1)S(1)}, u32[]{:S(2)}, u32[]{:S(2)}) %collective-permute-start.17) | collective-permute-done | bytes 131104 | tf_op jit(solution)/shard_map/ppermute | solution.py:23
  65.7 4.2 %collective-permute-done.16.refs_2_ = bf16[32,2048]{1,0:T(8,128)(2,1)S(1)} collective-permute-done((bf16[32,2048]{1,0:T(8,128)(2,1)S(1)}, bf16[32,2048]{1,0:T(8,128)(2,1)S(1)}, u32[]{:S(2)}, u32[]{:S(2)}) %collective-permute-start.16) | collective-permute-done | bytes 131104 | tf_op jit(solution)/shard_map/ppermute | solution.py:23
  70.0 0.9 %collective-permute-done.15.refs_1_ = bf16[32,2048]{1,0:T(8,128)(2,1)S(1)} collective-permute-done((bf16[32,2048]{1,0:T(8,128)(2,1)S(1)}, bf16[32,2048]{1,0:T(8,128)(2,1)S(1)}, u32[]{:S(2)}, u32[]{:S(2)}) %collective-permute-start.15) | collective-permute-done | bytes 131104 | tf_op jit(solution)/shard_map/ppermute | solution.py:23
  70.9 1.4 %shard_map.58 = bf16[32,8192]{1,0:T(8,128)(2,1)} custom-call(s32[4]{0:T(128)S(1)} %pad_add_fusion.where_ref, bf16[32,2048]{1,0:T(8,128)(2,1)S(1)} %get-tuple-element.38.refs_0_, bf16[32,2048]{1,0:T(8,128)(2,1)S(1)} %collective-permute-done.15.refs_1_, bf16[32,2048]{1,0:T(8,128)(2,1)S(1)} %collective-permute-done.16.refs_2_, ...), custom_call_target="tpu_custom_call" | custom-call | tf_op jit(solution)/shard_map/pallas_call | solution.py:48
  (15 shorter events, 0.2 us)
Async XLA Ops:
  0.0 23.8 %copy-start = (bf16[1,4096,64]{1,2,0:T(8,128)(2,1)S(1)}, bf16[1,4096,64]{1,2,0:T(8,128)(2,1)}, u32[]{:S(2)}) copy-start(bf16[1,4096,64]{1,2,0:T(8,128)(2,1)} %param.8) | copy-start | bytes 1572868
  0.0 17.8 %copy-start.5 = (s32[1,256,1]{1,2,0:T(1,128)S(1)}, s32[1,256,1]{1,2,0:T(1,128)}, u32[]{:S(2)}) copy-start(s32[1,256,1]{1,2,0:T(1,128)} %param.6) | copy-start | bytes 3076
  0.0 20.2 %collective-permute-start.1 = (bf16[64,4096]{1,0:T(8,128)(2,1)}, bf16[64,4096]{1,0:T(8,128)(2,1)S(1)}, u32[]{:S(2)}, u32[]{:S(2)}) collective-permute-start(bf16[64,4096]{1,0:T(8,128)(2,1)} %bitcast.39), channel_id=1, source_target_pairs={{4,0},{12,4},{8,12},{0,8},{5,1},{13,5},{9,13},{1,9},{6,2},{14,6},{... | collective-permute-start | bytes 1572872 | tf_op jit(solution)/shard_map/ppermute | solution.py:23
  4.0 1.1 %copy-start.3 = (bf16[1,64,4096]{2,1,0:T(8,128)(2,1)S(1)}, bf16[1,64,4096]{2,1,0:T(8,128)(2,1)}, u32[]{:S(2)}) copy-start(bf16[1,64,4096]{2,1,0:T(8,128)(2,1)} %param.5) | copy-start | bytes 1572868
  5.1 11.0 %copy-start.4 = (bf16[1,64,4096]{2,1,0:T(8,128)(2,1)S(1)}, bf16[1,64,4096]{2,1,0:T(8,128)(2,1)}, u32[]{:S(2)}) copy-start(bf16[1,64,4096]{2,1,0:T(8,128)(2,1)} %param.5) | copy-start | bytes 1572868
  12.7 6.7 %collective-permute-start.4 = (bf16[8,2048]{1,0:T(8,128)(2,1)S(1)}, bf16[8,2048]{1,0:T(8,128)(2,1)S(1)}, u32[]{:S(2)}, u32[]{:S(2)}) collective-permute-start(bf16[8,2048]{1,0:T(8,128)(2,1)S(1)} %get-tuple-element.32), channel_id=1, source_target_pairs={{0,4},{4,12},{12,8},{8,0},{1,5},{5,13},{13,9},{9,1},{2,6},{6,14},{... | collective-permute-start | bytes 98312 | tf_op jit(solution)/shard_map/ppermute | solution.py:23
  12.8 6.7 %collective-permute-start.3 = (bf16[8,2048]{1,0:T(8,128)(2,1)S(1)}, bf16[8,2048]{1,0:T(8,128)(2,1)S(1)}, u32[]{:S(2)}, u32[]{:S(2)}) collective-permute-start(bf16[8,2048]{1,0:T(8,128)(2,1)S(1)} %get-tuple-element.33), channel_id=1, source_target_pairs={{0,12},{12,0},{4,8},{8,4},{1,13},{13,1},{5,9},{9,5},{2,14},{14,2},... | collective-permute-start | bytes 98312 | tf_op jit(solution)/shard_map/ppermute | solution.py:23
  15.8 4.4 %collective-permute-start.2 = (bf16[8,2048]{1,0:T(8,128)(2,1)S(1)}, bf16[8,2048]{1,0:T(8,128)(2,1)S(1)}, u32[]{:S(2)}, u32[]{:S(2)}) collective-permute-start(bf16[8,2048]{1,0:T(8,128)(2,1)S(1)} %get-tuple-element.34), channel_id=1, source_target_pairs={{4,0},{12,4},{8,12},{0,8},{5,1},{13,5},{9,13},{1,9},{6,2},{14,6},{... | collective-permute-start | bytes 98312 | tf_op jit(solution)/shard_map/ppermute | solution.py:23
  16.1 20.0 %collective-permute-start = (bf16[64,4096]{1,0:T(8,128)(2,1)S(1)}, bf16[64,4096]{1,0:T(8,128)(2,1)S(1)}, u32[]{:S(2)}, u32[]{:S(2)}) collective-permute-start(bf16[64,4096]{1,0:T(8,128)(2,1)S(1)} %bitcast.41), channel_id=1, source_target_pairs={{0,4},{4,12},{12,8},{8,0},{1,5},{5,13},{13,9},{9,1},{2,6},{6,14},{... | collective-permute-start | bytes 1572872 | tf_op jit(solution)/shard_map/ppermute | solution.py:23
  20.2 14.3 %collective-permute-start.7 = (bf16[4,8,2048]{2,1,0:T(8,128)(2,1)S(1)}, bf16[4,8,2048]{2,1,0:T(8,128)(2,1)S(1)}, u32[]{:S(2)}, u32[]{:S(2)}) collective-permute-start(bf16[4,8,2048]{2,1,0:T(8,128)(2,1)S(1)} %pad_maximum_fusion.1), channel_id=1, source_target_pairs={{0,16},{16,0},{1,17},{17,1},{2,18},{18,2},{3,19},{19,3},{4,20},{20... | collective-permute-start | bytes 393224 | tf_op jit(solution)/shard_map/ppermute | solution.py:27
  21.8 14.7 %collective-permute-start.5 = (bf16[64,4096]{1,0:T(8,128)(2,1)S(1)}, bf16[64,4096]{1,0:T(8,128)(2,1)S(1)}, u32[]{:S(2)}, u32[]{:S(2)}) collective-permute-start(bf16[64,4096]{1,0:T(8,128)(2,1)S(1)} %bitcast.42), channel_id=1, source_target_pairs={{4,8},{8,4},{5,9},{9,5},{6,10},{10,6},{7,11},{11,7},{20,24},{24,20... | collective-permute-start | bytes 1572872 | tf_op jit(solution)/shard_map/ppermute | solution.py:23
  22.4 20.1 %collective-permute-start.6 = (bf16[64,4096]{1,0:T(8,128)(2,1)S(1)}, bf16[64,4096]{1,0:T(8,128)(2,1)S(1)}, u32[]{:S(2)}, u32[]{:S(2)}) collective-permute-start(bf16[64,4096]{1,0:T(8,128)(2,1)S(1)} %collective-permute-done.1.x_ref), channel_id=1, source_target_pairs={{8,12},{4,0},{9,13},{5,1},{10,14},{6,2},{11,15},{7,3},{24,28},{20,... | collective-permute-start | bytes 1572872 | tf_op jit(solution)/shard_map/ppermute | solution.py:23
  24.3 5.8 %copy-start.1 = (bf16[4096,2048]{1,0:T(8,128)(2,1)S(1)}, bf16[4096,2048]{1,0:T(8,128)(2,1)}, u32[]{:S(2)}) copy-start(bf16[4096,2048]{1,0:T(8,128)(2,1)} %refs_4_.1) | copy-start | bytes 50331652
  30.1 18.6 %copy-start.2 = (bf16[4096,2048]{1,0:T(8,128)(2,1)S(1)}, bf16[4096,2048]{1,0:T(8,128)(2,1)}, u32[]{:S(2)}) copy-start(bf16[4096,2048]{1,0:T(8,128)(2,1)} %refs_4_.1) | copy-start | bytes 50331652
  34.5 11.8 %collective-permute-start.10 = (bf16[64,2048]{1,0:T(8,128)(2,1)S(1)}, bf16[64,2048]{1,0:T(8,128)(2,1)S(1)}, u32[]{:S(2)}, u32[]{:S(2)}) collective-permute-start(bf16[64,2048]{1,0:T(8,128)(2,1)S(1)} %pad_maximum_fusion.refs_0_), channel_id=1, source_target_pairs={{0,3},{1,2},{2,1},{3,0},{4,7},{5,6},{6,5},{7,4},{8,11},{9,10},{10,... | collective-permute-start | bytes 786440 | tf_op jit(solution)/shard_map/ppermute | solution.py:23
  34.6 14.2 %collective-permute-start.9 = (bf16[64,2048]{1,0:T(8,128)(2,1)S(1)}, bf16[64,2048]{1,0:T(8,128)(2,1)S(1)}, u32[]{:S(2)}, u32[]{:S(2)}) collective-permute-start(bf16[64,2048]{1,0:T(8,128)(2,1)S(1)} %pad_maximum_fusion.refs_0_), channel_id=1, source_target_pairs={{0,2},{1,3},{2,0},{3,1},{4,6},{5,7},{6,4},{7,5},{8,10},{9,11},{10,... | collective-permute-start | bytes 786440 | tf_op jit(solution)/shard_map/ppermute | solution.py:23
  36.1 12.6 %collective-permute-start.8 = (bf16[64,2048]{1,0:T(8,128)(2,1)S(1)}, bf16[64,2048]{1,0:T(8,128)(2,1)S(1)}, u32[]{:S(2)}, u32[]{:S(2)}) collective-permute-start(bf16[64,2048]{1,0:T(8,128)(2,1)S(1)} %pad_maximum_fusion.refs_0_), channel_id=1, source_target_pairs={{0,1},{1,0},{2,3},{3,2},{4,5},{5,4},{6,7},{7,6},{8,9},{9,8},{10,11... | collective-permute-start | bytes 786440 | tf_op jit(solution)/shard_map/ppermute | solution.py:23
  43.2 10.8 %collective-permute-start.13 = (bf16[256,64]{1,0:T(8,128)(2,1)S(1)}, bf16[256,64]{1,0:T(8,128)(2,1)S(1)}, u32[]{:S(2)}, u32[]{:S(2)}) collective-permute-start(bf16[256,64]{1,0:T(8,128)(2,1)S(1)} %pad_maximum_fusion.2), channel_id=1, source_target_pairs={{0,4},{4,12},{12,8},{8,0},{1,5},{5,13},{13,9},{9,1},{2,6},{6,14},{... | collective-permute-start | bytes 98312 | tf_op jit(solution)/shard_map/ppermute | solution.py:23
  43.8 10.2 %collective-permute-start.12 = (bf16[256,64]{1,0:T(8,128)(2,1)S(1)}, bf16[256,64]{1,0:T(8,128)(2,1)S(1)}, u32[]{:S(2)}, u32[]{:S(2)}) collective-permute-start(bf16[256,64]{1,0:T(8,128)(2,1)S(1)} %pad_maximum_fusion.2), channel_id=1, source_target_pairs={{0,12},{12,0},{4,8},{8,4},{1,13},{13,1},{5,9},{9,5},{2,14},{14,2},... | collective-permute-start | bytes 98312 | tf_op jit(solution)/shard_map/ppermute | solution.py:23
  46.3 7.7 %collective-permute-start.11 = (bf16[256,64]{1,0:T(8,128)(2,1)S(1)}, bf16[256,64]{1,0:T(8,128)(2,1)S(1)}, u32[]{:S(2)}, u32[]{:S(2)}) collective-permute-start(bf16[256,64]{1,0:T(8,128)(2,1)S(1)} %pad_maximum_fusion.2), channel_id=1, source_target_pairs={{4,0},{12,4},{8,12},{0,8},{5,1},{13,5},{9,13},{1,9},{6,2},{14,6},{... | collective-permute-start | bytes 98312 | tf_op jit(solution)/shard_map/ppermute | solution.py:23
  54.8 2.0 %collective-permute-start.14 = (bf16[128,2048]{1,0:T(8,128)(2,1)S(1)}, bf16[128,2048]{1,0:T(8,128)(2,1)S(1)}, u32[]{:S(2)}, u32[]{:S(2)}) collective-permute-start(bf16[128,2048]{1,0:T(8,128)(2,1)S(1)} %fusion.4), channel_id=1, source_target_pairs={{0,1},{1,0},{2,3},{3,2},{4,5},{5,4},{6,7},{7,6},{8,9},{9,8},{10,11... | collective-permute-start | bytes 1572872 | tf_op jit(solution)/shard_map/ppermute | solution.py:27
  57.2 8.6 %collective-permute-start.17 = (bf16[32,2048]{1,0:T(8,128)(2,1)S(1)}, bf16[32,2048]{1,0:T(8,128)(2,1)S(1)}, u32[]{:S(2)}, u32[]{:S(2)}) collective-permute-start(bf16[32,2048]{1,0:T(8,128)(2,1)S(1)} %get-tuple-element.35), channel_id=1, source_target_pairs={{0,4},{4,12},{12,8},{8,0},{1,5},{5,13},{13,9},{9,1},{2,6},{6,14},{... | collective-permute-start | bytes 393224 | tf_op jit(solution)/shard_map/ppermute | solution.py:23
  60.6 9.3 %collective-permute-start.16 = (bf16[32,2048]{1,0:T(8,128)(2,1)S(1)}, bf16[32,2048]{1,0:T(8,128)(2,1)S(1)}, u32[]{:S(2)}, u32[]{:S(2)}) collective-permute-start(bf16[32,2048]{1,0:T(8,128)(2,1)S(1)} %get-tuple-element.36), channel_id=1, source_target_pairs={{0,12},{12,0},{4,8},{8,4},{1,13},{13,1},{5,9},{9,5},{2,14},{14,2},... | collective-permute-start | bytes 393224 | tf_op jit(solution)/shard_map/ppermute | solution.py:23
  62.7 8.1 %collective-permute-start.15 = (bf16[32,2048]{1,0:T(8,128)(2,1)S(1)}, bf16[32,2048]{1,0:T(8,128)(2,1)S(1)}, u32[]{:S(2)}, u32[]{:S(2)}) collective-permute-start(bf16[32,2048]{1,0:T(8,128)(2,1)S(1)} %get-tuple-element.37), channel_id=1, source_target_pairs={{4,0},{12,4},{8,12},{0,8},{5,1},{13,5},{9,13},{1,9},{6,2},{14,6},{... | collective-permute-start | bytes 393224 | tf_op jit(solution)/shard_map/ppermute | solution.py:23

commit v6 on v5

--- a/solution.py
+++ b/solution.py
@@ -192,10 +192,10 @@
     x1, part, own = lax.optimization_barrier((x1, part, own))
     x2a = shift(own, INNER)
     x2b = shift(x1, RELAY)
-    base1 = stream(x1, query_weight, NEXT_LIMIT)
+    part = jnp.concatenate([part.reshape(4 * share, width), swap(part, "groups").reshape(4 * share, width)])
+    base1 = stream(after(x1, part), query_weight, NEXT_LIMIT)
+    parts = [part] + [shift(part, [(i, i ^ k) for i in range(peers)], inside) for k in range(1, peers)]
     x3, x2a, x2b, base1 = lax.optimization_barrier((x3, x2a, x2b, base1))
-    part = jnp.concatenate([part.reshape(4 * share, width), swap(part, "groups").reshape(4 * share, width)])
-    parts = [part] + [shift(part, [(i, i ^ k) for i in range(peers)], inside) for k in range(1, peers)]
 
     x2 = jnp.where(inner, x2a, x2b)
     ranks = []

time: 72.7 us -> 70.7 us (0.972)
  starting transfers between devices: 24.8 us -> 22.7 us
    ppermute x16, starting transfers between devices: 23.1 us -> 21.1 us  [shift(): return lax.ppermute(x, axis, pairs)]
    ppermute x2, waiting for transfers between devices: 1.87 us -> 2.76 us  [swap(): return lax.ppermute(x, axis, ((0, 1), (1, 0)))]
  transfers between devices with their start and end apart: 18 -> 18, of which waited for: 8 -> 6; matrix products, arithmetic and copies ran while one was open for 4% -> 4% of each run, Pallas kernels for 22% -> 22%
where the time goes in v6:
time: 70.7 us; the launch traced here: 70.5 us
  starting transfers between devices  22.7 us (32%)
  waiting for transfers between devices  19.5 us (28%)
  Pallas kernels  17.1 us (24%)
  local copies, waits for them, and re-layouts  8.33 us (12%)
  matrix products  1.84 us (3%)
    ppermute x16, starting transfers between devices, shift(): return lax.ppermute(x, axis, pairs)  21.1 us
    ppermute x16, waiting for transfers between devices, shift(): return lax.ppermute(x, axis, pairs)  16.8 us
    pallas_call x2, Pallas kernels, stream(): pl.pallas_call(stream_kernel, out_shape=jax.ShapeDtypeStruct((rows, width...  10.8 us
    unnamed x12, local copies, waits for them, and re-layouts  6.86 us
    pallas_call x1, Pallas kernels, last(): pl.pallas_call(last_kernel, out_shape=[jax.ShapeDtypeStruct((2 * rows, wi...  5 us
    ppermute x2, waiting for transfers between devices, swap(): return lax.ppermute(x, axis, ((0, 1), (1, 0)))  2.76 us
    dot_general x6, matrix products, dot(): return jnp.dot(a, b, preferred_element_type=F32)  1.84 us
    ppermute x2, starting transfers between devices, swap(): return lax.ppermute(x, axis, ((0, 1), (1, 0)))  1.66 us
  transfers between devices with their start and end apart: 18, of which 6 were waited for; matrix products, arithmetic and copies ran while one was open for 4% of the time, Pallas kernels for 22%

profile of v6, /device:TPU:0, one launch (start us, length us, event | category | flops | bytes accessed | tf_op | source)
XLA Modules:
  0.0 70.5 jit_solution(11115491131383689469)
XLA Ops:
  0.0 0.0 copy-start
  0.0 0.0 copy-start.5
  0.0 4.0 %collective-permute-start.1 = (bf16[64,4096]{1,0:T(8,128)(2,1)}, bf16[64,4096]{1,0:T(8,128)(2,1)S(1)}, u32[]{:S(2)}, u32[]{:S(2)}) collective-permute-start(bf16[64,4096]{1,0:T(8,128)(2,1)} %bitcast.39), channel_id=1, source_target_pairs={{4,0},{12,4},{8,12},{0,8},{5,1},{13,5},{9,13},{1,9},{6,2},{14,6},{... | collective-permute-start | bytes 1572872 | tf_op jit(solution)/shard_map/ppermute | solution.py:23
  4.0 1.1 %copy-done.3 = bf16[1,64,4096]{2,1,0:T(8,128)(2,1)S(1)} copy-done((bf16[1,64,4096]{2,1,0:T(8,128)(2,1)S(1)}, bf16[1,64,4096]{2,1,0:T(8,128)(2,1)}, u32[]{:S(2)}) %copy-start.3) | copy-done | bytes 524312
  5.1 6.5 %shard_map.55 = f32[64,2048]{1,0:T(8,128)S(1)} custom-call(bf16[64,4096]{1,0:T(8,128)(2,1)S(1)} %bitcast.40, bf16[4096,2048]{1,0:T(8,128)(2,1)} %refs_4_.1), custom_call_target="tpu_custom_call" | custom-call | flops 1073741824 | bytes 16777216 | tf_op jit(solution)/shard_map/pallas_call | solution.py:86
  11.6 1.1 %dynamic-slice_bitcast_fusion = (bf16[1,8,2048]{2,1,0:T(8,128)(2,1)S(1)}, bf16[8,2048]{1,0:T(8,128)(2,1)S(1)}, bf16[8,2048]{1,0:T(8,128)(2,1)S(1)}, bf16[8,2048]{1,0:T(8,128)(2,1)S(1)}) fusion(bf16[64,8192]{1,0:T(8,128)(2,1)} %bitcast.49, s32[]{:T(128)S(6)} %select_n.98, s32[]{:T(128)S(6)} %select_n.100, s32[]{:T(128)S(6)} %select_n.106, s32[]{:T(128)S(6)} %select_n.104, ...), kind=kLoop, calls=%fused_computation.42 | loop fusion | bytes 262164 | tf_op jit(solution)/shard_map/stack | solution.py:189
  12.7 0.1 collective-permute-start.4
  12.8 3.0 %collective-permute-start.3 = (bf16[8,2048]{1,0:T(8,128)(2,1)S(1)}, bf16[8,2048]{1,0:T(8,128)(2,1)S(1)}, u32[]{:S(2)}, u32[]{:S(2)}) collective-permute-start(bf16[8,2048]{1,0:T(8,128)(2,1)S(1)} %get-tuple-element.35), channel_id=1, source_target_pairs={{0,12},{12,0},{4,8},{8,4},{1,13},{13,1},{5,9},{9,5},{2,14},{14,2},... | collective-permute-start | bytes 98312 | tf_op jit(solution)/shard_map/ppermute | solution.py:23
  15.8 0.4 collective-permute-start.2
  16.1 0.0 copy-done.4
  16.1 1.7 %collective-permute-start = (bf16[64,4096]{1,0:T(8,128)(2,1)S(1)}, bf16[64,4096]{1,0:T(8,128)(2,1)S(1)}, u32[]{:S(2)}, u32[]{:S(2)}) collective-permute-start(bf16[64,4096]{1,0:T(8,128)(2,1)S(1)} %bitcast.41), channel_id=1, source_target_pairs={{0,4},{4,12},{12,8},{8,0},{1,5},{5,13},{13,9},{9,1},{2,6},{6,14},{... | collective-permute-start | bytes 1572872 | tf_op jit(solution)/shard_map/ppermute | solution.py:23
  17.8 0.0 copy-done.5
  17.8 0.1 compare_bitcast_fusion.3
  18.0 0.1 pad_add_fusion.1.facts_ref
  18.0 1.4 %collective-permute-done.4 = bf16[8,2048]{1,0:T(8,128)(2,1)S(1)} collective-permute-done((bf16[8,2048]{1,0:T(8,128)(2,1)S(1)}, bf16[8,2048]{1,0:T(8,128)(2,1)S(1)}, u32[]{:S(2)}, u32[]{:S(2)}) %collective-permute-start.4) | collective-permute-done | bytes 32800 | tf_op jit(solution)/shard_map/ppermute | solution.py:23
  19.4 0.0 collective-permute-done.3
  19.4 0.7 collective-permute-done.2
  20.2 0.0 collective-permute-done.1.x_ref
  20.2 1.6 %collective-permute-start.7 = (bf16[4,8,2048]{2,1,0:T(8,128)(2,1)S(1)}, bf16[4,8,2048]{2,1,0:T(8,128)(2,1)S(1)}, u32[]{:S(2)}, u32[]{:S(2)}) collective-permute-start(bf16[4,8,2048]{2,1,0:T(8,128)(2,1)S(1)} %pad_maximum_fusion.1), channel_id=1, source_target_pairs={{0,16},{16,0},{1,17},{17,1},{2,18},{18,2},{3,19},{19,3},{4,20},{20... | collective-permute-start | bytes 393224 | tf_op jit(solution)/shard_map/ppermute | solution.py:27
  21.8 0.7 collective-permute-start.5
  22.4 1.3 %collective-permute-start.6 = (bf16[64,4096]{1,0:T(8,128)(2,1)S(1)}, bf16[64,4096]{1,0:T(8,128)(2,1)S(1)}, u32[]{:S(2)}, u32[]{:S(2)}) collective-permute-start(bf16[64,4096]{1,0:T(8,128)(2,1)S(1)} %collective-permute-done.1.x_ref), channel_id=1, source_target_pairs={{8,12},{4,0},{9,13},{5,1},{10,14},{6,2},{11,15},{7,3},{24,28},{20,... | collective-permute-start | bytes 1572872 | tf_op jit(solution)/shard_map/ppermute | solution.py:23
  23.7 0.0 copy-done
  23.8 0.3 fusion.5
  24.1 0.3 fusion.6
  24.3 0.9 %collective-permute-done.7 = bf16[4,8,2048]{2,1,0:T(8,128)(2,1)S(1)} collective-permute-done((bf16[4,8,2048]{2,1,0:T(8,128)(2,1)S(1)}, bf16[4,8,2048]{2,1,0:T(8,128)(2,1)S(1)}, u32[]{:S(2)}, u32[]{:S(2)}) %collective-permute-start.7) | collective-permute-done | bytes 131104 | tf_op jit(solution)/shard_map/ppermute | solution.py:27
  25.2 0.1 collective-permute-start.10
  25.3 1.6 %collective-permute-start.9 = (bf16[64,2048]{1,0:T(8,128)(2,1)S(1)}, bf16[64,2048]{1,0:T(8,128)(2,1)S(1)}, u32[]{:S(2)}, u32[]{:S(2)}) collective-permute-start(bf16[64,2048]{1,0:T(8,128)(2,1)S(1)} %pad_maximum_fusion.refs_0_), channel_id=1, source_target_pairs={{0,2},{1,3},{2,0},{3,1},{4,6},{5,7},{6,4},{7,5},{8,10},{9,11},{10,... | collective-permute-start | bytes 786440 | tf_op jit(solution)/shard_map/ppermute | solution.py:23
  26.9 5.8 %copy-done.1 = bf16[4096,2048]{1,0:T(8,128)(2,1)S(1)} copy-done((bf16[4096,2048]{1,0:T(8,128)(2,1)S(1)}, bf16[4096,2048]{1,0:T(8,128)(2,1)}, u32[]{:S(2)}) %copy-start.1) | copy-done | bytes 16777240
  32.6 4.3 %shard_map.56 = f32[64,2048]{1,0:T(8,128)S(1)} custom-call(bf16[64,4096]{1,0:T(8,128)(2,1)S(1)} %collective-permute-done.1.x_ref, bf16[4096,2048]{1,0:T(8,128)(2,1)S(1)} %copy-done.1), custom_call_target="tpu_custom_call" | custom-call | flops 1073741824 | bytes 16777216 | tf_op jit(solution)/shard_map/pallas_call | solution.py:86
  37.0 0.0 collective-permute-done.x3_ref
  37.0 0.4 collective-permute-start.8
  37.3 0.0 collective-permute-done.5.x2a_ref
  37.3 5.2 %collective-permute-done.6.x2b_ref = bf16[64,4096]{1,0:T(8,128)(2,1)S(1)} collective-permute-done((bf16[64,4096]{1,0:T(8,128)(2,1)S(1)}, bf16[64,4096]{1,0:T(8,128)(2,1)S(1)}, u32[]{:S(2)}, u32[]{:S(2)}) %collective-permute-start.6) | collective-permute-done | bytes 524320 | tf_op jit(solution)/shard_map/ppermute | solution.py:23
  42.5 0.3 fusion.7
  42.9 0.3 fusion.8
  43.2 0.6 collective-permute-start.13
  43.8 2.5 %collective-permute-start.12 = (bf16[256,64]{1,0:T(8,128)(2,1)S(1)}, bf16[256,64]{1,0:T(8,128)(2,1)S(1)}, u32[]{:S(2)}, u32[]{:S(2)}) collective-permute-start(bf16[256,64]{1,0:T(8,128)(2,1)S(1)} %pad_maximum_fusion.2), channel_id=1, source_target_pairs={{0,12},{12,0},{4,8},{8,4},{1,13},{13,1},{5,9},{9,5},{2,14},{14,2},... | collective-permute-start | bytes 98312 | tf_op jit(solution)/shard_map/ppermute | solution.py:23
  46.3 0.0 collective-permute-done.10.refs_3_
  46.3 1.4 %collective-permute-start.11 = (bf16[256,64]{1,0:T(8,128)(2,1)S(1)}, bf16[256,64]{1,0:T(8,128)(2,1)S(1)}, u32[]{:S(2)}, u32[]{:S(2)}) collective-permute-start(bf16[256,64]{1,0:T(8,128)(2,1)S(1)} %pad_maximum_fusion.2), channel_id=1, source_target_pairs={{4,0},{12,4},{8,12},{0,8},{5,1},{13,5},{9,13},{1,9},{6,2},{14,6},{... | collective-permute-start | bytes 98312 | tf_op jit(solution)/shard_map/ppermute | solution.py:23
  47.7 0.0 collective-permute-done.9.refs_2_
  47.7 0.0 collective-permute-done.8.refs_1_
  47.7 0.0 copy-done.2
  47.8 5.0 %shard_map.57 = (f32[128,2048]{1,0:T(8,128)S(1)}, bf16[256,2048]{1,0:T(8,128)(2,1)S(1)}) custom-call(s32[3]{0:T(128)S(1)} %pad_add_fusion.1.facts_ref, bf16[64,4096]{1,0:T(8,128)(2,1)S(1)} %collective-permute-done.x3_ref, bf16[64,4096]{1,0:T(8,128)(2,1)S(1)} %collective-permute-done.5.x2a_ref, bf16[64,4096]{1,0:T(8,128)(2,1)S(1)} %collective-permute-done.6.x2b_ref, ...), custom_call_target="tpu_custom_call" | custom-call | flops 2147483648 | bytes 16777216 | tf_op jit(solution)/shard_map/pallas_call | solution.py:139
  52.8 0.1 fusion.31
  52.8 0.1 constant_dynamic-slice_fusion.4
  53.0 0.0 collective-permute-done.13
  53.0 0.0 collective-permute-done.12
  53.0 0.0 collective-permute-done.11
  53.1 0.1 pad_maximum_fusion.5
  53.2 0.1 pad_maximum_fusion.6
  53.3 0.1 pad_maximum_fusion.4
  53.4 0.1 pad_maximum_fusion.3
  53.5 0.3 fusion.4
  53.8 0.1 collective-permute-start.14
  53.9 1.9 %collective-permute-done.14 = bf16[128,2048]{1,0:T(8,128)(2,1)S(1)} collective-permute-done((bf16[128,2048]{1,0:T(8,128)(2,1)S(1)}, bf16[128,2048]{1,0:T(8,128)(2,1)S(1)}, u32[]{:S(2)}, u32[]{:S(2)}) %collective-permute-start.14) | collective-permute-done | bytes 524320 | tf_op jit(solution)/shard_map/ppermute | solution.py:27
  55.8 0.3 fusion.3
  56.2 0.7 collective-permute-start.17
  56.8 1.8 %collective-permute-start.16 = (bf16[32,2048]{1,0:T(8,128)(2,1)S(1)}, bf16[32,2048]{1,0:T(8,128)(2,1)S(1)}, u32[]{:S(2)}, u32[]{:S(2)}) collective-permute-start(bf16[32,2048]{1,0:T(8,128)(2,1)S(1)} %get-tuple-element.38), channel_id=1, source_target_pairs={{0,12},{12,0},{4,8},{8,4},{1,13},{13,1},{5,9},{9,5},{2,14},{14,2},... | collective-permute-start | bytes 393224 | tf_op jit(solution)/shard_map/ppermute | solution.py:23
  58.6 1.0 %collective-permute-start.15 = (bf16[32,2048]{1,0:T(8,128)(2,1)S(1)}, bf16[32,2048]{1,0:T(8,128)(2,1)S(1)}, u32[]{:S(2)}, u32[]{:S(2)}) collective-permute-start(bf16[32,2048]{1,0:T(8,128)(2,1)S(1)} %get-tuple-element.39), channel_id=1, source_target_pairs={{4,0},{12,4},{8,12},{0,8},{5,1},{13,5},{9,13},{1,9},{6,2},{14,6},{... | collective-permute-start | bytes 393224 | tf_op jit(solution)/shard_map/ppermute | solution.py:23
  59.6 0.1 pad_add_fusion.where_ref
  59.7 9.4 %collective-permute-done.17.refs_3_ = bf16[32,2048]{1,0:T(8,128)(2,1)S(1)} collective-permute-done((bf16[32,2048]{1,0:T(8,128)(2,1)S(1)}, bf16[32,2048]{1,0:T(8,128)(2,1)S(1)}, u32[]{:S(2)}, u32[]{:S(2)}) %collective-permute-start.17) | collective-permute-done | bytes 131104 | tf_op jit(solution)/shard_map/ppermute | solution.py:23
  69.1 0.0 collective-permute-done.16.refs_2_
  69.1 0.0 collective-permute-done.15.refs_1_
  69.1 1.4 %shard_map.58 = bf16[32,8192]{1,0:T(8,128)(2,1)} custom-call(s32[4]{0:T(128)S(1)} %pad_add_fusion.where_ref, bf16[32,2048]{1,0:T(8,128)(2,1)S(1)} %get-tuple-element.40.refs_0_, bf16[32,2048]{1,0:T(8,128)(2,1)S(1)} %collective-permute-done.15.refs_1_, bf16[32,2048]{1,0:T(8,128)(2,1)S(1)} %collective-permute-done.16.refs_2_, ...), custom_call_target="tpu_custom_call" | custom-call | tf_op jit(solution)/shard_map/pallas_call | solution.py:48
  (15 shorter events, 0.2 us)
Async XLA Ops:
  0.0 23.8 %copy-start = (bf16[1,4096,64]{1,2,0:T(8,128)(2,1)S(1)}, bf16[1,4096,64]{1,2,0:T(8,128)(2,1)}, u32[]{:S(2)}) copy-start(bf16[1,4096,64]{1,2,0:T(8,128)(2,1)} %param.8) | copy-start | bytes 1572868
  0.0 17.8 %copy-start.5 = (s32[1,256,1]{1,2,0:T(1,128)S(1)}, s32[1,256,1]{1,2,0:T(1,128)}, u32[]{:S(2)}) copy-start(s32[1,256,1]{1,2,0:T(1,128)} %param.6) | copy-start | bytes 3076
  0.0 20.2 %collective-permute-start.1 = (bf16[64,4096]{1,0:T(8,128)(2,1)}, bf16[64,4096]{1,0:T(8,128)(2,1)S(1)}, u32[]{:S(2)}, u32[]{:S(2)}) collective-permute-start(bf16[64,4096]{1,0:T(8,128)(2,1)} %bitcast.39), channel_id=1, source_target_pairs={{4,0},{12,4},{8,12},{0,8},{5,1},{13,5},{9,13},{1,9},{6,2},{14,6},{... | collective-permute-start | bytes 1572872 | tf_op jit(solution)/shard_map/ppermute | solution.py:23
  4.0 1.1 %copy-start.3 = (bf16[1,64,4096]{2,1,0:T(8,128)(2,1)S(1)}, bf16[1,64,4096]{2,1,0:T(8,128)(2,1)}, u32[]{:S(2)}) copy-start(bf16[1,64,4096]{2,1,0:T(8,128)(2,1)} %param.5) | copy-start | bytes 1572868
  5.1 11.0 %copy-start.4 = (bf16[1,64,4096]{2,1,0:T(8,128)(2,1)S(1)}, bf16[1,64,4096]{2,1,0:T(8,128)(2,1)}, u32[]{:S(2)}) copy-start(bf16[1,64,4096]{2,1,0:T(8,128)(2,1)} %param.5) | copy-start | bytes 1572868
  12.7 6.7 %collective-permute-start.4 = (bf16[8,2048]{1,0:T(8,128)(2,1)S(1)}, bf16[8,2048]{1,0:T(8,128)(2,1)S(1)}, u32[]{:S(2)}, u32[]{:S(2)}) collective-permute-start(bf16[8,2048]{1,0:T(8,128)(2,1)S(1)} %get-tuple-element.34), channel_id=1, source_target_pairs={{0,4},{4,12},{12,8},{8,0},{1,5},{5,13},{13,9},{9,1},{2,6},{6,14},{... | collective-permute-start | bytes 98312 | tf_op jit(solution)/shard_map/ppermute | solution.py:23
  12.8 6.7 %collective-permute-start.3 = (bf16[8,2048]{1,0:T(8,128)(2,1)S(1)}, bf16[8,2048]{1,0:T(8,128)(2,1)S(1)}, u32[]{:S(2)}, u32[]{:S(2)}) collective-permute-start(bf16[8,2048]{1,0:T(8,128)(2,1)S(1)} %get-tuple-element.35), channel_id=1, source_target_pairs={{0,12},{12,0},{4,8},{8,4},{1,13},{13,1},{5,9},{9,5},{2,14},{14,2},... | collective-permute-start | bytes 98312 | tf_op jit(solution)/shard_map/ppermute | solution.py:23
  15.8 4.4 %collective-permute-start.2 = (bf16[8,2048]{1,0:T(8,128)(2,1)S(1)}, bf16[8,2048]{1,0:T(8,128)(2,1)S(1)}, u32[]{:S(2)}, u32[]{:S(2)}) collective-permute-start(bf16[8,2048]{1,0:T(8,128)(2,1)S(1)} %get-tuple-element.36), channel_id=1, source_target_pairs={{4,0},{12,4},{8,12},{0,8},{5,1},{13,5},{9,13},{1,9},{6,2},{14,6},{... | collective-permute-start | bytes 98312 | tf_op jit(solution)/shard_map/ppermute | solution.py:23
  16.1 20.8 %collective-permute-start = (bf16[64,4096]{1,0:T(8,128)(2,1)S(1)}, bf16[64,4096]{1,0:T(8,128)(2,1)S(1)}, u32[]{:S(2)}, u32[]{:S(2)}) collective-permute-start(bf16[64,4096]{1,0:T(8,128)(2,1)S(1)} %bitcast.41), channel_id=1, source_target_pairs={{0,4},{4,12},{12,8},{8,0},{1,5},{5,13},{13,9},{9,1},{2,6},{6,14},{... | collective-permute-start | bytes 1572872 | tf_op jit(solution)/shard_map/ppermute | solution.py:23
  20.2 5.0 %collective-permute-start.7 = (bf16[4,8,2048]{2,1,0:T(8,128)(2,1)S(1)}, bf16[4,8,2048]{2,1,0:T(8,128)(2,1)S(1)}, u32[]{:S(2)}, u32[]{:S(2)}) collective-permute-start(bf16[4,8,2048]{2,1,0:T(8,128)(2,1)S(1)} %pad_maximum_fusion.1), channel_id=1, source_target_pairs={{0,16},{16,0},{1,17},{17,1},{2,18},{18,2},{3,19},{19,3},{4,20},{20... | collective-permute-start | bytes 393224 | tf_op jit(solution)/shard_map/ppermute | solution.py:27
  21.8 15.6 %collective-permute-start.5 = (bf16[64,4096]{1,0:T(8,128)(2,1)S(1)}, bf16[64,4096]{1,0:T(8,128)(2,1)S(1)}, u32[]{:S(2)}, u32[]{:S(2)}) collective-permute-start(bf16[64,4096]{1,0:T(8,128)(2,1)S(1)} %bitcast.42), channel_id=1, source_target_pairs={{4,8},{8,4},{5,9},{9,5},{6,10},{10,6},{7,11},{11,7},{20,24},{24,20... | collective-permute-start | bytes 1572872 | tf_op jit(solution)/shard_map/ppermute | solution.py:23
  22.4 20.1 %collective-permute-start.6 = (bf16[64,4096]{1,0:T(8,128)(2,1)S(1)}, bf16[64,4096]{1,0:T(8,128)(2,1)S(1)}, u32[]{:S(2)}, u32[]{:S(2)}) collective-permute-start(bf16[64,4096]{1,0:T(8,128)(2,1)S(1)} %collective-permute-done.1.x_ref), channel_id=1, source_target_pairs={{8,12},{4,0},{9,13},{5,1},{10,14},{6,2},{11,15},{7,3},{24,28},{20,... | collective-permute-start | bytes 1572872 | tf_op jit(solution)/shard_map/ppermute | solution.py:23
  25.2 21.1 %collective-permute-start.10 = (bf16[64,2048]{1,0:T(8,128)(2,1)S(1)}, bf16[64,2048]{1,0:T(8,128)(2,1)S(1)}, u32[]{:S(2)}, u32[]{:S(2)}) collective-permute-start(bf16[64,2048]{1,0:T(8,128)(2,1)S(1)} %pad_maximum_fusion.refs_0_), channel_id=1, source_target_pairs={{0,3},{1,2},{2,1},{3,0},{4,7},{5,6},{6,5},{7,4},{8,11},{9,10},{10,... | collective-permute-start | bytes 786440 | tf_op jit(solution)/shard_map/ppermute | solution.py:23
  25.3 22.4 %collective-permute-start.9 = (bf16[64,2048]{1,0:T(8,128)(2,1)S(1)}, bf16[64,2048]{1,0:T(8,128)(2,1)S(1)}, u32[]{:S(2)}, u32[]{:S(2)}) collective-permute-start(bf16[64,2048]{1,0:T(8,128)(2,1)S(1)} %pad_maximum_fusion.refs_0_), channel_id=1, source_target_pairs={{0,2},{1,3},{2,0},{3,1},{4,6},{5,7},{6,4},{7,5},{8,10},{9,11},{10,... | collective-permute-start | bytes 786440 | tf_op jit(solution)/shard_map/ppermute | solution.py:23
  26.9 5.8 %copy-start.1 = (bf16[4096,2048]{1,0:T(8,128)(2,1)S(1)}, bf16[4096,2048]{1,0:T(8,128)(2,1)}, u32[]{:S(2)}) copy-start(bf16[4096,2048]{1,0:T(8,128)(2,1)} %refs_4_.1) | copy-start | bytes 50331652
  32.6 15.1 %copy-start.2 = (bf16[4096,2048]{1,0:T(8,128)(2,1)S(1)}, bf16[4096,2048]{1,0:T(8,128)(2,1)}, u32[]{:S(2)}) copy-start(bf16[4096,2048]{1,0:T(8,128)(2,1)} %refs_4_.1) | copy-start | bytes 50331652
  37.0 10.8 %collective-permute-start.8 = (bf16[64,2048]{1,0:T(8,128)(2,1)S(1)}, bf16[64,2048]{1,0:T(8,128)(2,1)S(1)}, u32[]{:S(2)}, u32[]{:S(2)}) collective-permute-start(bf16[64,2048]{1,0:T(8,128)(2,1)S(1)} %pad_maximum_fusion.refs_0_), channel_id=1, source_target_pairs={{0,1},{1,0},{2,3},{3,2},{4,5},{5,4},{6,7},{7,6},{8,9},{9,8},{10,11... | collective-permute-start | bytes 786440 | tf_op jit(solution)/shard_map/ppermute | solution.py:23
  43.2 9.8 %collective-permute-start.13 = (bf16[256,64]{1,0:T(8,128)(2,1)S(1)}, bf16[256,64]{1,0:T(8,128)(2,1)S(1)}, u32[]{:S(2)}, u32[]{:S(2)}) collective-permute-start(bf16[256,64]{1,0:T(8,128)(2,1)S(1)} %pad_maximum_fusion.2), channel_id=1, source_target_pairs={{0,4},{4,12},{12,8},{8,0},{1,5},{5,13},{13,9},{9,1},{2,6},{6,14},{... | collective-permute-start | bytes 98312 | tf_op jit(solution)/shard_map/ppermute | solution.py:23
  43.8 9.2 %collective-permute-start.12 = (bf16[256,64]{1,0:T(8,128)(2,1)S(1)}, bf16[256,64]{1,0:T(8,128)(2,1)S(1)}, u32[]{:S(2)}, u32[]{:S(2)}) collective-permute-start(bf16[256,64]{1,0:T(8,128)(2,1)S(1)} %pad_maximum_fusion.2), channel_id=1, source_target_pairs={{0,12},{12,0},{4,8},{8,4},{1,13},{13,1},{5,9},{9,5},{2,14},{14,2},... | collective-permute-start | bytes 98312 | tf_op jit(solution)/shard_map/ppermute | solution.py:23
  46.3 6.7 %collective-permute-start.11 = (bf16[256,64]{1,0:T(8,128)(2,1)S(1)}, bf16[256,64]{1,0:T(8,128)(2,1)S(1)}, u32[]{:S(2)}, u32[]{:S(2)}) collective-permute-start(bf16[256,64]{1,0:T(8,128)(2,1)S(1)} %pad_maximum_fusion.2), channel_id=1, source_target_pairs={{4,0},{12,4},{8,12},{0,8},{5,1},{13,5},{9,13},{1,9},{6,2},{14,6},{... | collective-permute-start | bytes 98312 | tf_op jit(solution)/shard_map/ppermute | solution.py:23
  53.8 2.0 %collective-permute-start.14 = (bf16[128,2048]{1,0:T(8,128)(2,1)S(1)}, bf16[128,2048]{1,0:T(8,128)(2,1)S(1)}, u32[]{:S(2)}, u32[]{:S(2)}) collective-permute-start(bf16[128,2048]{1,0:T(8,128)(2,1)S(1)} %fusion.4), channel_id=1, source_target_pairs={{0,1},{1,0},{2,3},{3,2},{4,5},{5,4},{6,7},{7,6},{8,9},{9,8},{10,11... | collective-permute-start | bytes 1572872 | tf_op jit(solution)/shard_map/ppermute | solution.py:27
  56.2 12.9 %collective-permute-start.17 = (bf16[32,2048]{1,0:T(8,128)(2,1)S(1)}, bf16[32,2048]{1,0:T(8,128)(2,1)S(1)}, u32[]{:S(2)}, u32[]{:S(2)}) collective-permute-start(bf16[32,2048]{1,0:T(8,128)(2,1)S(1)} %get-tuple-element.37), channel_id=1, source_target_pairs={{0,4},{4,12},{12,8},{8,0},{1,5},{5,13},{13,9},{9,1},{2,6},{6,14},{... | collective-permute-start | bytes 393224 | tf_op jit(solution)/shard_map/ppermute | solution.py:23
  56.8 12.3 %collective-permute-start.16 = (bf16[32,2048]{1,0:T(8,128)(2,1)S(1)}, bf16[32,2048]{1,0:T(8,128)(2,1)S(1)}, u32[]{:S(2)}, u32[]{:S(2)}) collective-permute-start(bf16[32,2048]{1,0:T(8,128)(2,1)S(1)} %get-tuple-element.38), channel_id=1, source_target_pairs={{0,12},{12,0},{4,8},{8,4},{1,13},{13,1},{5,9},{9,5},{2,14},{14,2},... | collective-permute-start | bytes 393224 | tf_op jit(solution)/shard_map/ppermute | solution.py:23
  58.6 10.5 %collective-permute-start.15 = (bf16[32,2048]{1,0:T(8,128)(2,1)S(1)}, bf16[32,2048]{1,0:T(8,128)(2,1)S(1)}, u32[]{:S(2)}, u32[]{:S(2)}) collective-permute-start(bf16[32,2048]{1,0:T(8,128)(2,1)S(1)} %get-tuple-element.39), channel_id=1, source_target_pairs={{4,0},{12,4},{8,12},{0,8},{5,1},{13,5},{9,13},{1,9},{6,2},{14,6},{... | collective-permute-start | bytes 393224 | tf_op jit(solution)/shard_map/ppermute | solution.py:23

commit v7 on v6

--- a/solution.py
+++ b/solution.py
@@ -125,7 +125,7 @@
             def _(at=at, first=first, second=second):
                 panel_ref[pl.ds(at, 2 * share)] = jnp.concatenate([second, first])
 
-    tile = 256
+    tile = 512
 
     @pl.loop(0, out_ref.shape[1] // tile)
     def _(n):

time: 70.7 us -> 69.7 us (0.986)
  Pallas kernels: 17.1 us -> 16.1 us
  starting transfers between devices: 22.7 us -> 23.5 us
  waiting for transfers between devices: 19.5 us -> 18.7 us
    pallas_call x1, Pallas kernels: 5 us -> 3.97 us  [last(): pl.pallas_call(last_kernel, out_shape=[jax.ShapeDtypeStruct((2 * rows, wi...]
    ppermute x16, waiting for transfers between devices: 16.8 us -> 15.9 us  [shift(): return lax.ppermute(x, axis, pairs)]
    ppermute x16, starting transfers between devices: 21.1 us -> 21.9 us  [shift(): return lax.ppermute(x, axis, pairs)]
  transfers between devices with their start and end apart: 18 -> 18, of which waited for: 6 -> 6; matrix products, arithmetic and copies ran while one was open for 4% -> 4% of each run, Pallas kernels for 22% -> 21%
where the time goes in v7:
time: 69.7 us; the launch traced here: 69.4 us
  starting transfers between devices  23.5 us (34%)
  waiting for transfers between devices  18.7 us (27%)
  Pallas kernels  16.1 us (23%)
  local copies, waits for them, and re-layouts  8.33 us (12%)
  matrix products  1.84 us (3%)
    ppermute x16, starting transfers between devices, shift(): return lax.ppermute(x, axis, pairs)  21.9 us
    ppermute x16, waiting for transfers between devices, shift(): return lax.ppermute(x, axis, pairs)  15.9 us
    pallas_call x2, Pallas kernels, stream(): pl.pallas_call(stream_kernel, out_shape=jax.ShapeDtypeStruct((rows, width...  10.8 us
    unnamed x12, local copies, waits for them, and re-layouts  6.86 us
    pallas_call x1, Pallas kernels, last(): pl.pallas_call(last_kernel, out_shape=[jax.ShapeDtypeStruct((2 * rows, wi...  3.97 us
    ppermute x2, waiting for transfers between devices, swap(): return lax.ppermute(x, axis, ((0, 1), (1, 0)))  2.76 us
    dot_general x6, matrix products, dot(): return jnp.dot(a, b, preferred_element_type=F32)  1.84 us
    ppermute x2, starting transfers between devices, swap(): return lax.ppermute(x, axis, ((0, 1), (1, 0)))  1.66 us
  transfers between devices with their start and end apart: 18, of which 6 were waited for; matrix products, arithmetic and copies ran while one was open for 4% of the time, Pallas kernels for 21%

profile of v7, /device:TPU:0, one launch (start us, length us, event | category | flops | bytes accessed | tf_op | source)
XLA Modules:
  0.0 69.4 jit_solution(12412683452792702017)
XLA Ops:
  0.0 0.0 copy-start
  0.0 0.0 copy-start.5
  0.0 4.0 %collective-permute-start.1 = (bf16[64,4096]{1,0:T(8,128)(2,1)}, bf16[64,4096]{1,0:T(8,128)(2,1)S(1)}, u32[]{:S(2)}, u32[]{:S(2)}) collective-permute-start(bf16[64,4096]{1,0:T(8,128)(2,1)} %bitcast.39), channel_id=1, source_target_pairs={{4,0},{12,4},{8,12},{0,8},{5,1},{13,5},{9,13},{1,9},{6,2},{14,6},{... | collective-permute-start | bytes 1572872 | tf_op jit(solution)/shard_map/ppermute | solution.py:23
  4.0 1.1 %copy-done.3 = bf16[1,64,4096]{2,1,0:T(8,128)(2,1)S(1)} copy-done((bf16[1,64,4096]{2,1,0:T(8,128)(2,1)S(1)}, bf16[1,64,4096]{2,1,0:T(8,128)(2,1)}, u32[]{:S(2)}) %copy-start.3) | copy-done | bytes 524312
  5.1 6.5 %shard_map.55 = f32[64,2048]{1,0:T(8,128)S(1)} custom-call(bf16[64,4096]{1,0:T(8,128)(2,1)S(1)} %bitcast.40, bf16[4096,2048]{1,0:T(8,128)(2,1)} %refs_4_.1), custom_call_target="tpu_custom_call" | custom-call | flops 1073741824 | bytes 16777216 | tf_op jit(solution)/shard_map/pallas_call | solution.py:86
  11.6 1.1 %dynamic-slice_bitcast_fusion = (bf16[1,8,2048]{2,1,0:T(8,128)(2,1)S(1)}, bf16[8,2048]{1,0:T(8,128)(2,1)S(1)}, bf16[8,2048]{1,0:T(8,128)(2,1)S(1)}, bf16[8,2048]{1,0:T(8,128)(2,1)S(1)}) fusion(bf16[64,8192]{1,0:T(8,128)(2,1)} %bitcast.49, s32[]{:T(128)S(6)} %select_n.98, s32[]{:T(128)S(6)} %select_n.100, s32[]{:T(128)S(6)} %select_n.106, s32[]{:T(128)S(6)} %select_n.104, ...), kind=kLoop, calls=%fused_computation.42 | loop fusion | bytes 262164 | tf_op jit(solution)/shard_map/stack | solution.py:189
  12.7 0.1 collective-permute-start.4
  12.8 3.0 %collective-permute-start.3 = (bf16[8,2048]{1,0:T(8,128)(2,1)S(1)}, bf16[8,2048]{1,0:T(8,128)(2,1)S(1)}, u32[]{:S(2)}, u32[]{:S(2)}) collective-permute-start(bf16[8,2048]{1,0:T(8,128)(2,1)S(1)} %get-tuple-element.35), channel_id=1, source_target_pairs={{0,12},{12,0},{4,8},{8,4},{1,13},{13,1},{5,9},{9,5},{2,14},{14,2},... | collective-permute-start | bytes 98312 | tf_op jit(solution)/shard_map/ppermute | solution.py:23
  15.8 0.4 collective-permute-start.2
  16.1 0.0 copy-done.4
  16.1 1.7 %collective-permute-start = (bf16[64,4096]{1,0:T(8,128)(2,1)S(1)}, bf16[64,4096]{1,0:T(8,128)(2,1)S(1)}, u32[]{:S(2)}, u32[]{:S(2)}) collective-permute-start(bf16[64,4096]{1,0:T(8,128)(2,1)S(1)} %bitcast.41), channel_id=1, source_target_pairs={{0,4},{4,12},{12,8},{8,0},{1,5},{5,13},{13,9},{9,1},{2,6},{6,14},{... | collective-permute-start | bytes 1572872 | tf_op jit(solution)/shard_map/ppermute | solution.py:23
  17.8 0.0 copy-done.5
  17.8 0.1 compare_bitcast_fusion.3
  18.0 0.1 pad_add_fusion.1.facts_ref
  18.0 1.4 %collective-permute-done.4 = bf16[8,2048]{1,0:T(8,128)(2,1)S(1)} collective-permute-done((bf16[8,2048]{1,0:T(8,128)(2,1)S(1)}, bf16[8,2048]{1,0:T(8,128)(2,1)S(1)}, u32[]{:S(2)}, u32[]{:S(2)}) %collective-permute-start.4) | collective-permute-done | bytes 32800 | tf_op jit(solution)/shard_map/ppermute | solution.py:23
  19.4 0.0 collective-permute-done.3
  19.4 0.7 collective-permute-done.2
  20.2 0.0 collective-permute-done.1.x_ref
  20.2 1.6 %collective-permute-start.7 = (bf16[4,8,2048]{2,1,0:T(8,128)(2,1)S(1)}, bf16[4,8,2048]{2,1,0:T(8,128)(2,1)S(1)}, u32[]{:S(2)}, u32[]{:S(2)}) collective-permute-start(bf16[4,8,2048]{2,1,0:T(8,128)(2,1)S(1)} %pad_maximum_fusion.1), channel_id=1, source_target_pairs={{0,16},{16,0},{1,17},{17,1},{2,18},{18,2},{3,19},{19,3},{4,20},{20... | collective-permute-start | bytes 393224 | tf_op jit(solution)/shard_map/ppermute | solution.py:27
  21.8 0.7 collective-permute-start.5
  22.4 1.3 %collective-permute-start.6 = (bf16[64,4096]{1,0:T(8,128)(2,1)S(1)}, bf16[64,4096]{1,0:T(8,128)(2,1)S(1)}, u32[]{:S(2)}, u32[]{:S(2)}) collective-permute-start(bf16[64,4096]{1,0:T(8,128)(2,1)S(1)} %collective-permute-done.1.x_ref), channel_id=1, source_target_pairs={{8,12},{4,0},{9,13},{5,1},{10,14},{6,2},{11,15},{7,3},{24,28},{20,... | collective-permute-start | bytes 1572872 | tf_op jit(solution)/shard_map/ppermute | solution.py:23
  23.7 0.0 copy-done
  23.8 0.3 fusion.5
  24.1 0.3 fusion.6
  24.3 0.9 %collective-permute-done.7 = bf16[4,8,2048]{2,1,0:T(8,128)(2,1)S(1)} collective-permute-done((bf16[4,8,2048]{2,1,0:T(8,128)(2,1)S(1)}, bf16[4,8,2048]{2,1,0:T(8,128)(2,1)S(1)}, u32[]{:S(2)}, u32[]{:S(2)}) %collective-permute-start.7) | collective-permute-done | bytes 131104 | tf_op jit(solution)/shard_map/ppermute | solution.py:27
  25.2 0.1 collective-permute-start.10
  25.3 1.6 %collective-permute-start.9 = (bf16[64,2048]{1,0:T(8,128)(2,1)S(1)}, bf16[64,2048]{1,0:T(8,128)(2,1)S(1)}, u32[]{:S(2)}, u32[]{:S(2)}) collective-permute-start(bf16[64,2048]{1,0:T(8,128)(2,1)S(1)} %pad_maximum_fusion.refs_0_), channel_id=1, source_target_pairs={{0,2},{1,3},{2,0},{3,1},{4,6},{5,7},{6,4},{7,5},{8,10},{9,11},{10,... | collective-permute-start | bytes 786440 | tf_op jit(solution)/shard_map/ppermute | solution.py:23
  26.9 5.8 %copy-done.1 = bf16[4096,2048]{1,0:T(8,128)(2,1)S(1)} copy-done((bf16[4096,2048]{1,0:T(8,128)(2,1)S(1)}, bf16[4096,2048]{1,0:T(8,128)(2,1)}, u32[]{:S(2)}) %copy-start.1) | copy-done | bytes 16777240
  32.6 4.3 %shard_map.56 = f32[64,2048]{1,0:T(8,128)S(1)} custom-call(bf16[64,4096]{1,0:T(8,128)(2,1)S(1)} %collective-permute-done.1.x_ref, bf16[4096,2048]{1,0:T(8,128)(2,1)S(1)} %copy-done.1), custom_call_target="tpu_custom_call" | custom-call | flops 1073741824 | bytes 16777216 | tf_op jit(solution)/shard_map/pallas_call | solution.py:86
  37.0 0.0 collective-permute-done.x3_ref
  37.0 0.4 collective-permute-start.8
  37.3 0.0 collective-permute-done.5.x2a_ref
  37.3 5.2 %collective-permute-done.6.x2b_ref = bf16[64,4096]{1,0:T(8,128)(2,1)S(1)} collective-permute-done((bf16[64,4096]{1,0:T(8,128)(2,1)S(1)}, bf16[64,4096]{1,0:T(8,128)(2,1)S(1)}, u32[]{:S(2)}, u32[]{:S(2)}) %collective-permute-start.6) | collective-permute-done | bytes 524320 | tf_op jit(solution)/shard_map/ppermute | solution.py:23
  42.5 0.3 fusion.7
  42.9 0.3 fusion.8
  43.2 0.6 collective-permute-start.13
  43.8 2.5 %collective-permute-start.12 = (bf16[256,64]{1,0:T(8,128)(2,1)S(1)}, bf16[256,64]{1,0:T(8,128)(2,1)S(1)}, u32[]{:S(2)}, u32[]{:S(2)}) collective-permute-start(bf16[256,64]{1,0:T(8,128)(2,1)S(1)} %pad_maximum_fusion.2), channel_id=1, source_target_pairs={{0,12},{12,0},{4,8},{8,4},{1,13},{13,1},{5,9},{9,5},{2,14},{14,2},... | collective-permute-start | bytes 98312 | tf_op jit(solution)/shard_map/ppermute | solution.py:23
  46.3 0.0 collective-permute-done.10.refs_3_
  46.3 1.4 %collective-permute-start.11 = (bf16[256,64]{1,0:T(8,128)(2,1)S(1)}, bf16[256,64]{1,0:T(8,128)(2,1)S(1)}, u32[]{:S(2)}, u32[]{:S(2)}) collective-permute-start(bf16[256,64]{1,0:T(8,128)(2,1)S(1)} %pad_maximum_fusion.2), channel_id=1, source_target_pairs={{4,0},{12,4},{8,12},{0,8},{5,1},{13,5},{9,13},{1,9},{6,2},{14,6},{... | collective-permute-start | bytes 98312 | tf_op jit(solution)/shard_map/ppermute | solution.py:23
  47.7 0.0 collective-permute-done.9.refs_2_
  47.7 0.0 collective-permute-done.8.refs_1_
  47.7 0.0 copy-done.2
  47.8 4.0 %shard_map.57 = (f32[128,2048]{1,0:T(8,128)S(1)}, bf16[256,2048]{1,0:T(8,128)(2,1)S(1)}) custom-call(s32[3]{0:T(128)S(1)} %pad_add_fusion.1.facts_ref, bf16[64,4096]{1,0:T(8,128)(2,1)S(1)} %collective-permute-done.x3_ref, bf16[64,4096]{1,0:T(8,128)(2,1)S(1)} %collective-permute-done.5.x2a_ref, bf16[64,4096]{1,0:T(8,128)(2,1)S(1)} %collective-permute-done.6.x2b_ref, ...), custom_call_target="tpu_custom_call" | custom-call | flops 2147483648 | bytes 16777216 | tf_op jit(solution)/shard_map/pallas_call | solution.py:139
  51.7 0.1 fusion.31
  51.8 0.1 constant_dynamic-slice_fusion.4
  52.0 0.0 collective-permute-done.13
  52.0 0.0 collective-permute-done.12
  52.0 0.0 collective-permute-done.11
  52.0 0.1 pad_maximum_fusion.5
  52.1 0.1 pad_maximum_fusion.6
  52.3 0.1 pad_maximum_fusion.4
  52.3 0.1 pad_maximum_fusion.3
  52.5 0.3 fusion.4
  52.8 0.1 collective-permute-start.14
  52.9 1.9 %collective-permute-done.14 = bf16[128,2048]{1,0:T(8,128)(2,1)S(1)} collective-permute-done((bf16[128,2048]{1,0:T(8,128)(2,1)S(1)}, bf16[128,2048]{1,0:T(8,128)(2,1)S(1)}, u32[]{:S(2)}, u32[]{:S(2)}) %collective-permute-start.14) | collective-permute-done | bytes 524320 | tf_op jit(solution)/shard_map/ppermute | solution.py:27
  54.8 0.3 fusion.3
  55.1 1.2 %collective-permute-start.17 = (bf16[32,2048]{1,0:T(8,128)(2,1)S(1)}, bf16[32,2048]{1,0:T(8,128)(2,1)S(1)}, u32[]{:S(2)}, u32[]{:S(2)}) collective-permute-start(bf16[32,2048]{1,0:T(8,128)(2,1)S(1)} %get-tuple-element.37), channel_id=1, source_target_pairs={{0,4},{4,12},{12,8},{8,0},{1,5},{5,13},{13,9},{9,1},{2,6},{6,14},{... | collective-permute-start | bytes 393224 | tf_op jit(solution)/shard_map/ppermute | solution.py:23
  56.4 2.2 %collective-permute-start.16 = (bf16[32,2048]{1,0:T(8,128)(2,1)S(1)}, bf16[32,2048]{1,0:T(8,128)(2,1)S(1)}, u32[]{:S(2)}, u32[]{:S(2)}) collective-permute-start(bf16[32,2048]{1,0:T(8,128)(2,1)S(1)} %get-tuple-element.38), channel_id=1, source_target_pairs={{0,12},{12,0},{4,8},{8,4},{1,13},{13,1},{5,9},{9,5},{2,14},{14,2},... | collective-permute-start | bytes 393224 | tf_op jit(solution)/shard_map/ppermute | solution.py:23
  58.6 0.8 %collective-permute-start.15 = (bf16[32,2048]{1,0:T(8,128)(2,1)S(1)}, bf16[32,2048]{1,0:T(8,128)(2,1)S(1)}, u32[]{:S(2)}, u32[]{:S(2)}) collective-permute-start(bf16[32,2048]{1,0:T(8,128)(2,1)S(1)} %get-tuple-element.39), channel_id=1, source_target_pairs={{4,0},{12,4},{8,12},{0,8},{5,1},{13,5},{9,13},{1,9},{6,2},{14,6},{... | collective-permute-start | bytes 393224 | tf_op jit(solution)/shard_map/ppermute | solution.py:23
  59.4 0.1 pad_add_fusion.where_ref
  59.4 8.6 %collective-permute-done.17.refs_3_ = bf16[32,2048]{1,0:T(8,128)(2,1)S(1)} collective-permute-done((bf16[32,2048]{1,0:T(8,128)(2,1)S(1)}, bf16[32,2048]{1,0:T(8,128)(2,1)S(1)}, u32[]{:S(2)}, u32[]{:S(2)}) %collective-permute-start.17) | collective-permute-done | bytes 131104 | tf_op jit(solution)/shard_map/ppermute | solution.py:23
  68.1 0.0 collective-permute-done.16.refs_2_
  68.1 0.0 collective-permute-done.15.refs_1_
  68.1 1.4 %shard_map.58 = bf16[32,8192]{1,0:T(8,128)(2,1)} custom-call(s32[4]{0:T(128)S(1)} %pad_add_fusion.where_ref, bf16[32,2048]{1,0:T(8,128)(2,1)S(1)} %get-tuple-element.40.refs_0_, bf16[32,2048]{1,0:T(8,128)(2,1)S(1)} %collective-permute-done.15.refs_1_, bf16[32,2048]{1,0:T(8,128)(2,1)S(1)} %collective-permute-done.16.refs_2_, ...), custom_call_target="tpu_custom_call" | custom-call | tf_op jit(solution)/shard_map/pallas_call | solution.py:48
  (15 shorter events, 0.2 us)
Async XLA Ops:
  0.0 23.8 %copy-start = (bf16[1,4096,64]{1,2,0:T(8,128)(2,1)S(1)}, bf16[1,4096,64]{1,2,0:T(8,128)(2,1)}, u32[]{:S(2)}) copy-start(bf16[1,4096,64]{1,2,0:T(8,128)(2,1)} %param.8) | copy-start | bytes 1572868
  0.0 17.8 %copy-start.5 = (s32[1,256,1]{1,2,0:T(1,128)S(1)}, s32[1,256,1]{1,2,0:T(1,128)}, u32[]{:S(2)}) copy-start(s32[1,256,1]{1,2,0:T(1,128)} %param.6) | copy-start | bytes 3076
  0.0 20.2 %collective-permute-start.1 = (bf16[64,4096]{1,0:T(8,128)(2,1)}, bf16[64,4096]{1,0:T(8,128)(2,1)S(1)}, u32[]{:S(2)}, u32[]{:S(2)}) collective-permute-start(bf16[64,4096]{1,0:T(8,128)(2,1)} %bitcast.39), channel_id=1, source_target_pairs={{4,0},{12,4},{8,12},{0,8},{5,1},{13,5},{9,13},{1,9},{6,2},{14,6},{... | collective-permute-start | bytes 1572872 | tf_op jit(solution)/shard_map/ppermute | solution.py:23
  4.0 1.1 %copy-start.3 = (bf16[1,64,4096]{2,1,0:T(8,128)(2,1)S(1)}, bf16[1,64,4096]{2,1,0:T(8,128)(2,1)}, u32[]{:S(2)}) copy-start(bf16[1,64,4096]{2,1,0:T(8,128)(2,1)} %param.5) | copy-start | bytes 1572868
  5.1 11.0 %copy-start.4 = (bf16[1,64,4096]{2,1,0:T(8,128)(2,1)S(1)}, bf16[1,64,4096]{2,1,0:T(8,128)(2,1)}, u32[]{:S(2)}) copy-start(bf16[1,64,4096]{2,1,0:T(8,128)(2,1)} %param.5) | copy-start | bytes 1572868
  12.7 6.7 %collective-permute-start.4 = (bf16[8,2048]{1,0:T(8,128)(2,1)S(1)}, bf16[8,2048]{1,0:T(8,128)(2,1)S(1)}, u32[]{:S(2)}, u32[]{:S(2)}) collective-permute-start(bf16[8,2048]{1,0:T(8,128)(2,1)S(1)} %get-tuple-element.34), channel_id=1, source_target_pairs={{0,4},{4,12},{12,8},{8,0},{1,5},{5,13},{13,9},{9,1},{2,6},{6,14},{... | collective-permute-start | bytes 98312 | tf_op jit(solution)/shard_map/ppermute | solution.py:23
  12.8 6.7 %collective-permute-start.3 = (bf16[8,2048]{1,0:T(8,128)(2,1)S(1)}, bf16[8,2048]{1,0:T(8,128)(2,1)S(1)}, u32[]{:S(2)}, u32[]{:S(2)}) collective-permute-start(bf16[8,2048]{1,0:T(8,128)(2,1)S(1)} %get-tuple-element.35), channel_id=1, source_target_pairs={{0,12},{12,0},{4,8},{8,4},{1,13},{13,1},{5,9},{9,5},{2,14},{14,2},... | collective-permute-start | bytes 98312 | tf_op jit(solution)/shard_map/ppermute | solution.py:23
  15.8 4.4 %collective-permute-start.2 = (bf16[8,2048]{1,0:T(8,128)(2,1)S(1)}, bf16[8,2048]{1,0:T(8,128)(2,1)S(1)}, u32[]{:S(2)}, u32[]{:S(2)}) collective-permute-start(bf16[8,2048]{1,0:T(8,128)(2,1)S(1)} %get-tuple-element.36), channel_id=1, source_target_pairs={{4,0},{12,4},{8,12},{0,8},{5,1},{13,5},{9,13},{1,9},{6,2},{14,6},{... | collective-permute-start | bytes 98312 | tf_op jit(solution)/shard_map/ppermute | solution.py:23
  16.1 20.8 %collective-permute-start = (bf16[64,4096]{1,0:T(8,128)(2,1)S(1)}, bf16[64,4096]{1,0:T(8,128)(2,1)S(1)}, u32[]{:S(2)}, u32[]{:S(2)}) collective-permute-start(bf16[64,4096]{1,0:T(8,128)(2,1)S(1)} %bitcast.41), channel_id=1, source_target_pairs={{0,4},{4,12},{12,8},{8,0},{1,5},{5,13},{13,9},{9,1},{2,6},{6,14},{... | collective-permute-start | bytes 1572872 | tf_op jit(solution)/shard_map/ppermute | solution.py:23
  20.2 5.0 %collective-permute-start.7 = (bf16[4,8,2048]{2,1,0:T(8,128)(2,1)S(1)}, bf16[4,8,2048]{2,1,0:T(8,128)(2,1)S(1)}, u32[]{:S(2)}, u32[]{:S(2)}) collective-permute-start(bf16[4,8,2048]{2,1,0:T(8,128)(2,1)S(1)} %pad_maximum_fusion.1), channel_id=1, source_target_pairs={{0,16},{16,0},{1,17},{17,1},{2,18},{18,2},{3,19},{19,3},{4,20},{20... | collective-permute-start | bytes 393224 | tf_op jit(solution)/shard_map/ppermute | solution.py:27
  21.8 15.6 %collective-permute-start.5 = (bf16[64,4096]{1,0:T(8,128)(2,1)S(1)}, bf16[64,4096]{1,0:T(8,128)(2,1)S(1)}, u32[]{:S(2)}, u32[]{:S(2)}) collective-permute-start(bf16[64,4096]{1,0:T(8,128)(2,1)S(1)} %bitcast.42), channel_id=1, source_target_pairs={{4,8},{8,4},{5,9},{9,5},{6,10},{10,6},{7,11},{11,7},{20,24},{24,20... | collective-permute-start | bytes 1572872 | tf_op jit(solution)/shard_map/ppermute | solution.py:23
  22.4 20.1 %collective-permute-start.6 = (bf16[64,4096]{1,0:T(8,128)(2,1)S(1)}, bf16[64,4096]{1,0:T(8,128)(2,1)S(1)}, u32[]{:S(2)}, u32[]{:S(2)}) collective-permute-start(bf16[64,4096]{1,0:T(8,128)(2,1)S(1)} %collective-permute-done.1.x_ref), channel_id=1, source_target_pairs={{8,12},{4,0},{9,13},{5,1},{10,14},{6,2},{11,15},{7,3},{24,28},{20,... | collective-permute-start | bytes 1572872 | tf_op jit(solution)/shard_map/ppermute | solution.py:23
  25.2 21.1 %collective-permute-start.10 = (bf16[64,2048]{1,0:T(8,128)(2,1)S(1)}, bf16[64,2048]{1,0:T(8,128)(2,1)S(1)}, u32[]{:S(2)}, u32[]{:S(2)}) collective-permute-start(bf16[64,2048]{1,0:T(8,128)(2,1)S(1)} %pad_maximum_fusion.refs_0_), channel_id=1, source_target_pairs={{0,3},{1,2},{2,1},{3,0},{4,7},{5,6},{6,5},{7,4},{8,11},{9,10},{10,... | collective-permute-start | bytes 786440 | tf_op jit(solution)/shard_map/ppermute | solution.py:23
  25.3 22.4 %collective-permute-start.9 = (bf16[64,2048]{1,0:T(8,128)(2,1)S(1)}, bf16[64,2048]{1,0:T(8,128)(2,1)S(1)}, u32[]{:S(2)}, u32[]{:S(2)}) collective-permute-start(bf16[64,2048]{1,0:T(8,128)(2,1)S(1)} %pad_maximum_fusion.refs_0_), channel_id=1, source_target_pairs={{0,2},{1,3},{2,0},{3,1},{4,6},{5,7},{6,4},{7,5},{8,10},{9,11},{10,... | collective-permute-start | bytes 786440 | tf_op jit(solution)/shard_map/ppermute | solution.py:23
  26.9 5.8 %copy-start.1 = (bf16[4096,2048]{1,0:T(8,128)(2,1)S(1)}, bf16[4096,2048]{1,0:T(8,128)(2,1)}, u32[]{:S(2)}) copy-start(bf16[4096,2048]{1,0:T(8,128)(2,1)} %refs_4_.1) | copy-start | bytes 50331652
  32.6 15.1 %copy-start.2 = (bf16[4096,2048]{1,0:T(8,128)(2,1)S(1)}, bf16[4096,2048]{1,0:T(8,128)(2,1)}, u32[]{:S(2)}) copy-start(bf16[4096,2048]{1,0:T(8,128)(2,1)} %refs_4_.1) | copy-start | bytes 50331652
  37.0 10.8 %collective-permute-start.8 = (bf16[64,2048]{1,0:T(8,128)(2,1)S(1)}, bf16[64,2048]{1,0:T(8,128)(2,1)S(1)}, u32[]{:S(2)}, u32[]{:S(2)}) collective-permute-start(bf16[64,2048]{1,0:T(8,128)(2,1)S(1)} %pad_maximum_fusion.refs_0_), channel_id=1, source_target_pairs={{0,1},{1,0},{2,3},{3,2},{4,5},{5,4},{6,7},{7,6},{8,9},{9,8},{10,11... | collective-permute-start | bytes 786440 | tf_op jit(solution)/shard_map/ppermute | solution.py:23
  43.2 8.8 %collective-permute-start.13 = (bf16[256,64]{1,0:T(8,128)(2,1)S(1)}, bf16[256,64]{1,0:T(8,128)(2,1)S(1)}, u32[]{:S(2)}, u32[]{:S(2)}) collective-permute-start(bf16[256,64]{1,0:T(8,128)(2,1)S(1)} %pad_maximum_fusion.2), channel_id=1, source_target_pairs={{0,4},{4,12},{12,8},{8,0},{1,5},{5,13},{13,9},{9,1},{2,6},{6,14},{... | collective-permute-start | bytes 98312 | tf_op jit(solution)/shard_map/ppermute | solution.py:23
  43.8 8.2 %collective-permute-start.12 = (bf16[256,64]{1,0:T(8,128)(2,1)S(1)}, bf16[256,64]{1,0:T(8,128)(2,1)S(1)}, u32[]{:S(2)}, u32[]{:S(2)}) collective-permute-start(bf16[256,64]{1,0:T(8,128)(2,1)S(1)} %pad_maximum_fusion.2), channel_id=1, source_target_pairs={{0,12},{12,0},{4,8},{8,4},{1,13},{13,1},{5,9},{9,5},{2,14},{14,2},... | collective-permute-start | bytes 98312 | tf_op jit(solution)/shard_map/ppermute | solution.py:23
  46.3 5.7 %collective-permute-start.11 = (bf16[256,64]{1,0:T(8,128)(2,1)S(1)}, bf16[256,64]{1,0:T(8,128)(2,1)S(1)}, u32[]{:S(2)}, u32[]{:S(2)}) collective-permute-start(bf16[256,64]{1,0:T(8,128)(2,1)S(1)} %pad_maximum_fusion.2), channel_id=1, source_target_pairs={{4,0},{12,4},{8,12},{0,8},{5,1},{13,5},{9,13},{1,9},{6,2},{14,6},{... | collective-permute-start | bytes 98312 | tf_op jit(solution)/shard_map/ppermute | solution.py:23
  52.8 2.0 %collective-permute-start.14 = (bf16[128,2048]{1,0:T(8,128)(2,1)S(1)}, bf16[128,2048]{1,0:T(8,128)(2,1)S(1)}, u32[]{:S(2)}, u32[]{:S(2)}) collective-permute-start(bf16[128,2048]{1,0:T(8,128)(2,1)S(1)} %fusion.4), channel_id=1, source_target_pairs={{0,1},{1,0},{2,3},{3,2},{4,5},{5,4},{6,7},{7,6},{8,9},{9,8},{10,11... | collective-permute-start | bytes 1572872 | tf_op jit(solution)/shard_map/ppermute | solution.py:27
  55.1 12.9 %collective-permute-start.17 = (bf16[32,2048]{1,0:T(8,128)(2,1)S(1)}, bf16[32,2048]{1,0:T(8,128)(2,1)S(1)}, u32[]{:S(2)}, u32[]{:S(2)}) collective-permute-start(bf16[32,2048]{1,0:T(8,128)(2,1)S(1)} %get-tuple-element.37), channel_id=1, source_target_pairs={{0,4},{4,12},{12,8},{8,0},{1,5},{5,13},{13,9},{9,1},{2,6},{6,14},{... | collective-permute-start | bytes 393224 | tf_op jit(solution)/shard_map/ppermute | solution.py:23
  56.4 11.7 %collective-permute-start.16 = (bf16[32,2048]{1,0:T(8,128)(2,1)S(1)}, bf16[32,2048]{1,0:T(8,128)(2,1)S(1)}, u32[]{:S(2)}, u32[]{:S(2)}) collective-permute-start(bf16[32,2048]{1,0:T(8,128)(2,1)S(1)} %get-tuple-element.38), channel_id=1, source_target_pairs={{0,12},{12,0},{4,8},{8,4},{1,13},{13,1},{5,9},{9,5},{2,14},{14,2},... | collective-permute-start | bytes 393224 | tf_op jit(solution)/shard_map/ppermute | solution.py:23
  58.6 9.5 %collective-permute-start.15 = (bf16[32,2048]{1,0:T(8,128)(2,1)S(1)}, bf16[32,2048]{1,0:T(8,128)(2,1)S(1)}, u32[]{:S(2)}, u32[]{:S(2)}) collective-permute-start(bf16[32,2048]{1,0:T(8,128)(2,1)S(1)} %get-tuple-element.39), channel_id=1, source_target_pairs={{4,0},{12,4},{8,12},{0,8},{5,1},{13,5},{9,13},{1,9},{6,2},{14,6},{... | collective-permute-start | bytes 393224 | tf_op jit(solution)/shard_map/ppermute | solution.py:23
